TPU v7x, 256 devices: a whole 4x4x8 slice. The times are simulated.
256 devices in a mesh: store: 32 (over y, z), head: 4 (over x), rep: 2 (over core).
Axes of the slice: x: 4, y: 4, z: 8, core: 2. Of those that a mesh axis runs over, the one named last changes fastest.
Arguments:
- queries: bfloat16 [64, 128, 8192], P(('store', 'rep'), None, 'head'), may hold values from -168 to 168
- span_keys: bfloat16 [64, 128, 1024], P(('store', 'rep'), None, 'head'), may hold values from -12 to 12
- span_values: bfloat16 [64, 128, 1024], P(('store', 'rep'), None, 'head'), may hold values from -6 to 6
- page_cache: bfloat16 [256, 2, 256, 1024], P('store', None, None, 'head'), may hold values from -8.5 to 8.5
- passage_ids: int32 [64, 8], P(('store', 'rep')), may hold values from 0 to 255, as said below
- starts: int32 [64, 8], P(('store', 'rep')), may hold values from 0 to 2815, as said below
- out_weight: bfloat16 [8192, 4, 2, 512], P('head', None, 'rep'), may hold values from -0.59765625 to 0.59765625
Outputs:
- layer_output: bfloat16 [64, 128, 4096], P(('store', 'rep'), None, 'head')
Inputs may be any that keep to these rules, and one draw needn't show every extreme that they name: `passage_ids`: each request names 8 different passages; passage p is held by index p // 8 of store, and at most 1 passages of one request share an index. A request's starts are its own offset plus 256 times a permutation of 0 to 7.
All inputs are finite; a program needn't handle non-finite values.
Results may differ from a plain program's by a relative error of at most 0.012.
The roundings to bfloat16 on the way count: a program that leaves them out, or rounds other values in their place, can miss the bound.
Values may be sent and summed in bfloat16 or wider, within the bound.
No kernel may reach another device: no remote copies, remote signals or barrier semaphores. Data moves between devices by JAX's collectives and lax.ppermute only.
A program may use at most 128 MiB of HBM per device.

v0:
```python
import math

import jax
import jax.numpy as jnp
from jax import lax
from jax.sharding import PartitionSpec as P

HD = 128


theta_base = 1000000.0


def rotate(values, positions):
    half_dim = values.shape[-1] // 2
    inverse_freq = jnp.exp(
        -(2.0 * jnp.arange(half_dim, dtype=jnp.float32) / values.shape[-1]) * math.log(theta_base)
    )
    angles = positions.astype(jnp.float32)[..., None] * inverse_freq
    cosine = jnp.cos(angles)
    sine_part = jnp.sin(angles)
    first_half = values[..., :half_dim]
    second = values[..., half_dim:]
    return jnp.concatenate(
        [first_half * cosine - second * sine_part, second * cosine + first_half * sine_part],
        axis=-1,
    )


def on_device(queries, span_keys, span_values, page_cache, passage_ids, starts, out_weight):
    store_count = lax.axis_size("store")
    own_index = lax.axis_index("store")
    per_store = page_cache.shape[0]
    page_len = page_cache.shape[2]
    row_width = page_cache.shape[3]
    pass_count = passage_ids.shape[1]
    capacity = max(1, pass_count // store_count)
    tokens = queries.shape[1]
    kv_local = row_width // HD
    heads_local = queries.shape[2] // HD
    group_size = heads_local // kv_local
    wanted = lax.all_gather(passage_ids, "store", axis=0, tiled=True)
    owners = wanted // per_store
    held_here = (owners == own_index).astype(jnp.int32)
    rank_among = jnp.cumsum(held_here, axis=1) - held_here
    slot_match = held_here[:, :, None] * (
        rank_among[:, :, None] == jnp.arange(capacity, dtype=jnp.int32)[None, None, :]
    ).astype(jnp.int32)
    local_index = jnp.sum(slot_match * (wanted % per_store)[:, :, None], axis=1)
    outgoing = page_cache[local_index.reshape(-1)].reshape(
        store_count, capacity, 2, page_len, row_width
    )
    arrived = lax.all_to_all(outgoing, "store", split_axis=0, concat_axis=0, tiled=True)
    own_ids = passage_ids[0]
    holder = own_ids // per_store
    position_index = jnp.arange(pass_count, dtype=jnp.int32)
    earlier = jnp.sum(
        (holder[None, :] == holder[:, None]) & (position_index[None, :] < position_index[:, None]),
        axis=1,
    )
    fetched = arrived.reshape(store_count * capacity, 2, page_len, row_width)[
        holder * capacity + earlier
    ]
    begins = starts[0]
    query_start = jnp.min(begins) + pass_count * page_len
    query_pos = query_start + jnp.arange(tokens, dtype=jnp.int32)
    query_rot = rotate(
        queries[0].reshape(tokens, heads_local, HD).astype(jnp.float32), query_pos[:, None]
    ).astype(jnp.bfloat16)
    near_keys = rotate(
        span_keys[0].reshape(tokens, kv_local, HD).astype(jnp.float32), query_pos[:, None]
    ).astype(jnp.bfloat16)
    near_values = span_values[0].reshape(tokens, kv_local, HD)
    page_pos = begins[:, None] + jnp.arange(page_len, dtype=jnp.int32)[None, :]
    far_keys = rotate(
        fetched[:, 0].reshape(pass_count, page_len, kv_local, HD).astype(jnp.float32),
        page_pos[:, :, None],
    )
    far_keys = far_keys.astype(jnp.bfloat16).reshape(pass_count * page_len, kv_local, HD)
    far_values = fetched[:, 1].reshape(pass_count * page_len, kv_local, HD)
    allowed = jnp.arange(tokens)[:, None] >= jnp.arange(tokens)[None, :]
    score_scale = 1.0 / math.sqrt(HD)
    outputs = []
    for kv_head in range(kv_local):
        query_group = query_rot[:, kv_head * group_size : (kv_head + 1) * group_size, :]
        far_scores = (
            jnp.einsum(
                "qgd,kd->gqk",
                query_group,
                far_keys[:, kv_head, :],
                preferred_element_type=jnp.float32,
            )
            * score_scale
        )
        near_scores = (
            jnp.einsum(
                "qgd,kd->gqk",
                query_group,
                near_keys[:, kv_head, :],
                preferred_element_type=jnp.float32,
            )
            * score_scale
        )
        near_scores = jnp.where(allowed, near_scores, -jnp.inf)
        row_max = jnp.maximum(jnp.max(far_scores, axis=-1), jnp.max(near_scores, axis=-1))[
            ..., None
        ]
        far_weights = jnp.exp(far_scores - row_max)
        near_weights = jnp.exp(near_scores - row_max)
        totals = jnp.sum(far_weights, axis=-1) + jnp.sum(near_weights, axis=-1)
        weighted = jnp.einsum(
            "gqk,kd->qgd",
            far_weights.astype(jnp.bfloat16),
            far_values[:, kv_head, :],
            preferred_element_type=jnp.float32,
        )
        weighted = weighted + jnp.einsum(
            "gqk,kd->qgd",
            near_weights.astype(jnp.bfloat16),
            near_values[:, kv_head, :],
            preferred_element_type=jnp.float32,
        )
        outputs.append(weighted / jnp.transpose(totals)[..., None])
    attention = jnp.stack(outputs, axis=1).astype(jnp.bfloat16).reshape(tokens, heads_local * HD)
    weight_part = lax.all_gather(out_weight, "rep", axis=2, tiled=True)
    flattened = weight_part.reshape(weight_part.shape[0], -1)
    product = jnp.dot(attention, flattened, preferred_element_type=jnp.float32)
    partials = product.reshape(
        tokens, weight_part.shape[1], weight_part.shape[2], weight_part.shape[3]
    )
    summed = lax.psum_scatter(partials, "head", scatter_dimension=1, tiled=True)
    result = summed.astype(jnp.bfloat16).reshape(1, tokens, -1)
    return result


def solution(mesh):
    return jax.shard_map(
        on_device,
        mesh=mesh,
        in_specs=(
            P(("store", "rep"), None, "head"),
            P(("store", "rep"), None, "head"),
            P(("store", "rep"), None, "head"),
            P("store", None, None, "head"),
            P(("store", "rep"), None),
            P(("store", "rep"), None),
            P("head", None, "rep", None),
        ),
        out_specs=P(("store", "rep"), None, "head"),
        check_vma=False,
    )
```

profile of v0, /device:TPU:1, one launch (start us, length us, event | category | flops | bytes accessed | tf_op | source)
XLA Modules:
  0.0 319.8 jit_solution(8860911330355839189)
XLA Ops:
  6.5 34.1 %all-gather = s32[32,1,8]{2,1,0:T(1,128)S(1)} all-gather(s32[1,1,8]{2,1,0:T(1,128)} %bitcast.177), channel_id=1, replica_groups=mesh['store'=32,'head'=4,'rep'=2] {'store'}, dimensions={0}, use_global_device_ids=true | all-gather | bytes 1056 | tf_op jit(solution)/shard_map/all_gather | solution.py:42
  40.9 4.8 %gather_fusion = bf16[32,2,256,256]{3,2,1,0:T(8,128)(2,1)} fusion(bf16[8,2,256,256]{3,2,1,0:T(8,128)(2,1)S(1)} %copy-done, s32[1024]{0:T(1024)S(1)} %pad_clamp_fusion.1), kind=kCustom, calls=%fused_computation | custom fusion | bytes 16777344 | tf_op jit(solution)/shard_map/gather | solution.py:50
  45.8 5.7 %all-to-all-start = ((bf16[32,1,2,256,256]{4,3,2,1,0:T(8,128)(2,1)}), bf16[32,1,2,256,256]{4,3,2,1,0:T(8,128)(2,1)}, u32[]{:S(2)}, u32[]{:S(2)}) async-start(bf16[32,1,2,256,256]{4,3,2,1,0:T(8,128)(2,1)} %bitcast.164), calls=%async_computation | async-start | bytes 16777216 | tf_op jit(solution)/shard_map/all_to_all | solution.py:53
  51.5 13.8 %copy.67 = bf16[2048,4,1,512]{0,3,2,1:T(8,128)(2,1)} copy(bf16[2048,4,1,512]{3,1,2,0:T(4,128)(2,1)} %param.13) | data formatting | bytes 16777216 | tf_op args[6]
  65.4 0.7 copy-done.9
  66.3 0.7 copy.63
  67.1 0.8 copy.83
  68.9 0.6 reduce_min.9
  71.3 1.0 subtract_convert_fusion.2
  72.2 1.1 fusion.79
  73.3 1.1 fusion.78
  74.4 5.5 %multiply_cosine_fusion = (f32[8,256,64]{2,1,0:T(8,128)}, f32[8,256,64]{2,1,0:T(8,128)}) fusion(f32[64]{0:T(128)S(1)} %multiply_exponential_fusion, f32[8,256]{1,0:T(8,128)S(1)} %add_convert_fusion.3), kind=kLoop, calls=%fused_computation.19 | loop fusion | flops 131072 | bytes 1057024 | tf_op jit(solution)/shard_map/cos | solution.py:20
  79.9 150.1 %all-to-all-done = bf16[32,1,2,256,256]{4,3,2,1,0:T(8,128)(2,1)} async-done(((bf16[32,1,2,256,256]{4,3,2,1,0:T(8,128)(2,1)}), bf16[32,1,2,256,256]{4,3,2,1,0:T(8,128)(2,1)}, u32[]{:S(2)}, u32[]{:S(2)}) %all-to-all-start) | async-done | bytes 8388640 | tf_op jit(solution)/shard_map/all_to_all | solution.py:53
  230.0 4.1 %gather_fusion.1 = bf16[8,2,256,256]{3,2,1,0:T(8,128)(2,1)S(1)} fusion(bf16[32,2,256,256]{3,2,1,0:T(8,128)(2,1)} %bitcast.5, s32[1024]{0:T(1024)S(1)} %pad_clamp_fusion), kind=kCustom, calls=%fused_computation.1 | custom fusion | bytes 4194336 | tf_op jit(solution)/shard_map/gather | solution.py:61
  234.1 2.0 fusion.73
  236.1 1.3 reshape.314
  237.5 2.3 fusion.75
  239.8 3.5 %copy.78 = bf16[2048,1,128]{0,2,1:T(8,128)(2,1)} copy(bf16[2048,1,128]{2,1,0:T(2,128)(2,1)} %get-tuple-element.13) | data formatting | bytes 1048576
  243.3 1.8 copy.85
  245.1 2.5 reshape.284
  247.6 2.3 fusion.74
  250.0 0.6 subtract_convert_fusion
  250.6 1.4 bitcast_reduce_fusion.1
  252.0 1.3 bitcast_reduce_fusion
  253.6 1.4 fusion.4
  255.0 1.6 fusion.12
  256.8 1.4 fusion.6
  258.2 1.6 fusion.15
  260.2 13.2 %fusion = f32[128,4,2,512]{3,0,2,1:T(8,128)} fusion(bf16[128,2048,1,1]{0,1,3,2:T(8,128)(2,1)S(1)} %bitcast.170, bf16[2048,4,2,512]{0,3,2,1:T(8,128)(2,1)} %all-gather.3.cloned.1.call-done), kind=kOutput, calls=%fused_computation.2 | convolution fusion | flops 2147483648 | bytes 19398656 | tf_op jit(solution)/shard_map/dot_general | solution.py:127
  273.5 37.4 %reduce-scatter.2.cloned.1.call-done = f32[128,1,2,512]{3,0,2,1:T(8,128)} async-done(((f32[128,4,2,512]{3,0,2,1:T(8,128)}), f32[128,1,2,512]{3,0,2,1:T(8,128)}) %reduce-scatter.2.cloned.1.call-update) | async-done | bytes 524304 | tf_op jit(solution)/shard_map/reduce_scatter | solution.py:131
  310.9 1.1 convert_element_type.89
  312.1 0.9 copy.70
  (66 shorter events, 3.8 us)
Async XLA Ops:
  6.5 34.4 %copy-start = (bf16[8,2,256,256]{3,2,1,0:T(8,128)(2,1)S(1)}, bf16[8,2,256,256]{3,2,1,0:T(8,128)(2,1)}, u32[]{:S(2)}) copy-start(bf16[8,2,256,256]{3,2,1,0:T(8,128)(2,1)} %param.10) | copy-start | bytes 6291460
  45.8 184.2 %all-to-all-start = ((bf16[32,1,2,256,256]{4,3,2,1,0:T(8,128)(2,1)}), bf16[32,1,2,256,256]{4,3,2,1,0:T(8,128)(2,1)}, u32[]{:S(2)}, u32[]{:S(2)}) async-start(bf16[32,1,2,256,256]{4,3,2,1,0:T(8,128)(2,1)} %bitcast.164), calls=%async_computation | async-start | bytes 16777216 | tf_op jit(solution)/shard_map/all_to_all | solution.py:53
  51.5 208.8 %all-gather.3.cloned.1.call-start = ((), (), s32[]{:S(2)}) async-start(), calls=%async_computation.2 | async-start | bytes 25165824 | tf_op jit(solution)/shard_map/all_gather | solution.py:125
  65.3 0.8 copy-start.9
  65.3 1.0 copy-start.10
  65.3 2.6 copy-start.8
  65.3 3.6 %copy-start.13 = (s32[1,8]{1,0:T(1,128)S(1)}, s32[1,8]{1,0:T(1,128)}, u32[]{:S(2)}) copy-start(s32[1,8]{1,0:T(1,128)} %param.12) | copy-start | bytes 100
  65.3 4.8 %copy-start.12 = (s32[1,8]{1,0:T(1,128)S(1)}, s32[1,8]{1,0:T(1,128)}, u32[]{:S(2)}) copy-start(s32[1,8]{1,0:T(1,128)} %param.11) | copy-start | bytes 100
  65.3 245.5 %reduce-scatter.2.cloned.1.call-start = ((), (), s32[]{:S(2)}) async-start(), calls=%async_computation.3 | async-start | bytes 2621440 | tf_op jit(solution)/shard_map/reduce_scatter | solution.py:131
  247.6 2.3 copy-start.2
  247.6 2.3 copy-start.3
  252.0 1.4 copy-start.7
  252.0 1.5 copy-start.6
  252.0 2.9 copy-start.5
  253.6 3.0 copy-start.11
  255.0 3.3 %copy-start.4 = (bf16[2048,1,128]{0,2,1:T(8,128)(2,1)S(1)}, bf16[2048,1,128]{0,2,1:T(8,128)(2,1)}, u32[]{:S(2)}) copy-start(bf16[2048,1,128]{0,2,1:T(8,128)(2,1)} %copy.85) | copy-start | bytes 1572868
  260.2 52.8 %copy-start.1 = (bf16[8,2,256,256]{3,2,1,0:T(8,128)(2,1)S(1)}, bf16[8,2,256,256]{3,2,1,0:T(8,128)(2,1)}, u32[]{:S(2)}) copy-start(bf16[8,2,256,256]{3,2,1,0:T(8,128)(2,1)} %param.10) | copy-start | bytes 6291460
Sparse Core Ops, SparseCore 0:
  65.5 46.8 all-gather.2
  273.6 37.2 reduce-scatter.1
where the time goes:
time: 320 us
  waiting for transfers between devices  188 us (59%)
  local copies, waits for them, and re-layouts  41 us (13%)
  blocking collectives  34.1 us (11%)
  matrix products  21.8 us (7%)
  other arithmetic  15.1 us (5%)
  between operations  14.4 us (4%)
  starting transfers between devices  5.74 us (2%)
    all_to_all x1, waiting for transfers between devices, on_device(): lax.all_to_all(outgoing, 'store', split_axis=0, concat_axis=0, tiled=True)  150 us
    reduce_scatter x1, waiting for transfers between devices, on_device(): summed = lax.psum_scatter(partials, 'head', scatter_dimension=1, tiled=True)  37.4 us
    all_gather x1, blocking collectives, on_device(): wanted = lax.all_gather(passage_ids, 'store', axis=0, tiled=True)  34.1 us
    unnamed x38, local copies, waits for them, and re-layouts  22.6 us
    dot_general x1, matrix products, on_device(): product = jnp.dot(attention, flattened, preferred_element_type=jnp.float32)  13.2 us
  transfers between devices with their start and end apart: 3, of which 2 were waited for; matrix products, arithmetic and copies ran while one was open for 18% of the time, Pallas kernels for 0%

commit v1 on v0

v1 whole, which is shorter than its diff:
```python
import functools
import math

import jax
import jax.numpy as jnp
from jax import lax
from jax.experimental import pallas as pl
from jax.experimental.pallas import tpu as pltpu
from jax.sharding import PartitionSpec as P

HD = 128
BLK = 16
THETA = 1000000.0
SWAP = [(0, 1), (1, 0)]


def angle_tables(positions):
    half = HD // 2
    inverse_freq = jnp.exp(
        -(2.0 * jnp.arange(half, dtype=jnp.float32) / HD) * math.log(THETA)
    )
    angles = positions.astype(jnp.float32)[..., None] * inverse_freq
    cosine, sine = jnp.cos(angles), jnp.sin(angles)
    return (
        jnp.concatenate([cosine, cosine], axis=-1),
        jnp.concatenate([-sine, sine], axis=-1),
    )


def turn(x, cosine, sine):
    x = x.astype(jnp.float32)
    other = jnp.concatenate([x[:, HD // 2 :], x[:, : HD // 2]], axis=1)
    return (x * cosine + other * sine).astype(jnp.bfloat16)


def select_kernel(ids_ref, held_ref, out_ref, *, request):
    def step(dest, carry):
        for slot in range(ids_ref.shape[1]):
            out_ref[dest, slot] = held_ref[ids_ref[2 * dest + request, slot]]
        return carry

    lax.fori_loop(0, out_ref.shape[0], step, 0, unroll=4)


def select(ids, held, request):
    dests, slots = ids.shape[0] // 2, ids.shape[1]
    return pl.pallas_call(
        functools.partial(select_kernel, request=request),
        out_shape=jax.ShapeDtypeStruct((dests, slots, BLK, HD), jnp.bfloat16),
        in_specs=[
            pl.BlockSpec(memory_space=pltpu.SMEM),
            pl.BlockSpec(memory_space=pltpu.VMEM),
        ],
        out_specs=pl.BlockSpec(memory_space=pltpu.VMEM),
        cost_estimate=pl.CostEstimate(flops=0, bytes_accessed=4 << 20, transcendentals=0),
        name=f"select{request}",
    )(ids, held)


def rope_kernel(x_ref, cos_ref, sin_ref, out_ref):
    for part in range(out_ref.shape[0]):
        out_ref[part] = turn(x_ref[:, part * HD : (part + 1) * HD], cos_ref[...], sin_ref[...])


def rope_heads(rows, cosine, sine):
    tokens, width = rows.shape
    return pl.pallas_call(
        rope_kernel,
        out_shape=jax.ShapeDtypeStruct((width // HD, tokens, HD), jnp.bfloat16),
        name="rope_heads",
    )(rows, cosine, sine)


def attention_kernel(
    q_ref, near_v_ref, far_ref, cos_ref, sin_ref, out_ref, key_ref, *, group, heads
):
    tokens = near_v_ref.shape[0]
    far_len = key_ref.shape[0]
    blocks = far_ref.shape[0] // 2
    key_ref[...] = turn(
        far_ref[:blocks].reshape(far_len, HD), cos_ref[...], sin_ref[...]
    )
    far_v = far_ref[blocks:].reshape(far_len, HD)
    near_k = q_ref[heads]
    near_v = near_v_ref[...]
    rows = group * tokens
    shape = (group, tokens, tokens)
    allowed = (
        lax.broadcasted_iota(jnp.int32, shape, 1) >= lax.broadcasted_iota(jnp.int32, shape, 2)
    ).reshape(rows, tokens)
    factor = math.log2(math.e) / math.sqrt(HD)
    contract = (((1,), (1,)), ((), ()))
    for first in range(0, heads, group):
        q = q_ref[first : first + group].reshape(rows, HD)
        far_s = lax.dot_general(q, key_ref[...], contract, preferred_element_type=jnp.float32)
        near_s = lax.dot_general(q, near_k, contract, preferred_element_type=jnp.float32)
        near_s = jnp.where(allowed, near_s, -jnp.inf)
        row_max = jnp.maximum(
            jnp.max(far_s, axis=1, keepdims=True), jnp.max(near_s, axis=1, keepdims=True)
        )
        far_w = jnp.exp2((far_s - row_max) * factor)
        near_w = jnp.exp2((near_s - row_max) * factor)
        totals = jnp.sum(far_w, axis=1, keepdims=True) + jnp.sum(near_w, axis=1, keepdims=True)
        mixed = jnp.dot(far_w.astype(jnp.bfloat16), far_v, preferred_element_type=jnp.float32)
        mixed = mixed + jnp.dot(
            near_w.astype(jnp.bfloat16), near_v, preferred_element_type=jnp.float32
        )
        done = (mixed / totals).astype(jnp.bfloat16)
        for part in range(group):
            out_ref[:, (first + part) * HD : (first + part + 1) * HD] = done[
                part * tokens : (part + 1) * tokens
            ]


def attend(q_and_key, near_v, far, cosine, sine, request):
    heads = q_and_key.shape[0] - 1
    tokens = near_v.shape[0]
    far_len = cosine.shape[0]
    return pl.pallas_call(
        functools.partial(attention_kernel, group=2, heads=heads),
        out_shape=jax.ShapeDtypeStruct((tokens, heads * HD), jnp.bfloat16),
        scratch_shapes=[pltpu.VMEM((far_len, HD), jnp.bfloat16)],
        compiler_params=pltpu.CompilerParams(vmem_limit_bytes=40 << 20),
        cost_estimate=pl.CostEstimate(
            flops=4 * heads * tokens * (far_len + tokens) * HD,
            bytes_accessed=4 << 20,
            transcendentals=heads * tokens * (far_len + tokens),
        ),
        name=f"attend{request}",
    )(q_and_key, near_v, far, cosine, sine)


def on_device(queries, span_keys, span_values, page_cache, passage_ids, starts, out_weight):
    stores = lax.axis_size("store")
    rep = lax.axis_index("rep")
    per_store, _, page_len, row_width = page_cache.shape
    pass_count = passage_ids.shape[1]
    tokens = queries.shape[1]
    half_width = queries.shape[2] // 2
    page_blocks = page_len // BLK

    both = jnp.concatenate([passage_ids, starts], axis=1)
    everyone = lax.all_to_all(
        jnp.broadcast_to(both, (2 * stores, 2 * pass_count)), ("store", "rep"), 0, 0, tiled=True
    )
    ids = everyone[:, :pass_count]

    own_head = lax.dynamic_slice_in_dim(page_cache, rep * HD, HD, axis=3)
    slices = own_head.reshape(per_store, 2, page_blocks, BLK, HD).transpose(1, 2, 0, 3, 4)
    held = lax.all_to_all(
        slices.reshape(stores, per_store, BLK, HD), "store", 0, 0, tiled=True
    ).reshape(stores * per_store, BLK, HD)

    far = [
        lax.all_to_all(select(ids, held, request), "store", 0, 0, tiled=True)
        for request in range(2)
    ]


    def head_part(which):
        return jnp.concatenate(
            [
                lax.dynamic_slice_in_dim(queries[0], which * half_width, half_width, axis=1),
                lax.dynamic_slice_in_dim(span_keys[0], which * HD, HD, axis=1),
                lax.dynamic_slice_in_dim(span_values[0], which * HD, HD, axis=1),
            ],
            axis=1,
        )

    kept = head_part(rep)
    swapped = lax.ppermute(head_part(1 - rep), "rep", SWAP)
    spans = [jnp.where(rep == 0, kept, swapped), jnp.where(rep == 0, swapped, kept)]
    own_store = lax.axis_index("store")
    chip_starts = lax.dynamic_slice_in_dim(everyone, 2 * own_store, 2, axis=0)[:, pass_count:]

    weight = out_weight[:, :, 0, :].transpose(1, 0, 2)
    head_count = weight.shape[0]
    block = jnp.arange(page_blocks, dtype=jnp.int32)[:, None, None] * BLK
    token = jnp.arange(BLK, dtype=jnp.int32)[None, None, :]
    results = []
    for request in range(2):
        begins = chip_starts[request]
        query_pos = jnp.min(begins) + pass_count * page_len + jnp.arange(tokens, dtype=jnp.int32)
        rotated = rope_heads(spans[request][:, : half_width + HD], *angle_tables(query_pos))
        far_pos = (block + token + begins[None, :, None]).reshape(-1)
        own_att = attend(
            rotated, spans[request][:, half_width + HD :], far[request],
            *angle_tables(far_pos), request,
        )
        other_att = lax.ppermute(own_att, "rep", SWAP)
        att = jnp.where(
            rep == 0,
            jnp.concatenate([own_att, other_att], axis=1),
            jnp.concatenate([other_att, own_att], axis=1),
        )
        partial = jnp.einsum("tk,hkn->htn", att, weight, preferred_element_type=jnp.float32)
        parts = lax.all_to_all(partial.astype(jnp.bfloat16), "head", 0, 0, tiled=True)
        results.append(jnp.sum(parts.astype(jnp.float32), axis=0).astype(jnp.bfloat16))

    mine = jnp.where(rep == 0, results[0], results[1])
    to_zero = lax.ppermute(results[0], "rep", [(1, 0)])
    to_one = lax.ppermute(results[1], "rep", [(0, 1)])
    other = jnp.where(rep == 0, to_zero, to_one)
    return jnp.where(
        rep == 0,
        jnp.concatenate([mine, other], axis=1),
        jnp.concatenate([other, mine], axis=1),
    )[None]


def solution(mesh):
    return jax.shard_map(
        on_device,
        mesh=mesh,
        in_specs=(
            P(("store", "rep"), None, "head"),
            P(("store", "rep"), None, "head"),
            P(("store", "rep"), None, "head"),
            P("store", None, None, "head"),
            P(("store", "rep"), None),
            P(("store", "rep"), None),
            P("head", None, "rep", None),
        ),
        out_specs=P(("store", "rep"), None, "head"),
        check_vma=False,
    )
```

time: 320 us -> 178 us (0.56)
  waiting for transfers between devices: 188 us -> 31.4 us
  starting transfers between devices: 5.74 us -> 46.5 us
  local copies, waits for them, and re-layouts: 41 us -> 11.7 us
  Pallas kernels: 0 us -> 18.2 us
  between operations: 14.4 us -> 1.51 us
  other arithmetic: 15.1 us -> 24.3 us
  matrix products: 21.8 us -> 14.7 us
  blocking collectives: 34.1 us -> 28.9 us
    all_to_all x1 -> x5, waiting for transfers between devices: 150 us -> 30.5 us  [the longest x2 14.3 us: on_device(): lax.all_to_all(select(ids, held, request), 'store', 0, 0, tiled=True)]
    reduce_scatter x1 -> x0, waiting for transfers between devices: 37.4 us -> none  [on_device(): summed = lax.psum_scatter(partials, 'head', scatter_dimension=1, tiled=True)]
    all_gather x1 -> x0, blocking collectives: 34.1 us -> none  [on_device(): wanted = lax.all_gather(passage_ids, 'store', axis=0, tiled=True)]
    all_to_all x1 -> x5, starting transfers between devices: 5.66 us -> 37.2 us  [the longest x2 16.6 us: on_device(): lax.all_to_all(select(ids, held, request), 'store', 0, 0, tiled=True)]
    all_to_all x0 -> x1, blocking collectives: none -> 28.9 us  [on_device(): lax.all_to_all(slices.reshape(stores, per_store, BLK, HD), 'store', 0, 0,...]
    pallas_call x0 -> x6, Pallas kernels: none -> 18.2 us  [the longest x2 9.39 us: attend(): pl.pallas_call(functools.partial(attention_kernel, group=2, heads=heads),...]
    unnamed x38 -> x24, local copies, waits for them, and re-layouts: 22.6 us -> 5.62 us
    neg x0 -> x2, other arithmetic: none -> 10.5 us  [angle_tables(): -sine]
  transfers between devices with their start and end apart: 3 -> 10, of which waited for: 2 -> 5; matrix products, arithmetic and copies ran while one was open for 18% -> 24% of each run, Pallas kernels for 0% -> 9%
where the time goes in v1:
time: 178 us; the launch traced here: 177 us
  starting transfers between devices  46.5 us (26%)
  waiting for transfers between devices  31.4 us (18%)
  blocking collectives  28.9 us (16%)
  other arithmetic  24.3 us (14%)
  Pallas kernels  18.2 us (10%)
  matrix products  14.7 us (8%)
  local copies, waits for them, and re-layouts  11.7 us (7%)
    all_to_all x1, blocking collectives, on_device(): lax.all_to_all(slices.reshape(stores, per_store, BLK, HD), 'store', 0, 0,...  28.9 us
    all_to_all x2, starting transfers between devices, on_device(): lax.all_to_all(select(ids, held, request), 'store', 0, 0, tiled=True)  16.6 us
    dot_general x2, matrix products, on_device(): jnp.einsum('tk,hkn->htn', att, weight, preferred_element_type=jnp.float32)  14.7 us
    all_to_all x2, waiting for transfers between devices, on_device(): lax.all_to_all(select(ids, held, request), 'store', 0, 0, tiled=True)  14.3 us
    all_to_all x1, starting transfers between devices, on_device(): lax.all_to_all(jnp.broadcast_to(both, (2 * stores, 2 * pass_count)), ('st...  13.2 us
    neg x2, other arithmetic, angle_tables(): -sine  10.5 us
    pallas_call x2, Pallas kernels, attend(): pl.pallas_call(functools.partial(attention_kernel, group=2, heads=heads),...  9.39 us
    all_to_all x1, waiting for transfers between devices, on_device(): lax.all_to_all(jnp.broadcast_to(both, (2 * stores, 2 * pass_count)), ('st...  8.7 us
  transfers between devices with their start and end apart: 10, of which 5 were waited for; matrix products, arithmetic and copies ran while one was open for 24% of the time, Pallas kernels for 9%

profile of v1, /device:TPU:1, one launch (start us, length us, event | category | flops | bytes accessed | tf_op | source)
XLA Modules:
  0.0 177.3 jit_solution(1490629319242559035)
XLA Ops:
  1.5 13.2 %all-to-all-start = ((s32[64,1,16]{2,1,0:T(1,128)}), s32[64,1,16]{2,1,0:T(1,128)S(1)}, u32[]{:S(2)}, u32[]{:S(2)}) async-start(s32[64,1,16]{2,1,0:T(1,128)} %broadcast_in_dim.2), calls=%async_computation | async-start | bytes 65536 | tf_op jit(solution)/shard_map/all_to_all | solution.py:143
  15.2 8.7 %all-to-all-done = s32[64,1,16]{2,1,0:T(1,128)S(1)} async-done(((s32[64,1,16]{2,1,0:T(1,128)}), s32[64,1,16]{2,1,0:T(1,128)S(1)}, u32[]{:S(2)}, u32[]{:S(2)}) %all-to-all-start) | async-done | bytes 4128 | tf_op jit(solution)/shard_map/all_to_all | solution.py:143
  23.9 28.9 %all_to_all.34 = bf16[32,8,16,128]{3,2,1,0:T(8,128)(2,1)} all-to-all(bf16[32,8,16,128]{3,2,1,0:T(8,128)(2,1)S(1)} %copy.13), channel_id=1, replica_groups=mesh['store'=32,'head'=4,'rep'=2] {'store'}, dimensions={0} | all-to-all | bytes 2097152 | tf_op jit(solution)/shard_map/all_to_all | solution.py:150
  52.8 2.5 %select1.1 = bf16[32,8,16,128]{3,2,1,0:T(8,128)(2,1)} custom-call(s32[64,8]{1,0:T(8,128)} %bitcast.47, bf16[256,16,128]{2,1,0:T(8,128)(2,1)} %bitcast.44), custom_call_target="tpu_custom_call" | custom-call | bytes 4194304 | tf_op jit(solution)/shard_map/select1/pallas_call | solution.py:47
  55.3 8.0 %all-to-all-start.4 = ((bf16[32,8,16,128]{3,2,1,0:T(8,128)(2,1)}), bf16[32,8,16,128]{3,2,1,0:T(8,128)(2,1)S(1)}, u32[]{:S(2)}, u32[]{:S(2)}) async-start(bf16[32,8,16,128]{3,2,1,0:T(8,128)(2,1)} %select1.1), calls=%async_computation.4 | async-start | bytes 2097152 | tf_op jit(solution)/shard_map/all_to_all | solution.py:155
  63.4 1.8 %dynamic-slice_bitcast_fusion.1 = (bf16[128,1024]{1,0:T(8,128)(2,1)}, bf16[128,1024]{1,0:T(8,128)(2,1)S(1)}) fusion(bf16[1,128,2048]{2,1,0:T(8,128)(2,1)} %param.7, s32[]{:T(128)S(6)} %select_n.82, s32[]{:T(128)S(6)} %select_n.84), kind=kLoop, calls=%fused_computation.40 | loop fusion | bytes 1048584 | tf_op jit(solution)/shard_map/dynamic_slice | solution.py:163
  65.9 1.5 collective-permute-start
  70.2 1.0 fusion.35
  71.2 2.6 %select0.1 = bf16[32,8,16,128]{3,2,1,0:T(8,128)(2,1)} custom-call(s32[64,8]{1,0:T(8,128)} %bitcast.48, bf16[256,16,128]{2,1,0:T(8,128)(2,1)} %bitcast.45), custom_call_target="tpu_custom_call" | custom-call | bytes 4194304 | tf_op jit(solution)/shard_map/select0/pallas_call | solution.py:47
  73.8 14.3 %all-to-all-done.4.far_ref = bf16[32,8,16,128]{3,2,1,0:T(8,128)(2,1)S(1)} async-done(((bf16[32,8,16,128]{3,2,1,0:T(8,128)(2,1)}), bf16[32,8,16,128]{3,2,1,0:T(8,128)(2,1)S(1)}, u32[]{:S(2)}, u32[]{:S(2)}) %all-to-all-start.4) | async-done | bytes 1048608 | tf_op jit(solution)/shard_map/all_to_all | solution.py:155
  88.0 8.6 %all-to-all-start.2 = ((bf16[32,8,16,128]{3,2,1,0:T(8,128)(2,1)}), bf16[32,8,16,128]{3,2,1,0:T(8,128)(2,1)}, u32[]{:S(2)}, u32[]{:S(2)}) async-start(bf16[32,8,16,128]{3,2,1,0:T(8,128)(2,1)} %select0.1), calls=%async_computation.2 | async-start | bytes 2097152 | tf_op jit(solution)/shard_map/all_to_all | solution.py:155
  98.4 9.5 %fusion.33 = (f32[2048,64]{1,0:T(8,128)S(1)}, f32[2048,64]{1,0:T(8,128)S(1)}, f32[2048,64]{1,0:T(8,128)S(1)}, f32[2048,64]{1,0:T(8,128)}, f32[2048,64]{1,0:T(8,128)}, /*index=5*/f32[2048,64]{1,0:T(8,128)}) fusion(f32[64]{0:T(128)} %copy-done.11, f32[2048]{0:T(1024)S(1)} %convert_element_type.57, f32[2048]{0:T(1024)S(1)} %convert_element_type.52), kind=kLoop, calls=%fused_computation.33 | loop fusion | flops 524288 | bytes 3162368 | tf_op jit(solution)/shard_map/neg | solution.py:26
  108.7 1.6 pad_maximum_fusion.2
  110.2 1.9 %broadcast_select_fusion = (bf16[128,1280]{1,0:T(8,128)(2,1)S(1)}, bf16[128,1280]{1,0:T(8,128)(2,1)}) fusion(bf16[128,1280]{1,0:T(8,128)(2,1)} %collective-permute-done, pred[]{:T(512)S(6)} %eq.2, bf16[128,128]{1,0:T(8,128)(2,1)S(1)} %get-tuple-element.13, bf16[128,128]{1,0:T(8,128)(2,1)S(1)} %get-tuple-element.38, bf16[128,1024]{1,0:T(8,128)(2,1)} %get-tuple-element.9), kind=kLoop, calls=%fused_computation.36 | loop fusion | flops 1310720 | bytes 1310721 | tf_op jit(solution)/shard_map/jit(_where)/select_n | solution.py:172
  112.9 1.9 %rope_heads.3.q_ref = bf16[9,128,128]{2,1,0:T(8,128)(2,1)} custom-call(bf16[128,1152]{1,0:T(8,128)(2,1)} %slice.34.x_ref, f32[128,128]{1,0:T(8,128)} %get-tuple-element.41.cos_ref, f32[128,128]{1,0:T(8,128)} %get-tuple-element.42.sin_ref), custom_call_target="tpu_custom_call" | custom-call | tf_op jit(solution)/shard_map/rope_heads/pallas_call | solution.py:67
  114.8 1.2 copy-done.1
  116.0 1.2 copy-done.4
  118.2 3.7 %attend1.1 = bf16[128,1024]{1,0:T(8,128)(2,1)S(1)} custom-call(bf16[9,128,128]{2,1,0:T(8,128)(2,1)S(1)} %copy-done.6, bf16[128,128]{1,0:T(8,128)(2,1)S(1)} %slice.35.near_v_ref, bf16[32,8,16,128]{3,2,1,0:T(8,128)(2,1)S(1)} %copy-done.4, f32[2048,128]{1,0:T(8,128)S(1)} %get-tuple-element.45.cos_ref, f32[2048,128]{1,0:T(8,128)S(1)} %copy-done.1), custom_call_target="tpu_custom_call" | custom-call | flops 1140850688 | bytes 4194304 | tf_op jit(solution)/shard_map/attend1/pallas_call | solution.py:119
  121.9 1.7 collective-permute-start.2
  123.6 3.7 %pad_maximum_fusion = (f32[2048,128]{1,0:T(8,128)S(1)}, f32[2048,128]{1,0:T(8,128)}) fusion(f32[2048,64]{1,0:T(8,128)} %get-tuple-element.31, f32[2048,64]{1,0:T(8,128)} %get-tuple-element.32, f32[2048,64]{1,0:T(8,128)} %get-tuple-element.33), kind=kLoop, calls=%fused_computation.12 | loop fusion | flops 524288 | bytes 3670016 | tf_op jit(solution)/shard_map/concatenate | solution.py:25
  127.4 1.6 pad_maximum_fusion.6
  129.8 1.9 %rope_heads.2.q_ref = bf16[9,128,128]{2,1,0:T(8,128)(2,1)} custom-call(bf16[128,1152]{1,0:T(8,128)(2,1)} %slice.31.x_ref, f32[128,128]{1,0:T(8,128)} %get-tuple-element.39.cos_ref, f32[128,128]{1,0:T(8,128)} %get-tuple-element.40.sin_ref), custom_call_target="tpu_custom_call" | custom-call | tf_op jit(solution)/shard_map/rope_heads/pallas_call | solution.py:67
  131.7 1.2 copy-done.2
  133.8 5.7 %attend0.1 = bf16[128,1024]{1,0:T(8,128)(2,1)} custom-call(bf16[9,128,128]{2,1,0:T(8,128)(2,1)S(1)} %copy-done.5, bf16[128,128]{1,0:T(8,128)(2,1)S(1)} %slice.32.near_v_ref, bf16[32,8,16,128]{3,2,1,0:T(8,128)(2,1)} %all-to-all-done.2.far_ref, f32[2048,128]{1,0:T(8,128)S(1)} %get-tuple-element.43.cos_ref, f32[2048,128]{1,0:T(8,128)S(1)} %copy-done.2), custom_call_target="tpu_custom_call" | custom-call | flops 1140850688 | bytes 4194304 | tf_op jit(solution)/shard_map/attend0/pallas_call | solution.py:119
  139.5 7.4 %fusion.10 = bf16[4,128,512]{2,1,0:T(8,128)(2,1)} fusion(bf16[4,2048,512]{2,0,1:T(4,128)(2,1)} %bitcast.50, bf16[128,1024]{1,0:T(8,128)(2,1)} %collective-permute-done.2, bf16[128,1024]{1,0:T(8,128)(2,1)S(1)} %attend1.1, pred[]{:T(512)S(6)} %eq.2), kind=kOutput, calls=%fused_computation.10 | convolution fusion | flops 1076363264 | bytes 9437185 | tf_op jit(solution)/shard_map/tk,hkn->htn/dot_general | solution.py:196
  146.9 4.0 %all-to-all-start.5 = ((bf16[4,128,512]{2,1,0:T(8,128)(2,1)}), bf16[4,128,512]{2,1,0:T(8,128)(2,1)S(1)}, u32[]{:S(2)}, u32[]{:S(2)}) async-start(bf16[4,128,512]{2,1,0:T(8,128)(2,1)} %fusion.10), calls=%async_computation.5 | async-start | bytes 1048576 | tf_op jit(solution)/shard_map/all_to_all | solution.py:197
  150.9 7.4 %fusion.13 = bf16[4,128,512]{2,1,0:T(8,128)(2,1)} fusion(bf16[4,2048,512]{2,0,1:T(4,128)(2,1)} %bitcast.51, bf16[128,1024]{1,0:T(8,128)(2,1)S(1)} %collective-permute-done.1, bf16[128,1024]{1,0:T(8,128)(2,1)} %attend0.1, pred[]{:T(512)S(6)} %eq.2), kind=kOutput, calls=%fused_computation.11 | convolution fusion | flops 1076363264 | bytes 9437185 | tf_op jit(solution)/shard_map/tk,hkn->htn/dot_general | solution.py:196
  158.3 1.4 all-to-all-done.5
  159.7 3.5 %all-to-all-start.3 = ((bf16[4,128,512]{2,1,0:T(8,128)(2,1)}), bf16[4,128,512]{2,1,0:T(8,128)(2,1)S(1)}, u32[]{:S(2)}, u32[]{:S(2)}) async-start(bf16[4,128,512]{2,1,0:T(8,128)(2,1)} %fusion.13), calls=%async_computation.3 | async-start | bytes 1048576 | tf_op jit(solution)/shard_map/all_to_all | solution.py:197
  163.2 1.3 collective-permute-start.4
  164.5 6.1 %all-to-all-done.3 = bf16[4,128,512]{2,1,0:T(8,128)(2,1)S(1)} async-done(((bf16[4,128,512]{2,1,0:T(8,128)(2,1)}), bf16[4,128,512]{2,1,0:T(8,128)(2,1)S(1)}, u32[]{:S(2)}, u32[]{:S(2)}) %all-to-all-start.3) | async-done | bytes 524320 | tf_op jit(solution)/shard_map/all_to_all | solution.py:197
  170.8 4.8 %collective-permute-start.3 = (bf16[128,512]{1,0:T(8,128)(2,1)S(1)}, bf16[128,512]{1,0:T(8,128)(2,1)S(1)}, u32[]{:S(2)}, u32[]{:S(2)}) collective-permute-start(bf16[128,512]{1,0:T(8,128)(2,1)S(1)} %reduce_sum.24), channel_id=1, source_target_pairs={{1,0},{3,2},{5,4},{7,6},{9,8},{11,10},{13,12},{15,14},{17,16},{19,... | collective-permute-start | bytes 393224 | tf_op jit(solution)/shard_map/ppermute | solution.py:201
  (54 shorter events, 12.2 us)
Async XLA Ops:
  0.0 14.7 %copy-start = (bf16[8,2,256,256]{3,2,1,0:T(8,128)(2,1)S(1)}, bf16[8,2,256,256]{3,2,1,0:T(8,128)(2,1)}, u32[]{:S(2)}) copy-start(bf16[8,2,256,256]{3,2,1,0:T(8,128)(2,1)} %param.10) | copy-start | bytes 6291460
  0.0 63.3 %copy-start.10 = (bf16[1,128,256]{2,1,0:T(8,128)(2,1)S(1)}, bf16[1,128,256]{2,1,0:T(8,128)(2,1)}, u32[]{:S(2)}) copy-start(bf16[1,128,256]{2,1,0:T(8,128)(2,1)} %param.8) | copy-start | bytes 196612
  0.0 63.3 %copy-start.9 = (bf16[1,128,256]{2,1,0:T(8,128)(2,1)S(1)}, bf16[1,128,256]{2,1,0:T(8,128)(2,1)}, u32[]{:S(2)}) copy-start(bf16[1,128,256]{2,1,0:T(8,128)(2,1)} %param.9) | copy-start | bytes 196612
  1.5 22.4 %all-to-all-start = ((s32[64,1,16]{2,1,0:T(1,128)}), s32[64,1,16]{2,1,0:T(1,128)S(1)}, u32[]{:S(2)}, u32[]{:S(2)}) async-start(s32[64,1,16]{2,1,0:T(1,128)} %broadcast_in_dim.2), calls=%async_computation | async-start | bytes 65536 | tf_op jit(solution)/shard_map/all_to_all | solution.py:143
  23.9 28.9 %copy-start.8 = (s32[64,1,16]{2,1,0:T(1,128)}, s32[64,1,16]{2,1,0:T(1,128)S(1)}, u32[]{:S(2)}) copy-start(s32[64,1,16]{2,1,0:T(1,128)S(1)} %all-to-all-done) | copy-start | bytes 12292
  55.3 32.7 %all-to-all-start.4 = ((bf16[32,8,16,128]{3,2,1,0:T(8,128)(2,1)}), bf16[32,8,16,128]{3,2,1,0:T(8,128)(2,1)S(1)}, u32[]{:S(2)}, u32[]{:S(2)}) async-start(bf16[32,8,16,128]{3,2,1,0:T(8,128)(2,1)} %select1.1), calls=%async_computation.4 | async-start | bytes 2097152 | tf_op jit(solution)/shard_map/all_to_all | solution.py:155
  65.9 44.3 %collective-permute-start = (bf16[128,1280]{1,0:T(8,128)(2,1)}, bf16[128,1280]{1,0:T(8,128)(2,1)}, u32[]{:S(2)}, u32[]{:S(2)}) collective-permute-start(bf16[128,1280]{1,0:T(8,128)(2,1)} %pad_maximum_fusion.5), channel_id=1, source_target_pairs={{0,1},{1,0},{2,3},{3,2},{4,5},{5,4},{6,7},{7,6},{8,9},{9,8},{10,11... | collective-permute-start | bytes 983048 | tf_op jit(solution)/shard_map/ppermute | solution.py:171
  67.4 29.2 %copy-start.11 = (f32[64]{0:T(128)}, f32[64]{0:T(128)S(1)}, u32[]{:S(2)}) copy-start(f32[64]{0:T(128)S(1)} %multiply_exponential_fusion) | copy-start | bytes 772
  88.0 20.6 %copy-start.3 = (bf16[32,8,16,128]{3,2,1,0:T(8,128)(2,1)}, bf16[32,8,16,128]{3,2,1,0:T(8,128)(2,1)S(1)}, u32[]{:S(2)}) copy-start(bf16[32,8,16,128]{3,2,1,0:T(8,128)(2,1)S(1)} %all-to-all-done.4.far_ref) | copy-start | bytes 3145732
  88.0 43.6 %all-to-all-start.2 = ((bf16[32,8,16,128]{3,2,1,0:T(8,128)(2,1)}), bf16[32,8,16,128]{3,2,1,0:T(8,128)(2,1)}, u32[]{:S(2)}, u32[]{:S(2)}) async-start(bf16[32,8,16,128]{3,2,1,0:T(8,128)(2,1)} %select0.1), calls=%async_computation.2 | async-start | bytes 2097152 | tf_op jit(solution)/shard_map/all_to_all | solution.py:155
  114.8 1.2 copy-start.1
  116.0 1.2 copy-start.4
  117.2 1.0 copy-start.6
  118.2 10.8 %copy-start.7 = (bf16[128,1280]{1,0:T(8,128)(2,1)S(1)}, bf16[128,1280]{1,0:T(8,128)(2,1)}, u32[]{:S(2)}) copy-start(bf16[128,1280]{1,0:T(8,128)(2,1)} %get-tuple-element.8) | copy-start | bytes 983044
  121.9 17.6 %collective-permute-start.2 = (bf16[128,1024]{1,0:T(8,128)(2,1)S(1)}, bf16[128,1024]{1,0:T(8,128)(2,1)}, u32[]{:S(2)}, u32[]{:S(2)}) collective-permute-start(bf16[128,1024]{1,0:T(8,128)(2,1)S(1)} %attend1.1), channel_id=1, source_target_pairs={{0,1},{1,0},{2,3},{3,2},{4,5},{5,4},{6,7},{7,6},{8,9},{9,8},{10,11... | collective-permute-start | bytes 786440 | tf_op jit(solution)/shard_map/ppermute | solution.py:190
  131.7 1.2 copy-start.2
  132.9 1.0 copy-start.5
  139.5 11.4 %collective-permute-start.1 = (bf16[128,1024]{1,0:T(8,128)(2,1)}, bf16[128,1024]{1,0:T(8,128)(2,1)S(1)}, u32[]{:S(2)}, u32[]{:S(2)}) collective-permute-start(bf16[128,1024]{1,0:T(8,128)(2,1)} %attend0.1), channel_id=1, source_target_pairs={{0,1},{1,0},{2,3},{3,2},{4,5},{5,4},{6,7},{7,6},{8,9},{9,8},{10,11... | collective-permute-start | bytes 786440 | tf_op jit(solution)/shard_map/ppermute | solution.py:190
  146.9 12.8 %all-to-all-start.5 = ((bf16[4,128,512]{2,1,0:T(8,128)(2,1)}), bf16[4,128,512]{2,1,0:T(8,128)(2,1)S(1)}, u32[]{:S(2)}, u32[]{:S(2)}) async-start(bf16[4,128,512]{2,1,0:T(8,128)(2,1)} %fusion.10), calls=%async_computation.5 | async-start | bytes 1048576 | tf_op jit(solution)/shard_map/all_to_all | solution.py:197
  159.7 11.0 %all-to-all-start.3 = ((bf16[4,128,512]{2,1,0:T(8,128)(2,1)}), bf16[4,128,512]{2,1,0:T(8,128)(2,1)S(1)}, u32[]{:S(2)}, u32[]{:S(2)}) async-start(bf16[4,128,512]{2,1,0:T(8,128)(2,1)} %fusion.13), calls=%async_computation.3 | async-start | bytes 1048576 | tf_op jit(solution)/shard_map/all_to_all | solution.py:197
  163.2 12.3 %collective-permute-start.4 = (bf16[128,512]{1,0:T(8,128)(2,1)S(1)}, bf16[128,512]{1,0:T(8,128)(2,1)S(1)}, u32[]{:S(2)}, u32[]{:S(2)}) collective-permute-start(bf16[128,512]{1,0:T(8,128)(2,1)S(1)} %reduce_sum.25), channel_id=1, source_target_pairs={{0,1},{2,3},{4,5},{6,7},{8,9},{10,11},{12,13},{14,15},{16,17},{18,... | collective-permute-start | bytes 393224 | tf_op jit(solution)/shard_map/ppermute | solution.py:202
  170.8 5.8 %collective-permute-start.3 = (bf16[128,512]{1,0:T(8,128)(2,1)S(1)}, bf16[128,512]{1,0:T(8,128)(2,1)S(1)}, u32[]{:S(2)}, u32[]{:S(2)}) collective-permute-start(bf16[128,512]{1,0:T(8,128)(2,1)S(1)} %reduce_sum.24), channel_id=1, source_target_pairs={{1,0},{3,2},{5,4},{7,6},{9,8},{11,10},{13,12},{15,14},{17,16},{19,... | collective-permute-start | bytes 393224 | tf_op jit(solution)/shard_map/ppermute | solution.py:201

commit v2 on v1

v2 whole, which is shorter than its diff:
```python
import functools
import math

import jax
import jax.numpy as jnp
from jax import lax
from jax.experimental import pallas as pl
from jax.experimental.pallas import tpu as pltpu
from jax.sharding import PartitionSpec as P

HD = 128
BLK = 16
IDS = 8
FULL = 50 << 20
GROUP = 2
THETA = 1000000.0
SWAP = [(0, 1), (1, 0)]
ANY = pl.BlockSpec(memory_space=pl.ANY)
SMEM = pl.BlockSpec(memory_space=pltpu.SMEM)
VMEM = pl.BlockSpec(memory_space=pltpu.VMEM)
HBM = pl.BlockSpec(memory_space=pltpu.HBM)


def cost(flops, moved, trans=0):
    return pl.CostEstimate(flops=flops, bytes_accessed=moved, transcendentals=trans)


def angle_tables(positions):
    half = HD // 2
    lane = jnp.arange(HD, dtype=jnp.int32)
    inverse_freq = jnp.exp(
        -(2.0 * (lane % half).astype(jnp.float32) / HD) * math.log(THETA)
    )
    angles = positions.astype(jnp.float32)[..., None] * inverse_freq
    return jnp.cos(angles), jnp.where(lane < half, -1.0, 1.0) * jnp.sin(angles)


def turn(x, cosine, sine):
    x = x.astype(jnp.float32)
    other = jnp.concatenate([x[:, HD // 2 :], x[:, : HD // 2]], axis=1)
    return (x * cosine + other * sine).astype(jnp.bfloat16)


def pack_kernel(own_ref, other_ref, cache_ref, out_ref, held_ref, rows_ref, sems, out_sems):
    passages, kinds, page_len, _ = cache_ref.shape
    blocks = page_len // BLK
    rep = lax.axis_index("rep")
    lanes = pl.ds(pl.multiple_of(rep * HD, HD), HD)
    copies = [
        pltpu.make_async_copy(cache_ref.at[:, kind, :, lanes], held_ref.at[kind], sems.at[kind])
        for kind in range(kinds)
    ]
    for copy in copies:
        copy.start()
    row = lax.broadcasted_iota(jnp.int32, (IDS, HD), 0)
    lane = lax.broadcasted_iota(jnp.int32, (IDS, HD), 1)
    named = jnp.zeros((IDS, HD), jnp.int32)
    for slot in range(own_ref.shape[1]):
        named = jnp.where((row == rep) & (lane == slot), own_ref[0, slot], named)
        named = jnp.where((row == 1 - rep) & (lane == slot), other_ref[0, slot], named)
    named = named.astype(jnp.float32).astype(jnp.bfloat16)
    outs = []
    for kind in range(kinds):
        copies[kind].wait()
        for block in range(blocks):
            for passage in range(passages):
                rows_ref[kind * blocks + block, passage * BLK : (passage + 1) * BLK] = held_ref[
                    kind, passage, block * BLK : (block + 1) * BLK
                ]
            rows_ref[kind * blocks + block, passages * BLK :] = named
        part = pl.ds(kind * blocks, blocks)
        outs.append(
            pltpu.make_async_copy(rows_ref.at[part], out_ref.at[part], out_sems.at[kind])
        )
        outs[kind].start()
    for copy in outs:
        copy.wait()


def pack(own_ids, other_ids, page_cache):
    passages, kinds, page_len, _ = page_cache.shape
    shape = (kinds * page_len // BLK, passages * BLK + IDS, HD)
    return pl.pallas_call(
        pack_kernel,
        out_shape=jax.ShapeDtypeStruct(shape, jnp.bfloat16),
        in_specs=[SMEM, SMEM, HBM],
        out_specs=HBM,
        scratch_shapes=[
            pltpu.VMEM((kinds, passages, page_len, HD), jnp.bfloat16),
            pltpu.VMEM(shape, jnp.bfloat16),
            pltpu.SemaphoreType.DMA((kinds,)),
            pltpu.SemaphoreType.DMA((kinds,)),
        ],
        compiler_params=pltpu.CompilerParams(vmem_limit_bytes=FULL),
        cost_estimate=cost(0, 2 << 20),
        name="pack",
    )(own_ids, other_ids, page_cache)


def select_kernel(ids_ref, held_ref, out_ref, chosen_ref, sems):
    stores, requests, slots = out_ref.shape[:3]
    passages = (held_ref.shape[1] - IDS) // BLK
    shift = passages.bit_length() - 1
    assert passages == 1 << shift
    rep = lax.axis_index("rep")
    chunks = sems.shape[0]
    per = stores // chunks
    copies = []
    for chunk in range(chunks):

        def step(at, carry):
            dest = chunk * per + at
            for request in range(requests):
                row = dest * requests + (rep ^ request)
                for slot in range(slots):
                    wanted = ids_ref[row, slot]
                    start = pl.multiple_of((wanted & (passages - 1)) * BLK, BLK)
                    chosen_ref[dest, request, slot] = held_ref[
                        lax.shift_right_logical(wanted, shift), pl.ds(start, BLK)
                    ]
            return carry

        lax.fori_loop(0, per, step, 0, unroll=True)
        part = pl.ds(chunk * per, per)
        copy = pltpu.make_async_copy(chosen_ref.at[part], out_ref.at[part], sems.at[chunk])
        copy.start()
        copies.append(copy)
    for copy in copies:
        copy.wait()


def select(ids, held, stores):
    slots = ids.shape[1]
    requests = ids.shape[0] // stores
    shape = (stores, requests, slots, BLK, HD)
    return pl.pallas_call(
        select_kernel,
        out_shape=jax.ShapeDtypeStruct(shape, jnp.bfloat16),
        in_specs=[SMEM, VMEM],
        out_specs=HBM,
        scratch_shapes=[pltpu.VMEM(shape, jnp.bfloat16), pltpu.SemaphoreType.DMA((8,))],
        compiler_params=pltpu.CompilerParams(vmem_limit_bytes=8 << 20),
        cost_estimate=cost(0, 2 << 20),
        name="select",
    )(ids, held)


def split_kernel(q_ref, k_ref, v_ref, kept_ref, sent_ref):
    rep = lax.axis_index("rep")
    width = q_ref.shape[2] // 2
    for chosen in range(2):

        @pl.when(rep == chosen)
        def _():
            for part, out_ref in ((chosen, kept_ref), (1 - chosen, sent_ref)):
                out_ref[:, :width] = q_ref[0, :, part * width : (part + 1) * width]
                out_ref[:, width : width + HD] = k_ref[0, :, part * HD : (part + 1) * HD]
                out_ref[:, width + HD :] = v_ref[0, :, part * HD : (part + 1) * HD]


def split_heads(queries, span_keys, span_values):
    tokens = queries.shape[1]
    width = queries.shape[2] // 2 + 2 * HD
    shape = jax.ShapeDtypeStruct((tokens, width), jnp.bfloat16)
    return pl.pallas_call(
        split_kernel,
        out_shape=(shape, shape),
        in_specs=[VMEM] * 3,
        out_specs=(VMEM, VMEM),
        compiler_params=pltpu.CompilerParams(vmem_limit_bytes=8 << 20),
        cost_estimate=cost(0, 2 << 20),
        name="split_heads",
    )(queries, span_keys, span_values)


def rope_kernel(kept_ref, got_ref, cos_ref, sin_ref, out_ref):
    heads = out_ref.shape[1] - 1
    for request, x_ref in enumerate((kept_ref, got_ref)):
        for part in range(heads):
            out_ref[request, part] = turn(
                x_ref[:, part * HD : (part + 1) * HD], cos_ref[request], sin_ref[request]
            )
        out_ref[request, heads] = x_ref[:, heads * HD :]


def rope_heads(kept, got, cosine, sine):
    tokens, width = kept.shape
    return pl.pallas_call(
        rope_kernel,
        out_shape=jax.ShapeDtypeStruct((2, width // HD, tokens, HD), jnp.bfloat16),
        in_specs=[VMEM] * 4,
        out_specs=VMEM,
        compiler_params=pltpu.CompilerParams(vmem_limit_bytes=8 << 20),
        cost_estimate=cost(0, 2 << 20),
        name="rope_heads",
    )(kept, got, cosine, sine)


def attention_kernel(span_ref, far_ref, block_ref, token_ref, *refs, request):
    out_ref, key_ref = refs[-2:]
    heads = span_ref.shape[1] - 2
    tokens = span_ref.shape[2]
    far_len = key_ref.shape[0]
    blocks = far_ref.shape[0] // 2
    rows = GROUP * tokens
    shape = (GROUP, tokens, tokens)
    allowed = (
        lax.broadcasted_iota(jnp.int32, shape, 1) >= lax.broadcasted_iota(jnp.int32, shape, 2)
    ).reshape(rows, tokens)
    factor = math.log2(math.e) / math.sqrt(HD)
    contract = (((1,), (1,)), ((), ()))
    block_cos, block_sin = block_ref[0][:, None, :], block_ref[1][:, None, :]
    token_cos, token_sin = token_ref[0][None], token_ref[1][None]
    cosine = block_cos * token_cos - block_sin * token_sin
    sine = block_sin * token_cos + block_cos * token_sin
    key_ref[...] = turn(
        far_ref[:blocks, request].reshape(far_len, HD),
        cosine.reshape(far_len, HD),
        sine.reshape(far_len, HD),
    )

    def scores(first):
        q = span_ref[request, first : first + GROUP].reshape(rows, HD)
        far_s = lax.dot_general(q, key_ref[...], contract, preferred_element_type=jnp.float32)
        near_s = lax.dot_general(
            q, span_ref[request, heads], contract, preferred_element_type=jnp.float32
        )
        return far_s, jnp.where(allowed, near_s, -jnp.inf)

    def mix(first, far_s, near_s):
        row_max = jnp.maximum(
            jnp.max(far_s, axis=1, keepdims=True), jnp.max(near_s, axis=1, keepdims=True)
        )
        far_w = jnp.exp2((far_s - row_max) * factor)
        near_w = jnp.exp2((near_s - row_max) * factor)
        totals = jnp.sum(far_w, axis=1, keepdims=True) + jnp.sum(near_w, axis=1, keepdims=True)
        mixed = jnp.dot(
            far_w.astype(jnp.bfloat16),
            far_ref[blocks:, request].reshape(far_len, HD),
            preferred_element_type=jnp.float32,
        ) + jnp.dot(
            near_w.astype(jnp.bfloat16),
            span_ref[request, heads + 1],
            preferred_element_type=jnp.float32,
        )
        done = (mixed / totals).astype(jnp.bfloat16)
        for part in range(GROUP):
            out_ref[:, (first + part) * HD : (first + part + 1) * HD] = done[
                part * tokens : (part + 1) * tokens
            ]

    now = scores(0)
    for first in range(0, heads, GROUP):
        later = scores(first + GROUP) if first + GROUP < heads else None
        mix(first, *now)
        now = later


def attend(span, far, block_angles, token_angles, request, deps=()):
    _, parts, tokens, _ = span.shape
    heads = parts - 2
    far_len = block_angles.shape[1] * BLK
    return pl.pallas_call(
        functools.partial(attention_kernel, request=request),
        out_shape=jax.ShapeDtypeStruct((tokens, heads * HD), jnp.bfloat16),
        in_specs=[VMEM] * 4 + [HBM] * len(deps),
        out_specs=VMEM,
        scratch_shapes=[pltpu.VMEM((far_len, HD), jnp.bfloat16)],
        compiler_params=pltpu.CompilerParams(vmem_limit_bytes=FULL),
        cost_estimate=cost(
            4 * heads * tokens * (far_len + tokens) * HD,
            4 << 20,
            heads * tokens * (far_len + tokens),
        ),
        name=f"attend{request}",
    )(span, far, block_angles, token_angles, *deps)


def regroup_kernel(own_ref, other_ref, out_ref):
    for part, ref in enumerate((own_ref, other_ref)):
        out_ref[part] = jnp.swapaxes(ref[...], 0, 1)


def regroup(own, other):
    rows, blocks, cols = own.shape
    step = 256
    return pl.pallas_call(
        regroup_kernel,
        out_shape=jax.ShapeDtypeStruct((2, blocks, rows, cols), own.dtype),
        grid=(rows // step,),
        in_specs=[pl.BlockSpec((step, blocks, cols), lambda i: (i, 0, 0))] * 2,
        out_specs=pl.BlockSpec((2, blocks, step, cols), lambda i: (0, 0, i, 0)),
        compiler_params=pltpu.CompilerParams(vmem_limit_bytes=FULL),
        cost_estimate=cost(0, 32 << 20),
        name="regroup",
    )(own, other)


def project_kernel(own_ref, other_ref, w_ref, *refs, shifts, split):
    out_refs, (weight_ref, sems) = refs[:-2], refs[-2:]
    _, blocks, _, cols = w_ref.shape
    head, rep = lax.axis_index("head"), lax.axis_index("rep")
    copies = []
    for at, shift in enumerate(shifts):
        for part in range(2):
            copy = pltpu.make_async_copy(
                w_ref.at[part, lax.rem(head + shift, blocks)],
                weight_ref.at[at, part],
                sems.at[at, part],
            )
            copy.start()
            copies.append(copy)
    width = own_ref.shape[1]
    own_rows = pl.ds(pl.multiple_of(rep * width, width), width)
    other_rows = pl.ds(pl.multiple_of((1 - rep) * width, width), width)
    for at in range(len(shifts)):
        for part, place in enumerate((rep, 1 - rep)):
            copies[2 * at + part].wait()
            value = jnp.dot(
                own_ref[...], weight_ref[at, part, own_rows], preferred_element_type=jnp.float32
            ) + jnp.dot(
                other_ref[...],
                weight_ref[at, part, other_rows],
                preferred_element_type=jnp.float32,
            )
            lanes = pl.ds(pl.multiple_of(place * cols, cols), cols)
            if split:
                half = value.shape[0] // 2
                out_refs[0][:, lanes] = value[:half].astype(out_refs[0].dtype)
                out_refs[1][:, lanes] = value[half:].astype(out_refs[1].dtype)
            else:
                out_refs[at][:, lanes] = value


def project(own, other, weights, shifts, split=False):
    _, blocks, rows, cols = weights.shape
    tokens = own.shape[0]
    if split:
        shape = [jax.ShapeDtypeStruct((tokens // 2, 2 * cols), jnp.bfloat16)] * 2
    else:
        shape = [jax.ShapeDtypeStruct((tokens, 2 * cols), jnp.float32)] * len(shifts)
    return pl.pallas_call(
        functools.partial(project_kernel, shifts=shifts, split=split),
        out_shape=shape,
        in_specs=[VMEM, VMEM, HBM],
        out_specs=[VMEM] * len(shape),
        scratch_shapes=[
            pltpu.VMEM((len(shifts), 2, rows, cols), jnp.bfloat16),
            pltpu.SemaphoreType.DMA((len(shifts), 2)),
        ],
        compiler_params=pltpu.CompilerParams(vmem_limit_bytes=FULL),
        cost_estimate=cost(4 * tokens * rows * cols * len(shifts), len(shifts) * 4 << 20),
        name="project" + "".join(str(shift) for shift in shifts),
    )(own, other, weights)


def on_device(queries, span_keys, span_values, page_cache, passage_ids, starts, out_weight):
    stores = lax.axis_size("store")
    head_count = lax.axis_size("head")
    per_store, _, page_len, _ = page_cache.shape
    pass_count = passage_ids.shape[1]
    tokens = queries.shape[1]
    page_blocks = page_len // BLK

    other_ids = lax.ppermute(passage_ids, "rep", SWAP)
    held = lax.all_to_all(pack(passage_ids, other_ids, page_cache), "store", 0, 0, tiled=True)
    ids = held[:, per_store * BLK : per_store * BLK + 2, :pass_count].astype(jnp.int32)
    ids = ids.reshape(2 * stores, pass_count)

    out_weight, _ = lax.optimization_barrier((out_weight, other_ids))
    raw = out_weight[:, :, 0, :]
    weights = regroup(raw, lax.ppermute(raw, "rep", SWAP))
    kept, sent = split_heads(queries, span_keys, span_values)
    got = lax.ppermute(sent, "rep", SWAP)
    begins = jnp.concatenate([starts, lax.ppermute(starts, "rep", SWAP)])
    query_pos = (
        jnp.min(begins, axis=1, keepdims=True)
        + pass_count * page_len
        + jnp.arange(tokens, dtype=jnp.int32)
    )
    span = rope_heads(kept, got, *angle_tables(query_pos))
    block_pos = jnp.arange(page_blocks, dtype=jnp.int32)[None, :, None] * BLK + begins[:, None, :]
    block_angles = jnp.stack(angle_tables(block_pos.reshape(2, -1)), axis=1)
    token_angles = jnp.stack(angle_tables(jnp.arange(BLK, dtype=jnp.int32)))

    far = lax.all_to_all(select(ids, held, stores), "store", 0, 0, tiled=True)

    other = attend(span, far, block_angles[1], token_angles, 1, (weights,))
    other = lax.ppermute(other, "rep", SWAP)
    own = attend(span, far, block_angles[0], token_angles, 0)

    up = [(i, (i + 1) % head_count) for i in range(head_count)]
    down = [(i, (i - 1) % head_count) for i in range(head_count)]
    top, bottom = project(own, other, weights, (2,), split=True)
    top = lax.ppermute(top, "head", up).astype(jnp.float32)
    bottom = lax.ppermute(bottom, "head", down).astype(jnp.float32)
    above, below = project(own, other, weights, (1, 3))
    half = tokens // 2
    above = jnp.concatenate([above[:half] + top, above[half:]]).astype(jnp.bfloat16)
    below = jnp.concatenate([below[:half], below[half:] + bottom]).astype(jnp.bfloat16)
    above = lax.ppermute(above, "head", up).astype(jnp.float32)
    below = lax.ppermute(below, "head", down).astype(jnp.float32)
    (total,) = project(own, other, weights, (0,))
    return (total + above + below).astype(jnp.bfloat16)[None]


def solution(mesh):
    return jax.shard_map(
        on_device,
        mesh=mesh,
        in_specs=(
            P(("store", "rep"), None, "head"),
            P(("store", "rep"), None, "head"),
            P(("store", "rep"), None, "head"),
            P("store", None, None, "head"),
            P(("store", "rep"), None),
            P(("store", "rep"), None),
            P("head", None, "rep", None),
        ),
        out_specs=P(("store", "rep"), None, "head"),
        check_vma=False,
    )
```

time: 178 us -> 137 us (0.77)
  starting transfers between devices: 46.5 us -> 17.5 us
  other arithmetic: 24.3 us -> 2.99 us
  Pallas kernels: 18.2 us -> 36.6 us
  matrix products: 14.7 us -> 0 us
  blocking collectives: 28.9 us -> 40.6 us
  local copies, waits for them, and re-layouts: 11.7 us -> 2.57 us
  waiting for transfers between devices: 31.4 us -> 34.8 us
    all_to_all x5 -> x1, starting transfers between devices: 37.2 us -> 4.15 us  [on_device(): far = lax.all_to_all(select(ids, held, stores), 'store', 0, 0, tiled=True)]
    pallas_call x6 -> x10, Pallas kernels: 18.2 us -> 36.6 us  [the longest x1 14.8 us: regroup(): pl.pallas_call(regroup_kernel, out_shape=jax.ShapeDtypeStruct((2, blocks,...]
    dot_general x2 -> x0, matrix products: 14.7 us -> none  [on_device(): jnp.einsum('tk,hkn->htn', att, weight, preferred_element_type=jnp.float32)]
    all_to_all x1, blocking collectives: 28.9 us -> 40.6 us  [on_device(): lax.all_to_all(pack(passage_ids, other_ids, page_cache), 'store', 0, 0, t...]
    neg x2 -> x0, other arithmetic: 10.5 us -> none  [angle_tables(): -sine]
    concatenate x8 -> x3, other arithmetic: 9.4 us -> 0.16 us  [the longest x1 0.12 us: on_device(): begins = jnp.concatenate([starts, lax.ppermute(starts, 'rep', SWAP)])]
    ppermute x5 -> x9, waiting for transfers between devices: 0.94 us -> 5.88 us  [the longest x1 3.13 us: on_device(): bottom = lax.ppermute(bottom, 'head', down).astype(jnp.float32)]
    ppermute x5 -> x9, starting transfers between devices: 9.31 us -> 13.3 us  [the longest x1 3.24 us: on_device(): other_ids = lax.ppermute(passage_ids, 'rep', SWAP)]
  transfers between devices with their start and end apart: 10 -> 10, of which waited for: 5 -> 4; matrix products, arithmetic and copies ran while one was open for 24% -> 2% of each run, Pallas kernels for 9% -> 22%
where the time goes in v2:
time: 137 us; the launch traced here: 135 us
  blocking collectives  40.6 us (30%)
  Pallas kernels  36.6 us (27%)
  waiting for transfers between devices  34.8 us (25%)
  starting transfers between devices  17.5 us (13%)
  other arithmetic  2.99 us (2%)
  local copies, waits for them, and re-layouts  2.57 us (2%)
    all_to_all x1, blocking collectives, on_device(): lax.all_to_all(pack(passage_ids, other_ids, page_cache), 'store', 0, 0, t...  40.6 us
    all_to_all x1, waiting for transfers between devices, on_device(): far = lax.all_to_all(select(ids, held, stores), 'store', 0, 0, tiled=True)  28.9 us
    pallas_call x1, Pallas kernels, regroup(): pl.pallas_call(regroup_kernel, out_shape=jax.ShapeDtypeStruct((2, blocks,...  14.8 us
    pallas_call x3, Pallas kernels, project(): pl.pallas_call(functools.partial(project_kernel, shifts=shifts, split=spl...  9.34 us
    pallas_call x2, Pallas kernels, attend(): pl.pallas_call(functools.partial(attention_kernel, request=request), out_...  7.14 us
    all_to_all x1, starting transfers between devices, on_device(): far = lax.all_to_all(select(ids, held, stores), 'store', 0, 0, tiled=True)  4.15 us
    ppermute x1, starting transfers between devices, on_device(): other_ids = lax.ppermute(passage_ids, 'rep', SWAP)  3.24 us
    pallas_call x1, Pallas kernels, select(): pl.pallas_call(select_kernel, out_shape=jax.ShapeDtypeStruct(shape, jnp.b...  3.23 us
  transfers between devices with their start and end apart: 10, of which 4 were waited for; matrix products, arithmetic and copies ran while one was open for 2% of the time, Pallas kernels for 22%

profile of v2, /device:TPU:1, one launch (start us, length us, event | category | flops | bytes accessed | tf_op | source)
XLA Modules:
  0.0 135.3 jit_solution(8620770842587529861)
XLA Ops:
  0.0 3.2 %collective-permute-start.2 = (s32[1,8]{1,0:T(1,128)}, s32[1,8]{1,0:T(1,128)S(1)}, u32[]{:S(2)}, u32[]{:S(2)}) collective-permute-start(s32[1,8]{1,0:T(1,128)} %own_ref.1), channel_id=1, source_target_pairs={{0,1},{1,0},{2,3},{3,2},{4,5},{5,4},{6,7},{7,6},{8,9},{9,8},{10,11... | collective-permute-start | bytes 104 | tf_op jit(solution)/shard_map/ppermute | solution.py:365
  3.2 1.0 collective-permute-done.2.other_ref
  4.2 0.3 collective-permute-start.3
  4.5 1.6 %copy-done = bf16[8,2,256,256]{3,2,1,0:T(8,128)(2,1)S(1)} copy-done((bf16[8,2,256,256]{3,2,1,0:T(8,128)(2,1)S(1)}, bf16[8,2,256,256]{3,2,1,0:T(8,128)(2,1)}, u32[]{:S(2)}) %copy-start) | copy-done | bytes 2097176
  6.1 0.7 copy-done.5
  6.7 1.0 pack.1
  7.8 40.6 %all_to_all.10.held_ref = bf16[32,136,128]{2,1,0:T(8,128)(2,1)S(1)} all-to-all(bf16[32,136,128]{2,1,0:T(8,128)(2,1)S(1)} %pack.1), channel_id=1, replica_groups=mesh['store'=32,'head'=4,'rep'=2] {'store'}, dimensions={0} | all-to-all | bytes 2228224 | tf_op jit(solution)/shard_map/all_to_all | solution.py:366
  48.4 3.2 %select.5 = bf16[32,2,8,16,128]{4,3,2,1,0:T(8,128)(2,1)} custom-call(s32[64,8]{1,0:T(8,128)S(1)} %convert.19.ids_ref, bf16[32,136,128]{2,1,0:T(8,128)(2,1)S(1)} %all_to_all.10.held_ref), custom_call_target="tpu_custom_call" | custom-call | bytes 2097152 | tf_op jit(solution)/shard_map/select/pallas_call | solution.py:136
  51.7 4.2 %all-to-all-start.1 = ((bf16[32,2,8,16,128]{4,3,2,1,0:T(8,128)(2,1)}), bf16[32,2,8,16,128]{4,3,2,1,0:T(8,128)(2,1)S(1)}, u32[]{:S(2)}, u32[]{:S(2)}) async-start(bf16[32,2,8,16,128]{4,3,2,1,0:T(8,128)(2,1)} %select.5), calls=%async_computation.1 | async-start | bytes 4194304 | tf_op jit(solution)/shard_map/all_to_all | solution.py:386
  55.9 1.4 %collective-permute-start.1 = (s32[1,8]{1,0:T(1,128)S(1)}, s32[1,8]{1,0:T(1,128)S(1)}, u32[]{:S(2)}, u32[]{:S(2)}) collective-permute-start(s32[1,8]{1,0:T(1,128)S(1)} %copy-done.6), channel_id=1, source_target_pairs={{0,1},{1,0},{2,3},{3,2},{4,5},{5,4},{6,7},{7,6},{8,9},{9,8},{10,11... | collective-permute-start | bytes 104 | tf_op jit(solution)/shard_map/ppermute | solution.py:375
  57.3 0.8 split_heads.1
  58.2 0.1 add.91
  58.3 0.1 multiply_cosine_fusion.2
  58.5 0.1 pad_add_fusion
  58.8 0.5 fusion.2
  59.3 0.7 fusion.5
  60.0 0.5 fusion.1
  60.5 0.3 rope_heads.1.span_ref
  60.8 14.8 %regroup.1.refs_0_.w_ref = bf16[2,4,2048,512]{3,2,1,0:T(8,128)(2,1)} custom-call(bf16[2048,4,512]{2,1,0:T(4,128)(2,1)} %bitcast.10, bf16[2048,4,512]{2,1,0:T(4,128)(2,1)} %collective-permute-done.3.other_ref), custom_call_target="tpu_custom_call" | custom-call | bytes 33554432 | tf_op jit(solution)/shard_map/regroup/pallas_call | solution.py:287
  75.6 28.9 %all-to-all-done.1.far_ref = bf16[32,2,8,16,128]{4,3,2,1,0:T(8,128)(2,1)S(1)} async-done(((bf16[32,2,8,16,128]{4,3,2,1,0:T(8,128)(2,1)}), bf16[32,2,8,16,128]{4,3,2,1,0:T(8,128)(2,1)S(1)}, u32[]{:S(2)}, u32[]{:S(2)}) %all-to-all-start.1) | async-done | bytes 2097184 | tf_op jit(solution)/shard_map/all_to_all | solution.py:386
  104.5 3.6 %attend1.1 = bf16[128,1024]{1,0:T(8,128)(2,1)S(1)} custom-call(bf16[2,10,128,128]{3,2,1,0:T(8,128)(2,1)S(1)} %rope_heads.1.span_ref, bf16[32,2,8,16,128]{4,3,2,1,0:T(8,128)(2,1)S(1)} %all-to-all-done.1.far_ref, f32[2,128,128]{2,1,0:T(8,128)S(1)} %get-tuple-element.19.block_ref, f32[2,16,128]{2,1,0:T(8,128)S(1)} %pad_maximum_fusion.3.token_ref, ...), custom_call_target="tpu_custom_call" | custom-call | flops 1140850688 | bytes 4194304 | tf_op jit(solution)/shard_map/attend1/pallas_call | solution.py:263
  108.0 2.7 %collective-permute-start.4 = (bf16[128,1024]{1,0:T(8,128)(2,1)S(1)}, bf16[128,1024]{1,0:T(8,128)(2,1)S(1)}, u32[]{:S(2)}, u32[]{:S(2)}) collective-permute-start(bf16[128,1024]{1,0:T(8,128)(2,1)S(1)} %attend1.1), channel_id=1, source_target_pairs={{0,1},{1,0},{2,3},{3,2},{4,5},{5,4},{6,7},{7,6},{8,9},{9,8},{10,11... | collective-permute-start | bytes 786440 | tf_op jit(solution)/shard_map/ppermute | solution.py:389
  110.7 3.6 %attend0.1.own_ref = bf16[128,1024]{1,0:T(8,128)(2,1)S(1)} custom-call(bf16[2,10,128,128]{3,2,1,0:T(8,128)(2,1)S(1)} %rope_heads.1.span_ref, bf16[32,2,8,16,128]{4,3,2,1,0:T(8,128)(2,1)S(1)} %all-to-all-done.1.far_ref, f32[2,128,128]{2,1,0:T(8,128)S(1)} %copy-done.2, f32[2,16,128]{2,1,0:T(8,128)S(1)} %pad_maximum_fusion.3.token_ref), custom_call_target="tpu_custom_call" | custom-call | flops 1140850688 | bytes 4194304 | tf_op jit(solution)/shard_map/attend0/pallas_call | solution.py:263
  114.3 2.7 %project2.1 = (bf16[64,1024]{1,0:T(8,128)(2,1)S(1)}, bf16[64,1024]{1,0:T(8,128)(2,1)S(1)}) custom-call(bf16[128,1024]{1,0:T(8,128)(2,1)S(1)} %attend0.1.own_ref, bf16[128,1024]{1,0:T(8,128)(2,1)S(1)} %collective-permute-done.4.other_ref, bf16[2,4,2048,512]{3,2,1,0:T(8,128)(2,1)} %regroup.1.refs_0_.w_ref), custom_call_target="tpu_custom_call" | custom-call | flops 536870912 | bytes 4194304 | tf_op jit(solution)/shard_map/project2/pallas_call | solution.py:342
  117.0 1.3 collective-permute-start.5
  118.3 4.0 %project13.1 = (f32[128,1024]{1,0:T(8,128)S(1)}, f32[128,1024]{1,0:T(8,128)S(1)}) custom-call(bf16[128,1024]{1,0:T(8,128)(2,1)S(1)} %attend0.1.own_ref, bf16[128,1024]{1,0:T(8,128)(2,1)S(1)} %collective-permute-done.4.other_ref, bf16[2,4,2048,512]{3,2,1,0:T(8,128)(2,1)} %regroup.1.refs_0_.w_ref), custom_call_target="tpu_custom_call" | custom-call | flops 1073741824 | bytes 8388608 | tf_op jit(solution)/shard_map/project13/pallas_call | solution.py:342
  122.3 1.5 %collective-permute-start.7 = (bf16[64,1024]{1,0:T(8,128)(2,1)S(1)}, bf16[64,1024]{1,0:T(8,128)(2,1)S(1)}, u32[]{:S(2)}, u32[]{:S(2)}) collective-permute-start(bf16[64,1024]{1,0:T(8,128)(2,1)S(1)} %get-tuple-element.18), channel_id=1, source_target_pairs={{0,6},{2,0},{4,2},{6,4},{1,7},{3,1},{5,3},{7,5},{8,14},{10,8},{12,... | collective-permute-start | bytes 393224 | tf_op jit(solution)/shard_map/ppermute | solution.py:396
  124.0 3.1 %collective-permute-done.7 = bf16[64,1024]{1,0:T(8,128)(2,1)S(1)} collective-permute-done((bf16[64,1024]{1,0:T(8,128)(2,1)S(1)}, bf16[64,1024]{1,0:T(8,128)(2,1)S(1)}, u32[]{:S(2)}, u32[]{:S(2)}) %collective-permute-start.7) | collective-permute-done | bytes 131104 | tf_op jit(solution)/shard_map/ppermute | solution.py:396
  127.2 2.8 %collective-permute-start.8 = (bf16[128,1024]{1,0:T(8,128)(2,1)S(1)}, bf16[128,1024]{1,0:T(8,128)(2,1)S(1)}, u32[]{:S(2)}, u32[]{:S(2)}) collective-permute-start(bf16[128,1024]{1,0:T(8,128)(2,1)S(1)} %pad_maximum_fusion.1), channel_id=1, source_target_pairs={{0,6},{2,0},{4,2},{6,4},{1,7},{3,1},{5,3},{7,5},{8,14},{10,8},{12,... | collective-permute-start | bytes 786440 | tf_op jit(solution)/shard_map/ppermute | solution.py:402
  130.0 2.7 %project0.1 = f32[128,1024]{1,0:T(8,128)S(1)} custom-call(bf16[128,1024]{1,0:T(8,128)(2,1)S(1)} %attend0.1.own_ref, bf16[128,1024]{1,0:T(8,128)(2,1)S(1)} %collective-permute-done.4.other_ref, bf16[2,4,2048,512]{3,2,1,0:T(8,128)(2,1)} %regroup.1.refs_0_.w_ref), custom_call_target="tpu_custom_call" | custom-call | flops 536870912 | bytes 4194304 | tf_op jit(solution)/shard_map/project0/pallas_call | solution.py:342
  132.7 1.8 %collective-permute-done.8 = bf16[128,1024]{1,0:T(8,128)(2,1)S(1)} collective-permute-done((bf16[128,1024]{1,0:T(8,128)(2,1)S(1)}, bf16[128,1024]{1,0:T(8,128)(2,1)S(1)}, u32[]{:S(2)}, u32[]{:S(2)}) %collective-permute-start.8) | collective-permute-done | bytes 262176 | tf_op jit(solution)/shard_map/ppermute | solution.py:402
  134.5 0.8 fusion
  (38 shorter events, 0.6 us)
Async XLA Ops:
  0.0 4.2 %collective-permute-start.2 = (s32[1,8]{1,0:T(1,128)}, s32[1,8]{1,0:T(1,128)S(1)}, u32[]{:S(2)}, u32[]{:S(2)}) collective-permute-start(s32[1,8]{1,0:T(1,128)} %own_ref.1), channel_id=1, source_target_pairs={{0,1},{1,0},{2,3},{3,2},{4,5},{5,4},{6,7},{7,6},{8,9},{9,8},{10,11... | collective-permute-start | bytes 104 | tf_op jit(solution)/shard_map/ppermute | solution.py:365
  4.2 56.6 %collective-permute-start.3 = (bf16[2048,4,512]{2,1,0:T(4,128)(2,1)}, bf16[2048,4,512]{2,1,0:T(4,128)(2,1)}, u32[]{:S(2)}, u32[]{:S(2)}) collective-permute-start(bf16[2048,4,512]{2,1,0:T(4,128)(2,1)} %bitcast.9), channel_id=1, source_target_pairs={{0,1},{1,0},{2,3},{3,2},{4,5},{5,4},{6,7},{7,6},{8,9},{9,8},{10,11... | collective-permute-start | bytes 25165832 | tf_op jit(solution)/shard_map/ppermute | solution.py:372
  4.5 1.6 %copy-start = (bf16[8,2,256,256]{3,2,1,0:T(8,128)(2,1)S(1)}, bf16[8,2,256,256]{3,2,1,0:T(8,128)(2,1)}, u32[]{:S(2)}) copy-start(bf16[8,2,256,256]{3,2,1,0:T(8,128)(2,1)} %cache_ref.1) | copy-start | bytes 6291460
  6.1 0.7 copy-start.5
  51.7 4.2 %copy-start.6 = (s32[1,8]{1,0:T(1,128)S(1)}, s32[1,8]{1,0:T(1,128)}, u32[]{:S(2)}) copy-start(s32[1,8]{1,0:T(1,128)} %param.12) | copy-start | bytes 100
  51.7 5.6 %copy-start.1 = (bf16[1,128,2048]{2,1,0:T(8,128)(2,1)S(1)}, bf16[1,128,2048]{2,1,0:T(8,128)(2,1)}, u32[]{:S(2)}) copy-start(bf16[1,128,2048]{2,1,0:T(8,128)(2,1)} %q_ref.1) | copy-start | bytes 1572868
  51.7 5.6 %copy-start.3 = (bf16[1,128,256]{2,1,0:T(8,128)(2,1)S(1)}, bf16[1,128,256]{2,1,0:T(8,128)(2,1)}, u32[]{:S(2)}) copy-start(bf16[1,128,256]{2,1,0:T(8,128)(2,1)} %k_ref.1) | copy-start | bytes 196612
  51.7 5.6 %copy-start.4 = (bf16[1,128,256]{2,1,0:T(8,128)(2,1)S(1)}, bf16[1,128,256]{2,1,0:T(8,128)(2,1)}, u32[]{:S(2)}) copy-start(bf16[1,128,256]{2,1,0:T(8,128)(2,1)} %v_ref.1) | copy-start | bytes 196612
  51.7 52.8 %all-to-all-start.1 = ((bf16[32,2,8,16,128]{4,3,2,1,0:T(8,128)(2,1)}), bf16[32,2,8,16,128]{4,3,2,1,0:T(8,128)(2,1)S(1)}, u32[]{:S(2)}, u32[]{:S(2)}) async-start(bf16[32,2,8,16,128]{4,3,2,1,0:T(8,128)(2,1)} %select.5), calls=%async_computation.1 | async-start | bytes 4194304 | tf_op jit(solution)/shard_map/all_to_all | solution.py:386
  55.9 2.6 %collective-permute-start.1 = (s32[1,8]{1,0:T(1,128)S(1)}, s32[1,8]{1,0:T(1,128)S(1)}, u32[]{:S(2)}, u32[]{:S(2)}) collective-permute-start(s32[1,8]{1,0:T(1,128)S(1)} %copy-done.6), channel_id=1, source_target_pairs={{0,1},{1,0},{2,3},{3,2},{4,5},{5,4},{6,7},{7,6},{8,9},{9,8},{10,11... | collective-permute-start | bytes 104 | tf_op jit(solution)/shard_map/ppermute | solution.py:375
  58.1 2.4 %collective-permute-start = (bf16[128,1280]{1,0:T(8,128)(2,1)}, bf16[128,1280]{1,0:T(8,128)(2,1)S(1)}, u32[]{:S(2)}, u32[]{:S(2)}) collective-permute-start(bf16[128,1280]{1,0:T(8,128)(2,1)} %get-tuple-element.13), channel_id=1, source_target_pairs={{0,1},{1,0},{2,3},{3,2},{4,5},{5,4},{6,7},{7,6},{8,9},{9,8},{10,11... | collective-permute-start | bytes 983048 | tf_op jit(solution)/shard_map/ppermute | solution.py:374
  104.5 6.2 %copy-start.2 = (f32[2,128,128]{2,1,0:T(8,128)S(1)}, f32[2,128,128]{2,1,0:T(8,128)}, u32[]{:S(2)}) copy-start(f32[2,128,128]{2,1,0:T(8,128)} %get-tuple-element.20.block_ref) | copy-start | bytes 393220
  108.0 6.2 %collective-permute-start.4 = (bf16[128,1024]{1,0:T(8,128)(2,1)S(1)}, bf16[128,1024]{1,0:T(8,128)(2,1)S(1)}, u32[]{:S(2)}, u32[]{:S(2)}) collective-permute-start(bf16[128,1024]{1,0:T(8,128)(2,1)S(1)} %attend1.1), channel_id=1, source_target_pairs={{0,1},{1,0},{2,3},{3,2},{4,5},{5,4},{6,7},{7,6},{8,9},{9,8},{10,11... | collective-permute-start | bytes 786440 | tf_op jit(solution)/shard_map/ppermute | solution.py:389
  117.0 6.8 %collective-permute-start.5 = (bf16[64,1024]{1,0:T(8,128)(2,1)S(1)}, bf16[64,1024]{1,0:T(8,128)(2,1)S(1)}, u32[]{:S(2)}, u32[]{:S(2)}) collective-permute-start(bf16[64,1024]{1,0:T(8,128)(2,1)S(1)} %get-tuple-element.16), channel_id=1, source_target_pairs={{0,2},{2,4},{4,6},{6,0},{1,3},{3,5},{5,7},{7,1},{8,10},{10,12},{12... | collective-permute-start | bytes 393224 | tf_op jit(solution)/shard_map/ppermute | solution.py:395
  122.3 4.9 %collective-permute-start.7 = (bf16[64,1024]{1,0:T(8,128)(2,1)S(1)}, bf16[64,1024]{1,0:T(8,128)(2,1)S(1)}, u32[]{:S(2)}, u32[]{:S(2)}) collective-permute-start(bf16[64,1024]{1,0:T(8,128)(2,1)S(1)} %get-tuple-element.18), channel_id=1, source_target_pairs={{0,6},{2,0},{4,2},{6,4},{1,7},{3,1},{5,3},{7,5},{8,14},{10,8},{12,... | collective-permute-start | bytes 393224 | tf_op jit(solution)/shard_map/ppermute | solution.py:396
  123.9 8.8 %collective-permute-start.6 = (bf16[128,1024]{1,0:T(8,128)(2,1)S(1)}, bf16[128,1024]{1,0:T(8,128)(2,1)S(1)}, u32[]{:S(2)}, u32[]{:S(2)}) collective-permute-start(bf16[128,1024]{1,0:T(8,128)(2,1)S(1)} %pad_maximum_fusion), channel_id=1, source_target_pairs={{0,2},{2,4},{4,6},{6,0},{1,3},{3,5},{5,7},{7,1},{8,10},{10,12},{12... | collective-permute-start | bytes 786440 | tf_op jit(solution)/shard_map/ppermute | solution.py:401
  127.2 7.2 %collective-permute-start.8 = (bf16[128,1024]{1,0:T(8,128)(2,1)S(1)}, bf16[128,1024]{1,0:T(8,128)(2,1)S(1)}, u32[]{:S(2)}, u32[]{:S(2)}) collective-permute-start(bf16[128,1024]{1,0:T(8,128)(2,1)S(1)} %pad_maximum_fusion.1), channel_id=1, source_target_pairs={{0,6},{2,0},{4,2},{6,4},{1,7},{3,1},{5,3},{7,5},{8,14},{10,8},{12,... | collective-permute-start | bytes 786440 | tf_op jit(solution)/shard_map/ppermute | solution.py:402

commit v3 on v2

--- a/solution.py
+++ b/solution.py
@@ -11,7 +11,7 @@
 HD = 128
 BLK = 16
 IDS = 8
-FULL = 50 << 20
+FULL = 24 << 20
 GROUP = 2
 THETA = 1000000.0
 SWAP = [(0, 1), (1, 0)]
@@ -19,6 +19,10 @@
 SMEM = pl.BlockSpec(memory_space=pltpu.SMEM)
 VMEM = pl.BlockSpec(memory_space=pltpu.VMEM)
 HBM = pl.BlockSpec(memory_space=pltpu.HBM)
+
+
+def in_hbm(x):
+    return pltpu.with_memory_space_constraint(x, pltpu.HBM)
 
 
 def cost(flops, moved, trans=0):
@@ -56,8 +60,8 @@
     lane = lax.broadcasted_iota(jnp.int32, (IDS, HD), 1)
     named = jnp.zeros((IDS, HD), jnp.int32)
     for slot in range(own_ref.shape[1]):
-        named = jnp.where((row == rep) & (lane == slot), own_ref[0, slot], named)
-        named = jnp.where((row == 1 - rep) & (lane == slot), other_ref[0, slot], named)
+        named = jnp.where((row == rep) & (lane == slot), own_ref[:, slot : slot + 1], named)
+        named = jnp.where((row == 1 - rep) & (lane == slot), other_ref[:, slot : slot + 1], named)
     named = named.astype(jnp.float32).astype(jnp.bfloat16)
     outs = []
     for kind in range(kinds):
@@ -82,8 +86,8 @@
     shape = (kinds * page_len // BLK, passages * BLK + IDS, HD)
     return pl.pallas_call(
         pack_kernel,
-        out_shape=jax.ShapeDtypeStruct(shape, jnp.bfloat16),
-        in_specs=[SMEM, SMEM, HBM],
+        out_shape=pltpu.HBM(shape, jnp.bfloat16),
+        in_specs=[VMEM, VMEM, HBM],
         out_specs=HBM,
         scratch_shapes=[
             pltpu.VMEM((kinds, passages, page_len, HD), jnp.bfloat16),
@@ -94,7 +98,7 @@
         compiler_params=pltpu.CompilerParams(vmem_limit_bytes=FULL),
         cost_estimate=cost(0, 2 << 20),
         name="pack",
-    )(own_ids, other_ids, page_cache)
+    )(own_ids, other_ids, in_hbm(page_cache))
 
 
 def select_kernel(ids_ref, held_ref, out_ref, chosen_ref, sems):
@@ -105,10 +109,13 @@
     rep = lax.axis_index("rep")
     chunks = sems.shape[0]
     per = stores // chunks
-    copies = []
-    for chunk in range(chunks):
-
-        def step(at, carry):
+
+    def copy_out(chunk):
+        part = pl.ds(chunk * per, per)
+        return pltpu.make_async_copy(chosen_ref.at[part], out_ref.at[part], sems.at[chunk])
+
+    def fill(chunk, carry):
+        for at in range(per):
             dest = chunk * per + at
             for request in range(requests):
                 row = dest * requests + (rep ^ request)
@@ -118,15 +125,12 @@
                     chosen_ref[dest, request, slot] = held_ref[
                         lax.shift_right_logical(wanted, shift), pl.ds(start, BLK)
                     ]
-            return carry
-
-        lax.fori_loop(0, per, step, 0, unroll=True)
-        part = pl.ds(chunk * per, per)
-        copy = pltpu.make_async_copy(chosen_ref.at[part], out_ref.at[part], sems.at[chunk])
-        copy.start()
-        copies.append(copy)
-    for copy in copies:
-        copy.wait()
+        copy_out(chunk).start()
+        return carry
+
+    lax.fori_loop(0, chunks, fill, 0)
+    for chunk in range(chunks):
+        copy_out(chunk).wait()
 
 
 def select(ids, held, stores):
@@ -135,7 +139,7 @@
     shape = (stores, requests, slots, BLK, HD)
     return pl.pallas_call(
         select_kernel,
-        out_shape=jax.ShapeDtypeStruct(shape, jnp.bfloat16),
+        out_shape=pltpu.HBM(shape, jnp.bfloat16),
         in_specs=[SMEM, VMEM],
         out_specs=HBM,
         scratch_shapes=[pltpu.VMEM(shape, jnp.bfloat16), pltpu.SemaphoreType.DMA((8,))],
@@ -196,8 +200,7 @@
     )(kept, got, cosine, sine)
 
 
-def attention_kernel(span_ref, far_ref, block_ref, token_ref, *refs, request):
-    out_ref, key_ref = refs[-2:]
+def attention(span_ref, far_ref, block_ref, token_ref, out_ref, key_ref, request):
     heads = span_ref.shape[1] - 2
     tokens = span_ref.shape[2]
     far_len = key_ref.shape[0]
@@ -256,24 +259,60 @@
         now = later
 
 
-def attend(span, far, block_angles, token_angles, request, deps=()):
+def fetch_weights(w_ref, out_refs, sems, shifts):
+    blocks = w_ref.shape[1]
+    rep, head = lax.axis_index("rep"), lax.axis_index("head")
+    copies = []
+    for at, (out_ref, shift) in enumerate(zip(out_refs, shifts)):
+        width = out_ref.shape[2]
+        block = lax.rem(head + jnp.where(rep == 0, shift[0], shift[1]), blocks)
+        for part in range(2):
+            for side, half in enumerate((rep, 1 - rep)):
+                copy = pltpu.make_async_copy(
+                    w_ref.at[part, block, pl.ds(pl.multiple_of(half * width, width), width)],
+                    out_ref.at[part, side],
+                    sems.at[at, part, side],
+                )
+                copy.start()
+                copies.append(copy)
+    return copies
+
+
+def attention_kernel(span_ref, far_ref, block_ref, token_ref, w_ref, *refs, request, shifts):
+    out_ref, *weight_refs, key_ref, sems = refs
+    copies = fetch_weights(w_ref, weight_refs, sems, shifts)
+
+    @pl.when(lax.axis_index("rep") >= 0)
+    def _():
+        attention(span_ref, far_ref, block_ref, token_ref, out_ref, key_ref, request)
+
+    for copy in copies:
+        copy.wait()
+
+
+def attend(span, far, block_angles, token_angles, weights, request, shifts):
     _, parts, tokens, _ = span.shape
     heads = parts - 2
     far_len = block_angles.shape[1] * BLK
-    return pl.pallas_call(
-        functools.partial(attention_kernel, request=request),
-        out_shape=jax.ShapeDtypeStruct((tokens, heads * HD), jnp.bfloat16),
-        in_specs=[VMEM] * 4 + [HBM] * len(deps),
-        out_specs=VMEM,
-        scratch_shapes=[pltpu.VMEM((far_len, HD), jnp.bfloat16)],
+    _, _, rows, cols = weights.shape
+    return pl.pallas_call(
+        functools.partial(attention_kernel, request=request, shifts=shifts),
+        out_shape=[jax.ShapeDtypeStruct((tokens, heads * HD), jnp.bfloat16)]
+        + [pltpu.VMEM((2, 2, rows // 2, cols), weights.dtype)] * len(shifts),
+        in_specs=[VMEM] * 4 + [HBM],
+        out_specs=[VMEM] * (1 + len(shifts)),
+        scratch_shapes=[
+            pltpu.VMEM((far_len, HD), jnp.bfloat16),
+            pltpu.SemaphoreType.DMA((len(shifts), 2, 2)),
+        ],
         compiler_params=pltpu.CompilerParams(vmem_limit_bytes=FULL),
         cost_estimate=cost(
             4 * heads * tokens * (far_len + tokens) * HD,
-            4 << 20,
+            12 << 20,
             heads * tokens * (far_len + tokens),
         ),
         name=f"attend{request}",
-    )(span, far, block_angles, token_angles, *deps)
+    )(span, far, block_angles, token_angles, in_hbm(weights))
 
 
 def regroup_kernel(own_ref, other_ref, out_ref):
@@ -296,62 +335,32 @@
     )(own, other)
 
 
-def project_kernel(own_ref, other_ref, w_ref, *refs, shifts, split):
-    out_refs, (weight_ref, sems) = refs[:-2], refs[-2:]
-    _, blocks, _, cols = w_ref.shape
-    head, rep = lax.axis_index("head"), lax.axis_index("rep")
-    copies = []
-    for at, shift in enumerate(shifts):
-        for part in range(2):
-            copy = pltpu.make_async_copy(
-                w_ref.at[part, lax.rem(head + shift, blocks)],
-                weight_ref.at[at, part],
-                sems.at[at, part],
-            )
-            copy.start()
-            copies.append(copy)
-    width = own_ref.shape[1]
-    own_rows = pl.ds(pl.multiple_of(rep * width, width), width)
-    other_rows = pl.ds(pl.multiple_of((1 - rep) * width, width), width)
-    for at in range(len(shifts)):
-        for part, place in enumerate((rep, 1 - rep)):
-            copies[2 * at + part].wait()
-            value = jnp.dot(
-                own_ref[...], weight_ref[at, part, own_rows], preferred_element_type=jnp.float32
-            ) + jnp.dot(
-                other_ref[...],
-                weight_ref[at, part, other_rows],
-                preferred_element_type=jnp.float32,
-            )
-            lanes = pl.ds(pl.multiple_of(place * cols, cols), cols)
-            if split:
-                half = value.shape[0] // 2
-                out_refs[0][:, lanes] = value[:half].astype(out_refs[0].dtype)
-                out_refs[1][:, lanes] = value[half:].astype(out_refs[1].dtype)
-            else:
-                out_refs[at][:, lanes] = value
-
-
-def project(own, other, weights, shifts, split=False):
-    _, blocks, rows, cols = weights.shape
+def project_kernel(own_ref, other_ref, weight_ref, *refs):
+    *more_refs, out_ref = refs
+    rep = lax.axis_index("rep")
+    cols = weight_ref.shape[3]
+    for part, place in enumerate((rep, 1 - rep)):
+        lanes = pl.ds(pl.multiple_of(place * cols, cols), cols)
+        value = jnp.dot(
+            own_ref[...], weight_ref[part, 0], preferred_element_type=jnp.float32
+        ) + jnp.dot(other_ref[...], weight_ref[part, 1], preferred_element_type=jnp.float32)
+        for more_ref in more_refs:
+            value = value + more_ref[:, lanes].astype(jnp.float32)
+        out_ref[:, lanes] = value.astype(out_ref.dtype)
+
+
+def project(own, other, weight, dtype, name, *more):
+    _, _, rows, cols = weight.shape
     tokens = own.shape[0]
-    if split:
-        shape = [jax.ShapeDtypeStruct((tokens // 2, 2 * cols), jnp.bfloat16)] * 2
-    else:
-        shape = [jax.ShapeDtypeStruct((tokens, 2 * cols), jnp.float32)] * len(shifts)
-    return pl.pallas_call(
-        functools.partial(project_kernel, shifts=shifts, split=split),
-        out_shape=shape,
-        in_specs=[VMEM, VMEM, HBM],
-        out_specs=[VMEM] * len(shape),
-        scratch_shapes=[
-            pltpu.VMEM((len(shifts), 2, rows, cols), jnp.bfloat16),
-            pltpu.SemaphoreType.DMA((len(shifts), 2)),
-        ],
+    return pl.pallas_call(
+        project_kernel,
+        out_shape=jax.ShapeDtypeStruct((tokens, 2 * cols), dtype),
+        in_specs=[VMEM] * (3 + len(more)),
+        out_specs=VMEM,
         compiler_params=pltpu.CompilerParams(vmem_limit_bytes=FULL),
-        cost_estimate=cost(4 * tokens * rows * cols * len(shifts), len(shifts) * 4 << 20),
-        name="project" + "".join(str(shift) for shift in shifts),
-    )(own, other, weights)
+        cost_estimate=cost(8 * tokens * rows * cols, 4 << 20),
+        name=name,
+    )(own, other, weight, *more)
 
 
 def on_device(queries, span_keys, span_values, page_cache, passage_ids, starts, out_weight):
@@ -385,23 +394,29 @@
 
     far = lax.all_to_all(select(ids, held, stores), "store", 0, 0, tiled=True)
 
-    other = attend(span, far, block_angles[1], token_angles, 1, (weights,))
+    other, opposite_w, plain_w = attend(
+        span, far, block_angles[1], token_angles, weights, 1, ((2, 2), (3, 1))
+    )
     other = lax.ppermute(other, "rep", SWAP)
-    own = attend(span, far, block_angles[0], token_angles, 0)
-
-    up = [(i, (i + 1) % head_count) for i in range(head_count)]
-    down = [(i, (i - 1) % head_count) for i in range(head_count)]
-    top, bottom = project(own, other, weights, (2,), split=True)
-    top = lax.ppermute(top, "head", up).astype(jnp.float32)
-    bottom = lax.ppermute(bottom, "head", down).astype(jnp.float32)
-    above, below = project(own, other, weights, (1, 3))
-    half = tokens // 2
-    above = jnp.concatenate([above[:half] + top, above[half:]]).astype(jnp.bfloat16)
-    below = jnp.concatenate([below[:half], below[half:] + bottom]).astype(jnp.bfloat16)
-    above = lax.ppermute(above, "head", up).astype(jnp.float32)
-    below = lax.ppermute(below, "head", down).astype(jnp.float32)
-    (total,) = project(own, other, weights, (0,))
-    return (total + above + below).astype(jnp.bfloat16)[None]
+    own, relayed_w, own_w = attend(
+        span, far, block_angles[0], token_angles, weights, 0, ((1, 3), (0, 0))
+    )
+
+    ahead, behind = [], []
+    for i in range(head_count):
+        after, before = (i + 1) % head_count, (i - 1) % head_count
+        ahead += [(2 * i, 2 * after), (2 * i + 1, 2 * before + 1)]
+        behind += [(2 * i, 2 * before), (2 * i + 1, 2 * after + 1)]
+    axes = ("head", "rep")
+    opposite = project(own, other, opposite_w, jnp.bfloat16, "opposite")
+    passing = lax.ppermute(opposite, axes, ahead)
+    plain = project(own, other, plain_w, jnp.bfloat16, "plain")
+    plain = lax.ppermute(plain, axes, behind)
+    relayed = project(own, other, relayed_w, jnp.bfloat16, "relayed", passing)
+    relayed = lax.ppermute(relayed, axes, ahead)
+    total = project(own, other, own_w, jnp.float32, "kept")
+    total = total + plain.astype(jnp.float32) + relayed.astype(jnp.float32)
+    return total.astype(jnp.bfloat16)[None]
 
 
 def solution(mesh):

time: 137 us -> 131 us (0.956)
  Pallas kernels: 36.6 us -> 28.4 us
  local copies, waits for them, and re-layouts: 2.57 us -> 6.01 us
    pallas_call x7 -> x8, Pallas kernels: 20.7 us -> 15.6 us  [the longest x2 7.33 us: attend(): pl.pallas_call(functools.partial(attention_kernel, request=request, shift...]
    unnamed x14 -> x16, local copies, waits for them, and re-layouts: 2.27 us -> 5.75 us
    pallas_call x1, Pallas kernels: 14.8 us -> 11.7 us  [regroup(): pl.pallas_call(regroup_kernel, out_shape=jax.ShapeDtypeStruct((2, blocks,...]
    all_to_all x1, waiting for transfers between devices: 28.9 us -> 27.5 us  [on_device(): far = lax.all_to_all(select(ids, held, stores), 'store', 0, 0, tiled=True)]
    ppermute x4 -> x3, waiting for transfers between devices: 4.92 us -> 5.88 us  [the longest x1 3.29 us: on_device(): passing = lax.ppermute(opposite, axes, ahead)]
    ppermute x4 -> x3, starting transfers between devices: 5.68 us -> 6.13 us  [the longest x1 3.49 us: on_device(): relayed = lax.ppermute(relayed, axes, ahead)]
  transfers between devices with their start and end apart: 10 -> 9, of which waited for: 4 -> 4; matrix products, arithmetic and copies ran while one was open for 2% -> 1% of each run, Pallas kernels for 22% -> 19%
where the time goes in v3:
time: 131 us; the launch traced here: 130 us
  blocking collectives  40.8 us (31%)
  waiting for transfers between devices  34.3 us (26%)
  Pallas kernels  28.4 us (22%)
  starting transfers between devices  17.6 us (13%)
  local copies, waits for them, and re-layouts  6.01 us (5%)
  other arithmetic  2.24 us (2%)
    all_to_all x1, blocking collectives, on_device(): lax.all_to_all(pack(passage_ids, other_ids, page_cache), 'store', 0, 0, t...  40.8 us
    all_to_all x1, waiting for transfers between devices, on_device(): far = lax.all_to_all(select(ids, held, stores), 'store', 0, 0, tiled=True)  27.5 us
    pallas_call x1, Pallas kernels, regroup(): pl.pallas_call(regroup_kernel, out_shape=jax.ShapeDtypeStruct((2, blocks,...  11.7 us
    pallas_call x2, Pallas kernels, attend(): pl.pallas_call(functools.partial(attention_kernel, request=request, shift...  7.33 us
    unnamed x16, local copies, waits for them, and re-layouts  5.75 us
    all_to_all x1, starting transfers between devices, on_device(): far = lax.all_to_all(select(ids, held, stores), 'store', 0, 0, tiled=True)  4.02 us
    ppermute x1, starting transfers between devices, on_device(): relayed = lax.ppermute(relayed, axes, ahead)  3.49 us
    pallas_call x1, Pallas kernels, select(): pl.pallas_call(select_kernel, out_shape=pltpu.HBM(shape, jnp.bfloat16), i...  3.31 us
  transfers between devices with their start and end apart: 9, of which 4 were waited for; matrix products, arithmetic and copies ran while one was open for 1% of the time, Pallas kernels for 19%

profile of v3, /device:TPU:1, one launch (start us, length us, event | category | flops | bytes accessed | tf_op | source)
XLA Modules:
  0.0 129.7 jit_solution(5601341325710477882)
XLA Ops:
  0.0 3.2 %collective-permute-start.2 = (s32[1,8]{1,0:T(1,128)}, s32[1,8]{1,0:T(1,128)S(1)}, u32[]{:S(2)}, u32[]{:S(2)}) collective-permute-start(s32[1,8]{1,0:T(1,128)} %own_ref.1), channel_id=1, source_target_pairs={{0,1},{1,0},{2,3},{3,2},{4,5},{5,4},{6,7},{7,6},{8,9},{9,8},{10,11... | collective-permute-start | bytes 104 | tf_op jit(solution)/shard_map/ppermute | solution.py:374
  3.2 1.0 collective-permute-done.2.other_ref
  4.2 0.3 collective-permute-start.3
  4.5 0.7 copy-done.6
  5.2 2.1 %pack.1 = bf16[32,136,128]{2,1,0:T(8,128)(2,1)} custom-call(s32[1,8]{1,0:T(1,128)S(1)} %copy-done.6, s32[1,8]{1,0:T(1,128)S(1)} %collective-permute-done.2.other_ref, bf16[8,2,256,256]{3,2,1,0:T(8,128)(2,1)} %cache_ref.1), custom_call_target="tpu_custom_call" | custom-call | bytes 2097152 | tf_op jit(solution)/shard_map/pack/pallas_call | solution.py:87
  7.3 40.8 %all_to_all.10.held_ref = bf16[32,136,128]{2,1,0:T(8,128)(2,1)S(1)} all-to-all(bf16[32,136,128]{2,1,0:T(8,128)(2,1)} %pack.1), channel_id=1, replica_groups=mesh['store'=32,'head'=4,'rep'=2] {'store'}, dimensions={0} | all-to-all | bytes 2228224 | tf_op jit(solution)/shard_map/all_to_all | solution.py:375
  48.2 3.3 %select.5 = bf16[32,2,8,16,128]{4,3,2,1,0:T(8,128)(2,1)} custom-call(s32[64,8]{1,0:T(8,128)S(1)} %convert.1.ids_ref, bf16[32,136,128]{2,1,0:T(8,128)(2,1)S(1)} %all_to_all.10.held_ref), custom_call_target="tpu_custom_call" | custom-call | bytes 2097152 | tf_op jit(solution)/shard_map/select/pallas_call | solution.py:140
  51.5 4.0 %all-to-all-start.1 = ((bf16[32,2,8,16,128]{4,3,2,1,0:T(8,128)(2,1)}), bf16[32,2,8,16,128]{4,3,2,1,0:T(8,128)(2,1)S(1)}, u32[]{:S(2)}, u32[]{:S(2)}) async-start(bf16[32,2,8,16,128]{4,3,2,1,0:T(8,128)(2,1)} %select.5), calls=%async_computation.1 | async-start | bytes 4194304 | tf_op jit(solution)/shard_map/all_to_all | solution.py:395
  55.5 1.4 %collective-permute-start.1 = (s32[1,8]{1,0:T(1,128)S(1)}, s32[1,8]{1,0:T(1,128)S(1)}, u32[]{:S(2)}, u32[]{:S(2)}) collective-permute-start(s32[1,8]{1,0:T(1,128)S(1)} %copy-done.7), channel_id=1, source_target_pairs={{0,1},{1,0},{2,3},{3,2},{4,5},{5,4},{6,7},{7,6},{8,9},{9,8},{10,11... | collective-permute-start | bytes 104 | tf_op jit(solution)/shard_map/ppermute | solution.py:384
  56.9 0.8 split_heads.1
  58.0 0.1 multiply_cosine_fusion.2
  58.1 0.1 pad_add_fusion
  58.4 0.5 fusion.2
  59.0 0.5 fusion.1
  59.6 0.7 copy-done.2
  60.3 1.0 copy-done.3
  61.3 0.3 rope_heads.1.span_ref
  61.6 3.4 %copy-done = bf16[2048,4,1,512]{3,1,2,0:T(4,128)(2,1)S(1)} copy-done((bf16[2048,4,1,512]{3,1,2,0:T(4,128)(2,1)S(1)}, bf16[2048,4,1,512]{3,1,2,0:T(4,128)(2,1)}, u32[]{:S(2)}) %copy-start) | copy-done | bytes 8388632
  65.0 11.7 %regroup.1.w_ref = bf16[2,4,2048,512]{3,2,1,0:T(8,128)(2,1)} custom-call(bf16[2048,4,512]{2,1,0:T(4,128)(2,1)S(1)} %bitcast.10, bf16[2048,4,512]{2,1,0:T(4,128)(2,1)} %collective-permute-done.3.other_ref), custom_call_target="tpu_custom_call" | custom-call | bytes 33554432 | tf_op jit(solution)/shard_map/regroup/pallas_call | solution.py:326
  76.7 27.5 %all-to-all-done.1.far_ref = bf16[32,2,8,16,128]{4,3,2,1,0:T(8,128)(2,1)S(1)} async-done(((bf16[32,2,8,16,128]{4,3,2,1,0:T(8,128)(2,1)}), bf16[32,2,8,16,128]{4,3,2,1,0:T(8,128)(2,1)S(1)}, u32[]{:S(2)}, u32[]{:S(2)}) %all-to-all-start.1) | async-done | bytes 2097184 | tf_op jit(solution)/shard_map/all_to_all | solution.py:395
  104.1 3.7 %attend1.1 = (bf16[128,1024]{1,0:T(8,128)(2,1)S(1)}, bf16[2,2,1024,512]{3,2,1,0:T(8,128)(2,1)S(1)}, bf16[2,2,1024,512]{3,2,1,0:T(8,128)(2,1)S(1)}) custom-call(bf16[2,10,128,128]{3,2,1,0:T(8,128)(2,1)S(1)} %rope_heads.1.span_ref, bf16[32,2,8,16,128]{4,3,2,1,0:T(8,128)(2,1)S(1)} %all-to-all-done.1.far_ref, f32[2,128,128]{2,1,0:T(8,128)S(1)} %get-tuple-element.23.block_ref, ...), custom_call_target="tpu_custom_call" | custom-call | flops 1140850688 | bytes 12582912 | tf_op jit(solution)/shard_map/attend1/pallas_call | solution.py:298
  107.8 2.5 %collective-permute-start.4 = (bf16[128,1024]{1,0:T(8,128)(2,1)S(1)}, bf16[128,1024]{1,0:T(8,128)(2,1)S(1)}, u32[]{:S(2)}, u32[]{:S(2)}) collective-permute-start(bf16[128,1024]{1,0:T(8,128)(2,1)S(1)} %get-tuple-element.18), channel_id=1, source_target_pairs={{0,1},{1,0},{2,3},{3,2},{4,5},{5,4},{6,7},{7,6},{8,9},{9,8},{10,11... | collective-permute-start | bytes 786440 | tf_op jit(solution)/shard_map/ppermute | solution.py:400
  110.3 3.7 %attend0.1 = (bf16[128,1024]{1,0:T(8,128)(2,1)S(1)}, bf16[2,2,1024,512]{3,2,1,0:T(8,128)(2,1)S(1)}, bf16[2,2,1024,512]{3,2,1,0:T(8,128)(2,1)S(1)}) custom-call(bf16[2,10,128,128]{3,2,1,0:T(8,128)(2,1)S(1)} %rope_heads.1.span_ref, bf16[32,2,8,16,128]{4,3,2,1,0:T(8,128)(2,1)S(1)} %all-to-all-done.1.far_ref, f32[2,128,128]{2,1,0:T(8,128)S(1)} %get-tuple-element.24.block_ref, ...), custom_call_target="tpu_custom_call" | custom-call | flops 1140850688 | bytes 12582912 | tf_op jit(solution)/shard_map/attend0/pallas_call | solution.py:298
  113.9 0.7 opposite.1
  114.7 2.6 %collective-permute-start.6 = (bf16[128,1024]{1,0:T(8,128)(2,1)S(1)}, bf16[128,1024]{1,0:T(8,128)(2,1)S(1)}, u32[]{:S(2)}, u32[]{:S(2)}) collective-permute-start(bf16[128,1024]{1,0:T(8,128)(2,1)S(1)} %opposite.1), channel_id=1, source_target_pairs={{0,2},{1,7},{2,4},{3,1},{4,6},{5,3},{6,0},{7,5},{8,10},{9,15},{10,... | collective-permute-start | bytes 786440 | tf_op jit(solution)/shard_map/ppermute | solution.py:412
  117.2 0.7 plain.1
  118.0 3.3 %collective-permute-done.6.refs_0_ = bf16[128,1024]{1,0:T(8,128)(2,1)S(1)} collective-permute-done((bf16[128,1024]{1,0:T(8,128)(2,1)S(1)}, bf16[128,1024]{1,0:T(8,128)(2,1)S(1)}, u32[]{:S(2)}, u32[]{:S(2)}) %collective-permute-start.6) | collective-permute-done | bytes 262176 | tf_op jit(solution)/shard_map/ppermute | solution.py:412
  121.3 0.7 relayed.1
  122.0 3.5 %collective-permute-start.7 = (bf16[128,1024]{1,0:T(8,128)(2,1)S(1)}, bf16[128,1024]{1,0:T(8,128)(2,1)S(1)}, u32[]{:S(2)}, u32[]{:S(2)}) collective-permute-start(bf16[128,1024]{1,0:T(8,128)(2,1)S(1)} %relayed.1), channel_id=1, source_target_pairs={{0,2},{1,7},{2,4},{3,1},{4,6},{5,3},{6,0},{7,5},{8,10},{9,15},{10,... | collective-permute-start | bytes 786440 | tf_op jit(solution)/shard_map/ppermute | solution.py:416
  125.5 0.7 kept.1
  126.3 2.6 %collective-permute-done.7 = bf16[128,1024]{1,0:T(8,128)(2,1)S(1)} collective-permute-done((bf16[128,1024]{1,0:T(8,128)(2,1)S(1)}, bf16[128,1024]{1,0:T(8,128)(2,1)S(1)}, u32[]{:S(2)}, u32[]{:S(2)}) %collective-permute-start.7) | collective-permute-done | bytes 262176 | tf_op jit(solution)/shard_map/ppermute | solution.py:416
  128.9 0.8 fusion
  (33 shorter events, 0.6 us)
Async XLA Ops:
  0.0 4.2 %collective-permute-start.2 = (s32[1,8]{1,0:T(1,128)}, s32[1,8]{1,0:T(1,128)S(1)}, u32[]{:S(2)}, u32[]{:S(2)}) collective-permute-start(s32[1,8]{1,0:T(1,128)} %own_ref.1), channel_id=1, source_target_pairs={{0,1},{1,0},{2,3},{3,2},{4,5},{5,4},{6,7},{7,6},{8,9},{9,8},{10,11... | collective-permute-start | bytes 104 | tf_op jit(solution)/shard_map/ppermute | solution.py:374
  4.2 57.4 %collective-permute-start.3 = (bf16[2048,4,512]{2,1,0:T(4,128)(2,1)}, bf16[2048,4,512]{2,1,0:T(4,128)(2,1)}, u32[]{:S(2)}, u32[]{:S(2)}) collective-permute-start(bf16[2048,4,512]{2,1,0:T(4,128)(2,1)} %bitcast.9), channel_id=1, source_target_pairs={{0,1},{1,0},{2,3},{3,2},{4,5},{5,4},{6,7},{7,6},{8,9},{9,8},{10,11... | collective-permute-start | bytes 25165832 | tf_op jit(solution)/shard_map/ppermute | solution.py:381
  4.5 0.7 copy-start.6
  48.1 7.4 %copy-start.7 = (s32[1,8]{1,0:T(1,128)S(1)}, s32[1,8]{1,0:T(1,128)}, u32[]{:S(2)}) copy-start(s32[1,8]{1,0:T(1,128)} %param.12) | copy-start | bytes 100
  48.1 8.8 %copy-start.1 = (bf16[1,128,2048]{2,1,0:T(8,128)(2,1)S(1)}, bf16[1,128,2048]{2,1,0:T(8,128)(2,1)}, u32[]{:S(2)}) copy-start(bf16[1,128,2048]{2,1,0:T(8,128)(2,1)} %q_ref.1) | copy-start | bytes 1572868
  48.1 8.8 %copy-start.4 = (bf16[1,128,256]{2,1,0:T(8,128)(2,1)S(1)}, bf16[1,128,256]{2,1,0:T(8,128)(2,1)}, u32[]{:S(2)}) copy-start(bf16[1,128,256]{2,1,0:T(8,128)(2,1)} %k_ref.1) | copy-start | bytes 196612
  48.1 8.8 %copy-start.5 = (bf16[1,128,256]{2,1,0:T(8,128)(2,1)S(1)}, bf16[1,128,256]{2,1,0:T(8,128)(2,1)}, u32[]{:S(2)}) copy-start(bf16[1,128,256]{2,1,0:T(8,128)(2,1)} %v_ref.1) | copy-start | bytes 196612
  51.5 52.6 %all-to-all-start.1 = ((bf16[32,2,8,16,128]{4,3,2,1,0:T(8,128)(2,1)}), bf16[32,2,8,16,128]{4,3,2,1,0:T(8,128)(2,1)S(1)}, u32[]{:S(2)}, u32[]{:S(2)}) async-start(bf16[32,2,8,16,128]{4,3,2,1,0:T(8,128)(2,1)} %select.5), calls=%async_computation.1 | async-start | bytes 4194304 | tf_op jit(solution)/shard_map/all_to_all | solution.py:395
  55.5 2.6 %collective-permute-start.1 = (s32[1,8]{1,0:T(1,128)S(1)}, s32[1,8]{1,0:T(1,128)S(1)}, u32[]{:S(2)}, u32[]{:S(2)}) collective-permute-start(s32[1,8]{1,0:T(1,128)S(1)} %copy-done.7), channel_id=1, source_target_pairs={{0,1},{1,0},{2,3},{3,2},{4,5},{5,4},{6,7},{7,6},{8,9},{9,8},{10,11... | collective-permute-start | bytes 104 | tf_op jit(solution)/shard_map/ppermute | solution.py:384
  57.7 1.8 %collective-permute-start = (bf16[128,1280]{1,0:T(8,128)(2,1)}, bf16[128,1280]{1,0:T(8,128)(2,1)S(1)}, u32[]{:S(2)}, u32[]{:S(2)}) collective-permute-start(bf16[128,1280]{1,0:T(8,128)(2,1)} %get-tuple-element.15), channel_id=1, source_target_pairs={{0,1},{1,0},{2,3},{3,2},{4,5},{5,4},{6,7},{7,6},{8,9},{9,8},{10,11... | collective-permute-start | bytes 983048 | tf_op jit(solution)/shard_map/ppermute | solution.py:383
  59.6 0.7 copy-start.2
  60.3 1.0 copy-start.3
  61.6 3.4 %copy-start = (bf16[2048,4,1,512]{3,1,2,0:T(4,128)(2,1)S(1)}, bf16[2048,4,1,512]{3,1,2,0:T(4,128)(2,1)}, u32[]{:S(2)}) copy-start(bf16[2048,4,1,512]{3,1,2,0:T(4,128)(2,1)} %param.13) | copy-start | bytes 25165828
  107.8 6.2 %collective-permute-start.4 = (bf16[128,1024]{1,0:T(8,128)(2,1)S(1)}, bf16[128,1024]{1,0:T(8,128)(2,1)S(1)}, u32[]{:S(2)}, u32[]{:S(2)}) collective-permute-start(bf16[128,1024]{1,0:T(8,128)(2,1)S(1)} %get-tuple-element.18), channel_id=1, source_target_pairs={{0,1},{1,0},{2,3},{3,2},{4,5},{5,4},{6,7},{7,6},{8,9},{9,8},{10,11... | collective-permute-start | bytes 786440 | tf_op jit(solution)/shard_map/ppermute | solution.py:400
  114.7 6.7 %collective-permute-start.6 = (bf16[128,1024]{1,0:T(8,128)(2,1)S(1)}, bf16[128,1024]{1,0:T(8,128)(2,1)S(1)}, u32[]{:S(2)}, u32[]{:S(2)}) collective-permute-start(bf16[128,1024]{1,0:T(8,128)(2,1)S(1)} %opposite.1), channel_id=1, source_target_pairs={{0,2},{1,7},{2,4},{3,1},{4,6},{5,3},{6,0},{7,5},{8,10},{9,15},{10,... | collective-permute-start | bytes 786440 | tf_op jit(solution)/shard_map/ppermute | solution.py:412
  117.9 8.3 %collective-permute-start.5 = (bf16[128,1024]{1,0:T(8,128)(2,1)S(1)}, bf16[128,1024]{1,0:T(8,128)(2,1)S(1)}, u32[]{:S(2)}, u32[]{:S(2)}) collective-permute-start(bf16[128,1024]{1,0:T(8,128)(2,1)S(1)} %plain.1), channel_id=1, source_target_pairs={{0,6},{1,3},{2,0},{3,5},{4,2},{5,7},{6,4},{7,1},{8,14},{9,11},{10,... | collective-permute-start | bytes 786440 | tf_op jit(solution)/shard_map/ppermute | solution.py:414
  122.0 6.8 %collective-permute-start.7 = (bf16[128,1024]{1,0:T(8,128)(2,1)S(1)}, bf16[128,1024]{1,0:T(8,128)(2,1)S(1)}, u32[]{:S(2)}, u32[]{:S(2)}) collective-permute-start(bf16[128,1024]{1,0:T(8,128)(2,1)S(1)} %relayed.1), channel_id=1, source_target_pairs={{0,2},{1,7},{2,4},{3,1},{4,6},{5,3},{6,0},{7,5},{8,10},{9,15},{10,... | collective-permute-start | bytes 786440 | tf_op jit(solution)/shard_map/ppermute | solution.py:416

commit v4 on v3

--- a/solution.py
+++ b/solution.py
@@ -45,24 +45,16 @@
     return (x * cosine + other * sine).astype(jnp.bfloat16)
 
 
-def pack_kernel(own_ref, other_ref, cache_ref, out_ref, held_ref, rows_ref, sems, out_sems):
+def pack_kernel(cache_ref, out_ref, held_ref, rows_ref, sems, out_sems):
     passages, kinds, page_len, _ = cache_ref.shape
     blocks = page_len // BLK
-    rep = lax.axis_index("rep")
-    lanes = pl.ds(pl.multiple_of(rep * HD, HD), HD)
+    lanes = pl.ds(pl.multiple_of(lax.axis_index("rep") * HD, HD), HD)
     copies = [
         pltpu.make_async_copy(cache_ref.at[:, kind, :, lanes], held_ref.at[kind], sems.at[kind])
         for kind in range(kinds)
     ]
     for copy in copies:
         copy.start()
-    row = lax.broadcasted_iota(jnp.int32, (IDS, HD), 0)
-    lane = lax.broadcasted_iota(jnp.int32, (IDS, HD), 1)
-    named = jnp.zeros((IDS, HD), jnp.int32)
-    for slot in range(own_ref.shape[1]):
-        named = jnp.where((row == rep) & (lane == slot), own_ref[:, slot : slot + 1], named)
-        named = jnp.where((row == 1 - rep) & (lane == slot), other_ref[:, slot : slot + 1], named)
-    named = named.astype(jnp.float32).astype(jnp.bfloat16)
     outs = []
     for kind in range(kinds):
         copies[kind].wait()
@@ -71,7 +63,7 @@
                 rows_ref[kind * blocks + block, passage * BLK : (passage + 1) * BLK] = held_ref[
                     kind, passage, block * BLK : (block + 1) * BLK
                 ]
-            rows_ref[kind * blocks + block, passages * BLK :] = named
+            rows_ref[kind * blocks + block, passages * BLK :] = jnp.zeros((IDS, HD), jnp.bfloat16)
         part = pl.ds(kind * blocks, blocks)
         outs.append(
             pltpu.make_async_copy(rows_ref.at[part], out_ref.at[part], out_sems.at[kind])
@@ -81,13 +73,13 @@
         copy.wait()
 
 
-def pack(own_ids, other_ids, page_cache):
+def pack(page_cache):
     passages, kinds, page_len, _ = page_cache.shape
     shape = (kinds * page_len // BLK, passages * BLK + IDS, HD)
     return pl.pallas_call(
         pack_kernel,
         out_shape=pltpu.HBM(shape, jnp.bfloat16),
-        in_specs=[VMEM, VMEM, HBM],
+        in_specs=[HBM],
         out_specs=HBM,
         scratch_shapes=[
             pltpu.VMEM((kinds, passages, page_len, HD), jnp.bfloat16),
@@ -98,17 +90,13 @@
         compiler_params=pltpu.CompilerParams(vmem_limit_bytes=FULL),
         cost_estimate=cost(0, 2 << 20),
         name="pack",
-    )(own_ids, other_ids, in_hbm(page_cache))
-
-
-def select_kernel(ids_ref, held_ref, out_ref, chosen_ref, sems):
-    stores, requests, slots = out_ref.shape[:3]
-    passages = (held_ref.shape[1] - IDS) // BLK
-    shift = passages.bit_length() - 1
-    assert passages == 1 << shift
-    rep = lax.axis_index("rep")
+    )(in_hbm(page_cache))
+
+
+def select_kernel(first_ref, held_ref, out_ref, chosen_ref, sems):
+    dests, slots, pieces = out_ref.shape[:3]
     chunks = sems.shape[0]
-    per = stores // chunks
+    per = dests // chunks
 
     def copy_out(chunk):
         part = pl.ds(chunk * per, per)
@@ -117,14 +105,8 @@
     def fill(chunk, carry):
         for at in range(per):
             dest = chunk * per + at
-            for request in range(requests):
-                row = dest * requests + (rep ^ request)
-                for slot in range(slots):
-                    wanted = ids_ref[row, slot]
-                    start = pl.multiple_of((wanted & (passages - 1)) * BLK, BLK)
-                    chosen_ref[dest, request, slot] = held_ref[
-                        lax.shift_right_logical(wanted, shift), pl.ds(start, BLK)
-                    ]
+            for slot in range(slots):
+                chosen_ref[dest, slot] = held_ref[pl.ds(first_ref[dest, slot], pieces)]
         copy_out(chunk).start()
         return carry
 
@@ -133,20 +115,18 @@
         copy_out(chunk).wait()
 
 
-def select(ids, held, stores):
-    slots = ids.shape[1]
-    requests = ids.shape[0] // stores
-    shape = (stores, requests, slots, BLK, HD)
+def select(first, held, pieces):
+    shape = first.shape + (pieces,) + held.shape[1:]
     return pl.pallas_call(
         select_kernel,
         out_shape=pltpu.HBM(shape, jnp.bfloat16),
         in_specs=[SMEM, VMEM],
         out_specs=HBM,
         scratch_shapes=[pltpu.VMEM(shape, jnp.bfloat16), pltpu.SemaphoreType.DMA((8,))],
-        compiler_params=pltpu.CompilerParams(vmem_limit_bytes=8 << 20),
+        compiler_params=pltpu.CompilerParams(vmem_limit_bytes=12 << 20),
         cost_estimate=cost(0, 2 << 20),
         name="select",
-    )(ids, held)
+    )(first, held)
 
 
 def split_kernel(q_ref, k_ref, v_ref, kept_ref, sent_ref):
@@ -371,12 +351,25 @@
     tokens = queries.shape[1]
     page_blocks = page_len // BLK
 
+    rep = lax.axis_index("rep")
     other_ids = lax.ppermute(passage_ids, "rep", SWAP)
-    held = lax.all_to_all(pack(passage_ids, other_ids, page_cache), "store", 0, 0, tiled=True)
+    row = jnp.arange(IDS, dtype=jnp.int32)[:, None]
+    named = jnp.where(row == rep, passage_ids, jnp.where(row == 1 - rep, other_ids, 0))
+    named = jnp.pad(named.astype(jnp.bfloat16), ((0, 0), (0, HD - pass_count)))
+    packed = lax.dynamic_update_slice(
+        pack(page_cache),
+        jnp.broadcast_to(named, (stores, IDS, HD)),
+        (0, per_store * BLK, 0),
+    )
+    held = lax.all_to_all(packed, "store", 0, 0, tiled=True)
     ids = held[:, per_store * BLK : per_store * BLK + 2, :pass_count].astype(jnp.int32)
-    ids = ids.reshape(2 * stores, pass_count)
-
-    out_weight, _ = lax.optimization_barrier((out_weight, other_ids))
+    ids = jnp.where(rep == 0, ids, ids[:, ::-1]).reshape(2 * stores, pass_count)
+    pieces = BLK // IDS
+    first = ids // per_store * (per_store * pieces + 1) + ids % per_store * pieces
+    chosen = select(first, held.reshape(-1, IDS, HD), pieces)
+    chosen = chosen.reshape(stores, 2, pass_count, BLK, HD)
+
+    out_weight, _ = lax.optimization_barrier((out_weight, packed))
     raw = out_weight[:, :, 0, :]
     weights = regroup(raw, lax.ppermute(raw, "rep", SWAP))
     kept, sent = split_heads(queries, span_keys, span_values)
@@ -392,7 +385,7 @@
     block_angles = jnp.stack(angle_tables(block_pos.reshape(2, -1)), axis=1)
     token_angles = jnp.stack(angle_tables(jnp.arange(BLK, dtype=jnp.int32)))
 
-    far = lax.all_to_all(select(ids, held, stores), "store", 0, 0, tiled=True)
+    far = lax.all_to_all(chosen, "store", 0, 0, tiled=True)
 
     other, opposite_w, plain_w = attend(
         span, far, block_angles[1], token_angles, weights, 1, ((2, 2), (3, 1))

time: 131 us -> 129 us (0.985)
  blocking collectives: 40.8 us -> 0 us
  waiting for transfers between devices: 34.3 us -> 59.7 us
  starting transfers between devices: 17.6 us -> 31.3 us
    all_to_all x1 -> x0, blocking collectives: 40.8 us -> none  [on_device(): lax.all_to_all(pack(passage_ids, other_ids, page_cache), 'store', 0, 0, t...]
    all_to_all x1 -> x2, waiting for transfers between devices: 27.5 us -> 53.8 us  [the longest x1 27.4 us: on_device(): far = lax.all_to_all(chosen, 'store', 0, 0, tiled=True)]
    all_to_all x1 -> x2, starting transfers between devices: 4.02 us -> 17.8 us  [the longest x1 9.47 us: on_device(): held = lax.all_to_all(packed, 'store', 0, 0, tiled=True)]
  transfers between devices with their start and end apart: 9 -> 10, of which waited for: 4 -> 4; matrix products, arithmetic and copies ran while one was open for 1% -> 1% of each run, Pallas kernels for 19% -> 18%
where the time goes in v4:
time: 129 us; the launch traced here: 128 us
  waiting for transfers between devices  59.7 us (46%)
  starting transfers between devices  31.3 us (24%)
  Pallas kernels  27.7 us (21%)
  local copies, waits for them, and re-layouts  6.11 us (5%)
  other arithmetic  2.39 us (2%)
    all_to_all x1, waiting for transfers between devices, on_device(): far = lax.all_to_all(chosen, 'store', 0, 0, tiled=True)  27.4 us
    all_to_all x1, waiting for transfers between devices, on_device(): held = lax.all_to_all(packed, 'store', 0, 0, tiled=True)  26.4 us
    pallas_call x1, Pallas kernels, regroup(): pl.pallas_call(regroup_kernel, out_shape=jax.ShapeDtypeStruct((2, blocks,...  11.7 us
    all_to_all x1, starting transfers between devices, on_device(): held = lax.all_to_all(packed, 'store', 0, 0, tiled=True)  9.47 us
    all_to_all x1, starting transfers between devices, on_device(): far = lax.all_to_all(chosen, 'store', 0, 0, tiled=True)  8.28 us
    pallas_call x2, Pallas kernels, attend(): pl.pallas_call(functools.partial(attention_kernel, request=request, shift...  7.32 us
    unnamed x16, local copies, waits for them, and re-layouts  5.11 us
    ppermute x1, starting transfers between devices, on_device(): relayed = lax.ppermute(relayed, axes, ahead)  3.49 us
  transfers between devices with their start and end apart: 10, of which 4 were waited for; matrix products, arithmetic and copies ran while one was open for 1% of the time, Pallas kernels for 18%

profile of v4, /device:TPU:1, one launch (start us, length us, event | category | flops | bytes accessed | tf_op | source)
XLA Modules:
  0.0 127.5 jit_solution(160854205997639613)
XLA Ops:
  0.0 3.2 %collective-permute-start.2 = (s32[1,8]{1,0:T(1,128)}, s32[1,8]{1,0:T(1,128)S(1)}, u32[]{:S(2)}, u32[]{:S(2)}) collective-permute-start(s32[1,8]{1,0:T(1,128)} %param.11), channel_id=1, source_target_pairs={{0,1},{1,0},{2,3},{3,2},{4,5},{5,4},{6,7},{7,6},{8,9},{9,8},{10,11... | collective-permute-start | bytes 104 | tf_op jit(solution)/shard_map/ppermute | solution.py:355
  3.2 2.1 %pack.1 = bf16[32,136,128]{2,1,0:T(8,128)(2,1)} custom-call(bf16[8,2,256,256]{3,2,1,0:T(8,128)(2,1)} %cache_ref.1), custom_call_target="tpu_custom_call" | custom-call | bytes 2097152 | tf_op jit(solution)/shard_map/pack/pallas_call | solution.py:79
  5.5 0.7 broadcast_dynamic-update-slice_fusion
  6.2 9.5 %all-to-all-start = ((bf16[32,136,128]{2,1,0:T(8,128)(2,1)}), bf16[32,136,128]{2,1,0:T(8,128)(2,1)S(1)}, u32[]{:S(2)}, u32[]{:S(2)}) async-start(bf16[32,136,128]{2,1,0:T(8,128)(2,1)} %broadcast_dynamic-update-slice_fusion), calls=%async_computation | async-start | bytes 2228224 | tf_op jit(solution)/shard_map/all_to_all | solution.py:364
  15.7 26.4 %all-to-all-done = bf16[32,136,128]{2,1,0:T(8,128)(2,1)S(1)} async-done(((bf16[32,136,128]{2,1,0:T(8,128)(2,1)}), bf16[32,136,128]{2,1,0:T(8,128)(2,1)S(1)}, u32[]{:S(2)}, u32[]{:S(2)}) %all-to-all-start) | async-done | bytes 1114144 | tf_op jit(solution)/shard_map/all_to_all | solution.py:364
  42.2 2.6 %select.12 = bf16[64,8,2,8,128]{4,3,2,1,0:T(8,128)(2,1)} custom-call(s32[64,8]{1,0:T(8,128)S(1)} %fusion.7.first_ref, bf16[544,8,128]{2,1,0:T(8,128)(2,1)S(1)} %bitcast.14), custom_call_target="tpu_custom_call" | custom-call | bytes 2097152 | tf_op jit(solution)/shard_map/select/pallas_call | solution.py:120
  44.9 8.3 %all-to-all-start.1 = ((bf16[32,2,8,16,128]{4,3,2,1,0:T(8,128)(2,1)}), bf16[32,2,8,16,128]{4,3,2,1,0:T(8,128)(2,1)S(1)}, u32[]{:S(2)}, u32[]{:S(2)}) async-start(bf16[32,2,8,16,128]{4,3,2,1,0:T(8,128)(2,1)} %bitcast.15), calls=%async_computation.1 | async-start | bytes 4194304 | tf_op jit(solution)/shard_map/all_to_all | solution.py:388
  53.2 1.6 %collective-permute-start.1 = (s32[1,8]{1,0:T(1,128)S(1)}, s32[1,8]{1,0:T(1,128)S(1)}, u32[]{:S(2)}, u32[]{:S(2)}) collective-permute-start(s32[1,8]{1,0:T(1,128)S(1)} %copy-done.6), channel_id=1, source_target_pairs={{0,1},{1,0},{2,3},{3,2},{4,5},{5,4},{6,7},{7,6},{8,9},{9,8},{10,11... | collective-permute-start | bytes 104 | tf_op jit(solution)/shard_map/ppermute | solution.py:377
  54.8 0.8 split_heads.1
  55.7 0.1 add.99
  55.8 0.1 multiply_cosine_fusion.2
  56.0 0.1 pad_add_fusion
  56.3 0.5 fusion.2
  56.9 0.5 fusion.1
  57.5 0.7 copy-done.2
  58.2 1.0 copy-done.3
  59.2 0.3 rope_heads.1.span_ref
  59.5 3.4 %copy-done = bf16[2048,4,1,512]{3,1,2,0:T(4,128)(2,1)S(1)} copy-done((bf16[2048,4,1,512]{3,1,2,0:T(4,128)(2,1)S(1)}, bf16[2048,4,1,512]{3,1,2,0:T(4,128)(2,1)}, u32[]{:S(2)}) %copy-start) | copy-done | bytes 8388632
  62.8 11.7 %regroup.1.w_ref = bf16[2,4,2048,512]{3,2,1,0:T(8,128)(2,1)} custom-call(bf16[2048,4,512]{2,1,0:T(4,128)(2,1)S(1)} %bitcast.13, bf16[2048,4,512]{2,1,0:T(4,128)(2,1)} %collective-permute-done.3.other_ref), custom_call_target="tpu_custom_call" | custom-call | bytes 33554432 | tf_op jit(solution)/shard_map/regroup/pallas_call | solution.py:306
  74.5 27.4 %all-to-all-done.1.far_ref = bf16[32,2,8,16,128]{4,3,2,1,0:T(8,128)(2,1)S(1)} async-done(((bf16[32,2,8,16,128]{4,3,2,1,0:T(8,128)(2,1)}), bf16[32,2,8,16,128]{4,3,2,1,0:T(8,128)(2,1)S(1)}, u32[]{:S(2)}, u32[]{:S(2)}) %all-to-all-start.1) | async-done | bytes 2097184 | tf_op jit(solution)/shard_map/all_to_all | solution.py:388
  101.9 3.7 %attend1.1 = (bf16[128,1024]{1,0:T(8,128)(2,1)S(1)}, bf16[2,2,1024,512]{3,2,1,0:T(8,128)(2,1)S(1)}, bf16[2,2,1024,512]{3,2,1,0:T(8,128)(2,1)S(1)}) custom-call(bf16[2,10,128,128]{3,2,1,0:T(8,128)(2,1)S(1)} %rope_heads.1.span_ref, bf16[32,2,8,16,128]{4,3,2,1,0:T(8,128)(2,1)S(1)} %all-to-all-done.1.far_ref, f32[2,128,128]{2,1,0:T(8,128)S(1)} %get-tuple-element.23.block_ref, ...), custom_call_target="tpu_custom_call" | custom-call | flops 1140850688 | bytes 12582912 | tf_op jit(solution)/shard_map/attend1/pallas_call | solution.py:278
  105.6 2.6 %collective-permute-start.4 = (bf16[128,1024]{1,0:T(8,128)(2,1)S(1)}, bf16[128,1024]{1,0:T(8,128)(2,1)S(1)}, u32[]{:S(2)}, u32[]{:S(2)}) collective-permute-start(bf16[128,1024]{1,0:T(8,128)(2,1)S(1)} %get-tuple-element.18), channel_id=1, source_target_pairs={{0,1},{1,0},{2,3},{3,2},{4,5},{5,4},{6,7},{7,6},{8,9},{9,8},{10,11... | collective-permute-start | bytes 786440 | tf_op jit(solution)/shard_map/ppermute | solution.py:393
  108.1 3.7 %attend0.1 = (bf16[128,1024]{1,0:T(8,128)(2,1)S(1)}, bf16[2,2,1024,512]{3,2,1,0:T(8,128)(2,1)S(1)}, bf16[2,2,1024,512]{3,2,1,0:T(8,128)(2,1)S(1)}) custom-call(bf16[2,10,128,128]{3,2,1,0:T(8,128)(2,1)S(1)} %rope_heads.1.span_ref, bf16[32,2,8,16,128]{4,3,2,1,0:T(8,128)(2,1)S(1)} %all-to-all-done.1.far_ref, f32[2,128,128]{2,1,0:T(8,128)S(1)} %get-tuple-element.24.block_ref, ...), custom_call_target="tpu_custom_call" | custom-call | flops 1140850688 | bytes 12582912 | tf_op jit(solution)/shard_map/attend0/pallas_call | solution.py:278
  111.8 0.7 opposite.1
  112.5 2.6 %collective-permute-start.6 = (bf16[128,1024]{1,0:T(8,128)(2,1)S(1)}, bf16[128,1024]{1,0:T(8,128)(2,1)S(1)}, u32[]{:S(2)}, u32[]{:S(2)}) collective-permute-start(bf16[128,1024]{1,0:T(8,128)(2,1)S(1)} %opposite.1), channel_id=1, source_target_pairs={{0,2},{1,7},{2,4},{3,1},{4,6},{5,3},{6,0},{7,5},{8,10},{9,15},{10,... | collective-permute-start | bytes 786440 | tf_op jit(solution)/shard_map/ppermute | solution.py:405
  115.1 0.7 plain.1
  115.9 3.3 %collective-permute-done.6.refs_0_ = bf16[128,1024]{1,0:T(8,128)(2,1)S(1)} collective-permute-done((bf16[128,1024]{1,0:T(8,128)(2,1)S(1)}, bf16[128,1024]{1,0:T(8,128)(2,1)S(1)}, u32[]{:S(2)}, u32[]{:S(2)}) %collective-permute-start.6) | collective-permute-done | bytes 262176 | tf_op jit(solution)/shard_map/ppermute | solution.py:405
  119.2 0.7 relayed.1
  119.9 3.5 %collective-permute-start.7 = (bf16[128,1024]{1,0:T(8,128)(2,1)S(1)}, bf16[128,1024]{1,0:T(8,128)(2,1)S(1)}, u32[]{:S(2)}, u32[]{:S(2)}) collective-permute-start(bf16[128,1024]{1,0:T(8,128)(2,1)S(1)} %relayed.1), channel_id=1, source_target_pairs={{0,2},{1,7},{2,4},{3,1},{4,6},{5,3},{6,0},{7,5},{8,10},{9,15},{10,... | collective-permute-start | bytes 786440 | tf_op jit(solution)/shard_map/ppermute | solution.py:409
  123.4 0.7 kept.1
  124.1 2.6 %collective-permute-done.7 = bf16[128,1024]{1,0:T(8,128)(2,1)S(1)} collective-permute-done((bf16[128,1024]{1,0:T(8,128)(2,1)S(1)}, bf16[128,1024]{1,0:T(8,128)(2,1)S(1)}, u32[]{:S(2)}, u32[]{:S(2)}) %collective-permute-start.7) | collective-permute-done | bytes 262176 | tf_op jit(solution)/shard_map/ppermute | solution.py:409
  126.7 0.8 fusion
  (40 shorter events, 0.8 us)
Async XLA Ops:
  0.0 5.4 %copy-start.7 = (s32[1,8]{1,0:T(1,128)S(1)}, s32[1,8]{1,0:T(1,128)}, u32[]{:S(2)}) copy-start(s32[1,8]{1,0:T(1,128)} %param.11) | copy-start | bytes 100
  0.0 5.4 %collective-permute-start.2 = (s32[1,8]{1,0:T(1,128)}, s32[1,8]{1,0:T(1,128)S(1)}, u32[]{:S(2)}, u32[]{:S(2)}) collective-permute-start(s32[1,8]{1,0:T(1,128)} %param.11), channel_id=1, source_target_pairs={{0,1},{1,0},{2,3},{3,2},{4,5},{5,4},{6,7},{7,6},{8,9},{9,8},{10,11... | collective-permute-start | bytes 104 | tf_op jit(solution)/shard_map/ppermute | solution.py:355
  6.2 53.3 %collective-permute-start.3 = (bf16[2048,4,512]{2,1,0:T(4,128)(2,1)}, bf16[2048,4,512]{2,1,0:T(4,128)(2,1)}, u32[]{:S(2)}, u32[]{:S(2)}) collective-permute-start(bf16[2048,4,512]{2,1,0:T(4,128)(2,1)} %bitcast.12), channel_id=1, source_target_pairs={{0,1},{1,0},{2,3},{3,2},{4,5},{5,4},{6,7},{7,6},{8,9},{9,8},{10,11... | collective-permute-start | bytes 25165832 | tf_op jit(solution)/shard_map/ppermute | solution.py:374
  6.2 35.9 %all-to-all-start = ((bf16[32,136,128]{2,1,0:T(8,128)(2,1)}), bf16[32,136,128]{2,1,0:T(8,128)(2,1)S(1)}, u32[]{:S(2)}, u32[]{:S(2)}) async-start(bf16[32,136,128]{2,1,0:T(8,128)(2,1)} %broadcast_dynamic-update-slice_fusion), calls=%async_computation | async-start | bytes 2228224 | tf_op jit(solution)/shard_map/all_to_all | solution.py:364
  44.9 8.3 %copy-start.6 = (s32[1,8]{1,0:T(1,128)S(1)}, s32[1,8]{1,0:T(1,128)}, u32[]{:S(2)}) copy-start(s32[1,8]{1,0:T(1,128)} %param.12) | copy-start | bytes 100
  44.9 9.9 %copy-start.1 = (bf16[1,128,2048]{2,1,0:T(8,128)(2,1)S(1)}, bf16[1,128,2048]{2,1,0:T(8,128)(2,1)}, u32[]{:S(2)}) copy-start(bf16[1,128,2048]{2,1,0:T(8,128)(2,1)} %q_ref.1) | copy-start | bytes 1572868
  44.9 9.9 %copy-start.4 = (bf16[1,128,256]{2,1,0:T(8,128)(2,1)S(1)}, bf16[1,128,256]{2,1,0:T(8,128)(2,1)}, u32[]{:S(2)}) copy-start(bf16[1,128,256]{2,1,0:T(8,128)(2,1)} %k_ref.1) | copy-start | bytes 196612
  44.9 9.9 %copy-start.5 = (bf16[1,128,256]{2,1,0:T(8,128)(2,1)S(1)}, bf16[1,128,256]{2,1,0:T(8,128)(2,1)}, u32[]{:S(2)}) copy-start(bf16[1,128,256]{2,1,0:T(8,128)(2,1)} %v_ref.1) | copy-start | bytes 196612
  44.9 57.0 %all-to-all-start.1 = ((bf16[32,2,8,16,128]{4,3,2,1,0:T(8,128)(2,1)}), bf16[32,2,8,16,128]{4,3,2,1,0:T(8,128)(2,1)S(1)}, u32[]{:S(2)}, u32[]{:S(2)}) async-start(bf16[32,2,8,16,128]{4,3,2,1,0:T(8,128)(2,1)} %bitcast.15), calls=%async_computation.1 | async-start | bytes 4194304 | tf_op jit(solution)/shard_map/all_to_all | solution.py:388
  53.2 2.8 %collective-permute-start.1 = (s32[1,8]{1,0:T(1,128)S(1)}, s32[1,8]{1,0:T(1,128)S(1)}, u32[]{:S(2)}, u32[]{:S(2)}) collective-permute-start(s32[1,8]{1,0:T(1,128)S(1)} %copy-done.6), channel_id=1, source_target_pairs={{0,1},{1,0},{2,3},{3,2},{4,5},{5,4},{6,7},{7,6},{8,9},{9,8},{10,11... | collective-permute-start | bytes 104 | tf_op jit(solution)/shard_map/ppermute | solution.py:377
  55.6 1.8 %collective-permute-start = (bf16[128,1280]{1,0:T(8,128)(2,1)}, bf16[128,1280]{1,0:T(8,128)(2,1)S(1)}, u32[]{:S(2)}, u32[]{:S(2)}) collective-permute-start(bf16[128,1280]{1,0:T(8,128)(2,1)} %get-tuple-element.15), channel_id=1, source_target_pairs={{0,1},{1,0},{2,3},{3,2},{4,5},{5,4},{6,7},{7,6},{8,9},{9,8},{10,11... | collective-permute-start | bytes 983048 | tf_op jit(solution)/shard_map/ppermute | solution.py:376
  57.5 0.7 copy-start.2
  58.2 1.0 copy-start.3
  59.5 3.4 %copy-start = (bf16[2048,4,1,512]{3,1,2,0:T(4,128)(2,1)S(1)}, bf16[2048,4,1,512]{3,1,2,0:T(4,128)(2,1)}, u32[]{:S(2)}) copy-start(bf16[2048,4,1,512]{3,1,2,0:T(4,128)(2,1)} %param.13) | copy-start | bytes 25165828
  105.6 6.2 %collective-permute-start.4 = (bf16[128,1024]{1,0:T(8,128)(2,1)S(1)}, bf16[128,1024]{1,0:T(8,128)(2,1)S(1)}, u32[]{:S(2)}, u32[]{:S(2)}) collective-permute-start(bf16[128,1024]{1,0:T(8,128)(2,1)S(1)} %get-tuple-element.18), channel_id=1, source_target_pairs={{0,1},{1,0},{2,3},{3,2},{4,5},{5,4},{6,7},{7,6},{8,9},{9,8},{10,11... | collective-permute-start | bytes 786440 | tf_op jit(solution)/shard_map/ppermute | solution.py:393
  112.5 6.7 %collective-permute-start.6 = (bf16[128,1024]{1,0:T(8,128)(2,1)S(1)}, bf16[128,1024]{1,0:T(8,128)(2,1)S(1)}, u32[]{:S(2)}, u32[]{:S(2)}) collective-permute-start(bf16[128,1024]{1,0:T(8,128)(2,1)S(1)} %opposite.1), channel_id=1, source_target_pairs={{0,2},{1,7},{2,4},{3,1},{4,6},{5,3},{6,0},{7,5},{8,10},{9,15},{10,... | collective-permute-start | bytes 786440 | tf_op jit(solution)/shard_map/ppermute | solution.py:405
  115.8 8.3 %collective-permute-start.5 = (bf16[128,1024]{1,0:T(8,128)(2,1)S(1)}, bf16[128,1024]{1,0:T(8,128)(2,1)S(1)}, u32[]{:S(2)}, u32[]{:S(2)}) collective-permute-start(bf16[128,1024]{1,0:T(8,128)(2,1)S(1)} %plain.1), channel_id=1, source_target_pairs={{0,6},{1,3},{2,0},{3,5},{4,2},{5,7},{6,4},{7,1},{8,14},{9,11},{10,... | collective-permute-start | bytes 786440 | tf_op jit(solution)/shard_map/ppermute | solution.py:407
  119.9 6.8 %collective-permute-start.7 = (bf16[128,1024]{1,0:T(8,128)(2,1)S(1)}, bf16[128,1024]{1,0:T(8,128)(2,1)S(1)}, u32[]{:S(2)}, u32[]{:S(2)}) collective-permute-start(bf16[128,1024]{1,0:T(8,128)(2,1)S(1)} %relayed.1), channel_id=1, source_target_pairs={{0,2},{1,7},{2,4},{3,1},{4,6},{5,3},{6,0},{7,5},{8,10},{9,15},{10,... | collective-permute-start | bytes 786440 | tf_op jit(solution)/shard_map/ppermute | solution.py:409

commit v5 on v4

--- a/solution.py
+++ b/solution.py
@@ -45,7 +45,7 @@
     return (x * cosine + other * sine).astype(jnp.bfloat16)
 
 
-def pack_kernel(cache_ref, out_ref, held_ref, rows_ref, sems, out_sems):
+def pack_kernel(cache_ref, early_ref, out_ref, held_ref, rows_ref, sems, out_sems):
     passages, kinds, page_len, _ = cache_ref.shape
     blocks = page_len // BLK
     lanes = pl.ds(pl.multiple_of(lax.axis_index("rep") * HD, HD), HD)
@@ -73,13 +73,13 @@
         copy.wait()
 
 
-def pack(page_cache):
+def pack(page_cache, early):
     passages, kinds, page_len, _ = page_cache.shape
     shape = (kinds * page_len // BLK, passages * BLK + IDS, HD)
     return pl.pallas_call(
         pack_kernel,
         out_shape=pltpu.HBM(shape, jnp.bfloat16),
-        in_specs=[HBM],
+        in_specs=[HBM, HBM],
         out_specs=HBM,
         scratch_shapes=[
             pltpu.VMEM((kinds, passages, page_len, HD), jnp.bfloat16),
@@ -90,7 +90,7 @@
         compiler_params=pltpu.CompilerParams(vmem_limit_bytes=FULL),
         cost_estimate=cost(0, 2 << 20),
         name="pack",
-    )(in_hbm(page_cache))
+    )(in_hbm(page_cache), in_hbm(early))
 
 
 def select_kernel(first_ref, held_ref, out_ref, chosen_ref, sems):
@@ -295,24 +295,95 @@
     )(span, far, block_angles, token_angles, in_hbm(weights))
 
 
-def regroup_kernel(own_ref, other_ref, out_ref):
-    for part, ref in enumerate((own_ref, other_ref)):
-        out_ref[part] = jnp.swapaxes(ref[...], 0, 1)
-
-
-def regroup(own, other):
+def regroup_part(raw_ref, out_ref, rows_ref, blocks_ref, sems, out_sems):
+    slots, step = rows_ref.shape[:2]
+    chunks = raw_ref.shape[0] // step
+
+    def copy_in(chunk):
+        part = pl.ds(pl.multiple_of(chunk * step, step), step)
+        slot = chunk % slots
+        return pltpu.make_async_copy(raw_ref.at[part], rows_ref.at[slot], sems.at[slot])
+
+    def copy_out(chunk):
+        part = pl.ds(pl.multiple_of(chunk * step, step), step)
+        slot = chunk % slots
+        return pltpu.make_async_copy(blocks_ref.at[slot], out_ref.at[:, part], out_sems.at[slot])
+
+    for chunk in range(slots):
+        copy_in(chunk).start()
+
+    def move(chunk, carry):
+        copy_in(chunk).wait()
+
+        @pl.when(chunk >= slots)
+        def _():
+            copy_out(chunk - slots).wait()
+
+        blocks_ref[chunk % slots] = jnp.swapaxes(rows_ref[chunk % slots], 0, 1)
+        copy_out(chunk).start()
+
+        @pl.when(chunk + slots < chunks)
+        def _():
+            copy_in(chunk + slots).start()
+
+        return carry
+
+    lax.fori_loop(0, chunks, move, 0)
+    for chunk in range(chunks - slots, chunks):
+        copy_out(chunk).wait()
+
+
+def regroup_scratch(raw):
+    rows, blocks, cols = raw.shape
+    step, slots = rows // 8, 2
+    return [
+        pltpu.VMEM((slots, step, blocks, cols), raw.dtype),
+        pltpu.VMEM((slots, blocks, step, cols), raw.dtype),
+        pltpu.SemaphoreType.DMA((slots,)),
+        pltpu.SemaphoreType.DMA((slots,)),
+    ]
+
+
+def regroup_early_kernel(own_ref, ids_ref, out_ref, *scratch):
+    @pl.when(lax.axis_index("rep") == 1)
+    def _():
+        regroup_part(own_ref, out_ref.at[0], *scratch)
+
+
+def regroup_early(own, ids):
     rows, blocks, cols = own.shape
-    step = 256
-    return pl.pallas_call(
-        regroup_kernel,
-        out_shape=jax.ShapeDtypeStruct((2, blocks, rows, cols), own.dtype),
-        grid=(rows // step,),
-        in_specs=[pl.BlockSpec((step, blocks, cols), lambda i: (i, 0, 0))] * 2,
-        out_specs=pl.BlockSpec((2, blocks, step, cols), lambda i: (0, 0, i, 0)),
+    return pl.pallas_call(
+        regroup_early_kernel,
+        out_shape=pltpu.HBM((2, blocks, rows, cols), own.dtype),
+        in_specs=[HBM, ANY],
+        out_specs=HBM,
+        scratch_shapes=regroup_scratch(own),
+        compiler_params=pltpu.CompilerParams(vmem_limit_bytes=FULL),
+        cost_estimate=cost(0, 16 << 20),
+        name="regroup_early",
+    )(in_hbm(own), ids)
+
+
+def regroup_late_kernel(own_ref, other_ref, early_ref, out_ref, *scratch):
+    @pl.when(lax.axis_index("rep") == 0)
+    def _():
+        regroup_part(own_ref, out_ref.at[0], *scratch)
+
+    regroup_part(other_ref, out_ref.at[1], *scratch)
+
+
+def regroup_late(own, other, early):
+    return pl.pallas_call(
+        regroup_late_kernel,
+        out_shape=pltpu.HBM(early.shape, early.dtype),
+        in_specs=[HBM] * 3,
+        out_specs=HBM,
+        input_output_aliases={2: 0},
+        scratch_shapes=regroup_scratch(own),
         compiler_params=pltpu.CompilerParams(vmem_limit_bytes=FULL),
         cost_estimate=cost(0, 32 << 20),
-        name="regroup",
-    )(own, other)
+        name="regroup_late",
+    )(in_hbm(own), in_hbm(other), early)
 
 
 def project_kernel(own_ref, other_ref, weight_ref, *refs):
@@ -353,11 +424,15 @@
 
     rep = lax.axis_index("rep")
     other_ids = lax.ppermute(passage_ids, "rep", SWAP)
+    out_weight, _ = lax.optimization_barrier((out_weight, other_ids))
+    raw = out_weight[:, :, 0, :]
+    other_raw = lax.ppermute(raw, "rep", SWAP)
+    early = regroup_early(raw, other_ids)
     row = jnp.arange(IDS, dtype=jnp.int32)[:, None]
     named = jnp.where(row == rep, passage_ids, jnp.where(row == 1 - rep, other_ids, 0))
     named = jnp.pad(named.astype(jnp.bfloat16), ((0, 0), (0, HD - pass_count)))
     packed = lax.dynamic_update_slice(
-        pack(page_cache),
+        pack(page_cache, early),
         jnp.broadcast_to(named, (stores, IDS, HD)),
         (0, per_store * BLK, 0),
     )
@@ -369,9 +444,7 @@
     chosen = select(first, held.reshape(-1, IDS, HD), pieces)
     chosen = chosen.reshape(stores, 2, pass_count, BLK, HD)
 
-    out_weight, _ = lax.optimization_barrier((out_weight, packed))
-    raw = out_weight[:, :, 0, :]
-    weights = regroup(raw, lax.ppermute(raw, "rep", SWAP))
+    weights = regroup_late(raw, other_raw, early)
     kept, sent = split_heads(queries, span_keys, span_values)
     got = lax.ppermute(sent, "rep", SWAP)
     begins = jnp.concatenate([starts, lax.ppermute(starts, "rep", SWAP)])

time: 129 us -> 127 us (0.984)
  Pallas kernels: 27.7 us -> 33.5 us
  starting transfers between devices: 31.3 us -> 25.9 us
  local copies, waits for them, and re-layouts: 6.11 us -> 2.72 us
    pallas_call x1 -> x2, Pallas kernels: 11.7 us -> 17.2 us  [the longest x1 8.61 us: regroup_early(): pl.pallas_call(regroup_early_kernel, out_shape=pltpu.HBM((2, blocks, rows...]
    all_to_all x1, waiting for transfers between devices: 26.4 us -> 21.6 us  [on_device(): held = lax.all_to_all(packed, 'store', 0, 0, tiled=True)]
    all_to_all x1, waiting for transfers between devices: 27.4 us -> 31.4 us  [on_device(): far = lax.all_to_all(chosen, 'store', 0, 0, tiled=True)]
    unnamed x16 -> x12, local copies, waits for them, and re-layouts: 5.11 us -> 1.72 us
    ppermute x1, starting transfers between devices: 2.56 us -> 0.09 us  [on_device(): other = lax.ppermute(other, 'rep', SWAP)]
    all_to_all x1, starting transfers between devices: 8.28 us -> 6.06 us  [on_device(): far = lax.all_to_all(chosen, 'store', 0, 0, tiled=True)]
    ppermute x1, starting transfers between devices: 1.6 us -> 0.09 us  [on_device(): begins = jnp.concatenate([starts, lax.ppermute(starts, 'rep', SWAP)])]
  transfers between devices with their start and end apart: 10 -> 10, of which waited for: 4 -> 5; matrix products, arithmetic and copies ran while one was open for 1% -> 3% of each run, Pallas kernels for 18% -> 23%
where the time goes in v5:
time: 127 us; the launch traced here: 125 us
  waiting for transfers between devices  59.8 us (47%)
  Pallas kernels  33.5 us (26%)
  starting transfers between devices  25.9 us (20%)
  other arithmetic  3.04 us (2%)
  local copies, waits for them, and re-layouts  2.72 us (2%)
    all_to_all x1, waiting for transfers between devices, on_device(): far = lax.all_to_all(chosen, 'store', 0, 0, tiled=True)  31.4 us
    all_to_all x1, waiting for transfers between devices, on_device(): held = lax.all_to_all(packed, 'store', 0, 0, tiled=True)  21.6 us
    all_to_all x1, starting transfers between devices, on_device(): held = lax.all_to_all(packed, 'store', 0, 0, tiled=True)  9.47 us
    pallas_call x1, Pallas kernels, regroup_early(): pl.pallas_call(regroup_early_kernel, out_shape=pltpu.HBM((2, blocks, rows...  8.61 us
    pallas_call x1, Pallas kernels, regroup_late(): pl.pallas_call(regroup_late_kernel, out_shape=pltpu.HBM(early.shape, earl...  8.59 us
    pallas_call x2, Pallas kernels, attend(): pl.pallas_call(functools.partial(attention_kernel, request=request, shift...  7.53 us
    all_to_all x1, starting transfers between devices, on_device(): far = lax.all_to_all(chosen, 'store', 0, 0, tiled=True)  6.06 us
    ppermute x1, starting transfers between devices, on_device(): relayed = lax.ppermute(relayed, axes, ahead)  3.49 us
  transfers between devices with their start and end apart: 10, of which 5 were waited for; matrix products, arithmetic and copies ran while one was open for 3% of the time, Pallas kernels for 23%

profile of v5, /device:TPU:1, one launch (start us, length us, event | category | flops | bytes accessed | tf_op | source)
XLA Modules:
  0.0 125.2 jit_solution(12584857784853726230)
XLA Ops:
  0.0 3.2 %collective-permute-start.2 = (s32[1,8]{1,0:T(1,128)}, s32[1,8]{1,0:T(1,128)S(1)}, u32[]{:S(2)}, u32[]{:S(2)}) collective-permute-start(s32[1,8]{1,0:T(1,128)} %param.11), channel_id=1, source_target_pairs={{0,1},{1,0},{2,3},{3,2},{4,5},{5,4},{6,7},{7,6},{8,9},{9,8},{10,11... | collective-permute-start | bytes 104 | tf_op jit(solution)/shard_map/ppermute | solution.py:426
  3.2 1.0 collective-permute-done.2.ids_ref
  4.2 0.3 collective-permute-start.3
  4.5 0.7 select_convert_fusion
  5.2 8.6 %regroup_early.1.early_ref = bf16[2,4,2048,512]{3,2,1,0:T(8,128)(2,1)} custom-call(bf16[2048,4,512]{2,1,0:T(4,128)(2,1)} %bitcast.15, s32[1,8]{1,0:T(1,128)S(1)} %collective-permute-done.2.ids_ref), custom_call_target="tpu_custom_call" | custom-call | bytes 16777216 | tf_op jit(solution)/shard_map/regroup_early/pallas_call | solution.py:355
  13.9 2.2 %pack.1 = bf16[32,136,128]{2,1,0:T(8,128)(2,1)} custom-call(bf16[8,2,256,256]{3,2,1,0:T(8,128)(2,1)} %cache_ref.1, bf16[2,4,2048,512]{3,2,1,0:T(8,128)(2,1)} %regroup_early.1.early_ref), custom_call_target="tpu_custom_call" | custom-call | bytes 2097152 | tf_op jit(solution)/shard_map/pack/pallas_call | solution.py:79
  16.1 0.7 broadcast_dynamic-update-slice_fusion
  16.7 9.5 %all-to-all-start = ((bf16[32,136,128]{2,1,0:T(8,128)(2,1)}), bf16[32,136,128]{2,1,0:T(8,128)(2,1)S(1)}, u32[]{:S(2)}, u32[]{:S(2)}) async-start(bf16[32,136,128]{2,1,0:T(8,128)(2,1)} %broadcast_dynamic-update-slice_fusion), calls=%async_computation | async-start | bytes 2228224 | tf_op jit(solution)/shard_map/all_to_all | solution.py:439
  26.2 21.6 %all-to-all-done = bf16[32,136,128]{2,1,0:T(8,128)(2,1)S(1)} async-done(((bf16[32,136,128]{2,1,0:T(8,128)(2,1)}), bf16[32,136,128]{2,1,0:T(8,128)(2,1)S(1)}, u32[]{:S(2)}, u32[]{:S(2)}) %all-to-all-start) | async-done | bytes 1114144 | tf_op jit(solution)/shard_map/all_to_all | solution.py:439
  48.0 2.6 %select.12 = bf16[64,8,2,8,128]{4,3,2,1,0:T(8,128)(2,1)} custom-call(s32[64,8]{1,0:T(8,128)S(1)} %fusion.7.first_ref, bf16[544,8,128]{2,1,0:T(8,128)(2,1)S(1)} %bitcast.12), custom_call_target="tpu_custom_call" | custom-call | bytes 2097152 | tf_op jit(solution)/shard_map/select/pallas_call | solution.py:120
  50.6 6.1 %all-to-all-start.1 = ((bf16[32,2,8,16,128]{4,3,2,1,0:T(8,128)(2,1)}), bf16[32,2,8,16,128]{4,3,2,1,0:T(8,128)(2,1)S(1)}, u32[]{:S(2)}, u32[]{:S(2)}) async-start(bf16[32,2,8,16,128]{4,3,2,1,0:T(8,128)(2,1)} %bitcast.17), calls=%async_computation.1 | async-start | bytes 4194304 | tf_op jit(solution)/shard_map/all_to_all | solution.py:461
  56.8 0.8 split_heads.1
  57.6 0.5 collective-permute-start
  58.4 0.1 pad_add_fusion
  58.8 0.5 fusion.2
  59.3 0.5 fusion.1
  59.9 0.7 copy-done.1
  60.6 1.0 copy-done.2
  61.6 0.3 rope_heads.1.span_ref
  61.9 8.6 %regroup_late.1.w_ref = bf16[2,4,2048,512]{3,2,1,0:T(8,128)(2,1)} custom-call(bf16[2048,4,512]{2,1,0:T(4,128)(2,1)} %bitcast.16, bf16[2048,4,512]{2,1,0:T(4,128)(2,1)} %collective-permute-done.3.other_ref, bf16[2,4,2048,512]{3,2,1,0:T(8,128)(2,1)} %regroup_early.1.early_ref), custom_call_target="tpu_custom_call", output_to_operand_aliasing={{}: (2, {})} | custom-call | bytes 33554432 | tf_op jit(solution)/shard_map/regroup_late/pallas_call | solution.py:376
  70.5 31.4 %all-to-all-done.1.far_ref = bf16[32,2,8,16,128]{4,3,2,1,0:T(8,128)(2,1)S(1)} async-done(((bf16[32,2,8,16,128]{4,3,2,1,0:T(8,128)(2,1)}), bf16[32,2,8,16,128]{4,3,2,1,0:T(8,128)(2,1)S(1)}, u32[]{:S(2)}, u32[]{:S(2)}) %all-to-all-start.1) | async-done | bytes 2097184 | tf_op jit(solution)/shard_map/all_to_all | solution.py:461
  101.9 3.7 %attend1.1 = (bf16[128,1024]{1,0:T(8,128)(2,1)S(1)}, bf16[2,2,1024,512]{3,2,1,0:T(8,128)(2,1)S(1)}, bf16[2,2,1024,512]{3,2,1,0:T(8,128)(2,1)S(1)}) custom-call(bf16[2,10,128,128]{3,2,1,0:T(8,128)(2,1)S(1)} %rope_heads.1.span_ref, bf16[32,2,8,16,128]{4,3,2,1,0:T(8,128)(2,1)S(1)} %all-to-all-done.1.far_ref, f32[2,128,128]{2,1,0:T(8,128)S(1)} %get-tuple-element.23.block_ref, ...), custom_call_target="tpu_custom_call" | custom-call | flops 1140850688 | bytes 12582912 | tf_op jit(solution)/shard_map/attend1/pallas_call | solution.py:278
  105.7 3.9 %attend0.1 = (bf16[128,1024]{1,0:T(8,128)(2,1)S(1)}, bf16[2,2,1024,512]{3,2,1,0:T(8,128)(2,1)S(1)}, bf16[2,2,1024,512]{3,2,1,0:T(8,128)(2,1)S(1)}) custom-call(bf16[2,10,128,128]{3,2,1,0:T(8,128)(2,1)S(1)} %rope_heads.1.span_ref, bf16[32,2,8,16,128]{4,3,2,1,0:T(8,128)(2,1)S(1)} %all-to-all-done.1.far_ref, f32[2,128,128]{2,1,0:T(8,128)S(1)} %get-tuple-element.24.block_ref, ...), custom_call_target="tpu_custom_call" | custom-call | flops 1140850688 | bytes 12582912 | tf_op jit(solution)/shard_map/attend0/pallas_call | solution.py:278
  109.6 0.7 opposite.1
  110.3 2.6 %collective-permute-start.6 = (bf16[128,1024]{1,0:T(8,128)(2,1)S(1)}, bf16[128,1024]{1,0:T(8,128)(2,1)S(1)}, u32[]{:S(2)}, u32[]{:S(2)}) collective-permute-start(bf16[128,1024]{1,0:T(8,128)(2,1)S(1)} %opposite.1), channel_id=1, source_target_pairs={{0,2},{1,7},{2,4},{3,1},{4,6},{5,3},{6,0},{7,5},{8,10},{9,15},{10,... | collective-permute-start | bytes 786440 | tf_op jit(solution)/shard_map/ppermute | solution.py:478
  112.9 0.7 plain.1
  113.7 3.2 %collective-permute-done.6.refs_0_ = bf16[128,1024]{1,0:T(8,128)(2,1)S(1)} collective-permute-done((bf16[128,1024]{1,0:T(8,128)(2,1)S(1)}, bf16[128,1024]{1,0:T(8,128)(2,1)S(1)}, u32[]{:S(2)}, u32[]{:S(2)}) %collective-permute-start.6) | collective-permute-done | bytes 262176 | tf_op jit(solution)/shard_map/ppermute | solution.py:478
  116.9 0.7 relayed.1
  117.6 3.5 %collective-permute-start.7 = (bf16[128,1024]{1,0:T(8,128)(2,1)S(1)}, bf16[128,1024]{1,0:T(8,128)(2,1)S(1)}, u32[]{:S(2)}, u32[]{:S(2)}) collective-permute-start(bf16[128,1024]{1,0:T(8,128)(2,1)S(1)} %relayed.1), channel_id=1, source_target_pairs={{0,2},{1,7},{2,4},{3,1},{4,6},{5,3},{6,0},{7,5},{8,10},{9,15},{10,... | collective-permute-start | bytes 786440 | tf_op jit(solution)/shard_map/ppermute | solution.py:482
  121.1 0.7 kept.1
  121.8 2.6 %collective-permute-done.7 = bf16[128,1024]{1,0:T(8,128)(2,1)S(1)} collective-permute-done((bf16[128,1024]{1,0:T(8,128)(2,1)S(1)}, bf16[128,1024]{1,0:T(8,128)(2,1)S(1)}, u32[]{:S(2)}, u32[]{:S(2)}) %collective-permute-start.7) | collective-permute-done | bytes 262176 | tf_op jit(solution)/shard_map/ppermute | solution.py:482
  124.4 0.8 fusion
  (37 shorter events, 1.0 us)
Async XLA Ops:
  0.0 4.2 %collective-permute-start.2 = (s32[1,8]{1,0:T(1,128)}, s32[1,8]{1,0:T(1,128)S(1)}, u32[]{:S(2)}, u32[]{:S(2)}) collective-permute-start(s32[1,8]{1,0:T(1,128)} %param.11), channel_id=1, source_target_pairs={{0,1},{1,0},{2,3},{3,2},{4,5},{5,4},{6,7},{7,6},{8,9},{9,8},{10,11... | collective-permute-start | bytes 104 | tf_op jit(solution)/shard_map/ppermute | solution.py:426
  4.2 57.7 %collective-permute-start.3 = (bf16[2048,4,512]{2,1,0:T(4,128)(2,1)}, bf16[2048,4,512]{2,1,0:T(4,128)(2,1)}, u32[]{:S(2)}, u32[]{:S(2)}) collective-permute-start(bf16[2048,4,512]{2,1,0:T(4,128)(2,1)} %bitcast.14), channel_id=1, source_target_pairs={{0,1},{1,0},{2,3},{3,2},{4,5},{5,4},{6,7},{7,6},{8,9},{9,8},{10,11... | collective-permute-start | bytes 25165832 | tf_op jit(solution)/shard_map/ppermute | solution.py:429
  16.7 31.1 %all-to-all-start = ((bf16[32,136,128]{2,1,0:T(8,128)(2,1)}), bf16[32,136,128]{2,1,0:T(8,128)(2,1)S(1)}, u32[]{:S(2)}, u32[]{:S(2)}) async-start(bf16[32,136,128]{2,1,0:T(8,128)(2,1)} %broadcast_dynamic-update-slice_fusion), calls=%async_computation | async-start | bytes 2228224 | tf_op jit(solution)/shard_map/all_to_all | solution.py:439
  50.6 6.1 %copy-start.5 = (s32[1,8]{1,0:T(1,128)S(1)}, s32[1,8]{1,0:T(1,128)}, u32[]{:S(2)}) copy-start(s32[1,8]{1,0:T(1,128)} %param.12) | copy-start | bytes 100
  50.6 6.2 %copy-start = (bf16[1,128,2048]{2,1,0:T(8,128)(2,1)S(1)}, bf16[1,128,2048]{2,1,0:T(8,128)(2,1)}, u32[]{:S(2)}) copy-start(bf16[1,128,2048]{2,1,0:T(8,128)(2,1)} %q_ref.1) | copy-start | bytes 1572868
  50.6 6.2 %copy-start.3 = (bf16[1,128,256]{2,1,0:T(8,128)(2,1)S(1)}, bf16[1,128,256]{2,1,0:T(8,128)(2,1)}, u32[]{:S(2)}) copy-start(bf16[1,128,256]{2,1,0:T(8,128)(2,1)} %k_ref.1) | copy-start | bytes 196612
  50.6 6.2 %copy-start.4 = (bf16[1,128,256]{2,1,0:T(8,128)(2,1)S(1)}, bf16[1,128,256]{2,1,0:T(8,128)(2,1)}, u32[]{:S(2)}) copy-start(bf16[1,128,256]{2,1,0:T(8,128)(2,1)} %v_ref.1) | copy-start | bytes 196612
  50.6 51.3 %all-to-all-start.1 = ((bf16[32,2,8,16,128]{4,3,2,1,0:T(8,128)(2,1)}), bf16[32,2,8,16,128]{4,3,2,1,0:T(8,128)(2,1)S(1)}, u32[]{:S(2)}, u32[]{:S(2)}) async-start(bf16[32,2,8,16,128]{4,3,2,1,0:T(8,128)(2,1)} %bitcast.17), calls=%async_computation.1 | async-start | bytes 4194304 | tf_op jit(solution)/shard_map/all_to_all | solution.py:461
  56.7 1.7 %collective-permute-start.1 = (s32[1,8]{1,0:T(1,128)S(1)}, s32[1,8]{1,0:T(1,128)S(1)}, u32[]{:S(2)}, u32[]{:S(2)}) collective-permute-start(s32[1,8]{1,0:T(1,128)S(1)} %copy-done.5), channel_id=1, source_target_pairs={{0,1},{1,0},{2,3},{3,2},{4,5},{5,4},{6,7},{7,6},{8,9},{9,8},{10,11... | collective-permute-start | bytes 104 | tf_op jit(solution)/shard_map/ppermute | solution.py:450
  57.6 2.2 %collective-permute-start = (bf16[128,1280]{1,0:T(8,128)(2,1)}, bf16[128,1280]{1,0:T(8,128)(2,1)S(1)}, u32[]{:S(2)}, u32[]{:S(2)}) collective-permute-start(bf16[128,1280]{1,0:T(8,128)(2,1)} %get-tuple-element.15), channel_id=1, source_target_pairs={{0,1},{1,0},{2,3},{3,2},{4,5},{5,4},{6,7},{7,6},{8,9},{9,8},{10,11... | collective-permute-start | bytes 983048 | tf_op jit(solution)/shard_map/ppermute | solution.py:449
  59.9 0.7 copy-start.1
  60.6 1.0 copy-start.2
  105.6 4.0 %collective-permute-start.4 = (bf16[128,1024]{1,0:T(8,128)(2,1)S(1)}, bf16[128,1024]{1,0:T(8,128)(2,1)S(1)}, u32[]{:S(2)}, u32[]{:S(2)}) collective-permute-start(bf16[128,1024]{1,0:T(8,128)(2,1)S(1)} %get-tuple-element.18), channel_id=1, source_target_pairs={{0,1},{1,0},{2,3},{3,2},{4,5},{5,4},{6,7},{7,6},{8,9},{9,8},{10,11... | collective-permute-start | bytes 786440 | tf_op jit(solution)/shard_map/ppermute | solution.py:466
  110.3 6.6 %collective-permute-start.6 = (bf16[128,1024]{1,0:T(8,128)(2,1)S(1)}, bf16[128,1024]{1,0:T(8,128)(2,1)S(1)}, u32[]{:S(2)}, u32[]{:S(2)}) collective-permute-start(bf16[128,1024]{1,0:T(8,128)(2,1)S(1)} %opposite.1), channel_id=1, source_target_pairs={{0,2},{1,7},{2,4},{3,1},{4,6},{5,3},{6,0},{7,5},{8,10},{9,15},{10,... | collective-permute-start | bytes 786440 | tf_op jit(solution)/shard_map/ppermute | solution.py:478
  113.6 8.2 %collective-permute-start.5 = (bf16[128,1024]{1,0:T(8,128)(2,1)S(1)}, bf16[128,1024]{1,0:T(8,128)(2,1)S(1)}, u32[]{:S(2)}, u32[]{:S(2)}) collective-permute-start(bf16[128,1024]{1,0:T(8,128)(2,1)S(1)} %plain.1), channel_id=1, source_target_pairs={{0,6},{1,3},{2,0},{3,5},{4,2},{5,7},{6,4},{7,1},{8,14},{9,11},{10,... | collective-permute-start | bytes 786440 | tf_op jit(solution)/shard_map/ppermute | solution.py:480
  117.6 6.8 %collective-permute-start.7 = (bf16[128,1024]{1,0:T(8,128)(2,1)S(1)}, bf16[128,1024]{1,0:T(8,128)(2,1)S(1)}, u32[]{:S(2)}, u32[]{:S(2)}) collective-permute-start(bf16[128,1024]{1,0:T(8,128)(2,1)S(1)} %relayed.1), channel_id=1, source_target_pairs={{0,2},{1,7},{2,4},{3,1},{4,6},{5,3},{6,0},{7,5},{8,10},{9,15},{10,... | collective-permute-start | bytes 786440 | tf_op jit(solution)/shard_map/ppermute | solution.py:482

commit v6 on v5

--- a/solution.py
+++ b/solution.py
@@ -45,16 +45,31 @@
     return (x * cosine + other * sine).astype(jnp.bfloat16)
 
 
-def pack_kernel(cache_ref, early_ref, out_ref, held_ref, rows_ref, sems, out_sems):
+def pack_kernel(
+    cache_ref, own_ref, other_ref, early_ref, out_ref, held_ref, ids_ref, rows_ref, *all_sems
+):
+    sems, out_sems, ids_sem = all_sems
     passages, kinds, page_len, _ = cache_ref.shape
     blocks = page_len // BLK
-    lanes = pl.ds(pl.multiple_of(lax.axis_index("rep") * HD, HD), HD)
+    rep = lax.axis_index("rep")
+    lanes = pl.ds(pl.multiple_of(rep * HD, HD), HD)
+    ids_copy = pltpu.make_async_copy(own_ref, ids_ref, ids_sem.at[0])
+    ids_copy.start()
     copies = [
         pltpu.make_async_copy(cache_ref.at[:, kind, :, lanes], held_ref.at[kind], sems.at[kind])
         for kind in range(kinds)
     ]
     for copy in copies:
         copy.start()
+    ids_copy.wait()
+    row = lax.broadcasted_iota(jnp.int32, (IDS, HD), 0)
+    lane = lax.broadcasted_iota(jnp.int32, (IDS, HD), 1)
+    named = jnp.zeros((IDS, HD), jnp.int32)
+    for slot in range(own_ref.shape[1]):
+        at = slice(slot, slot + 1)
+        named = jnp.where((row == rep) & (lane == slot), ids_ref[:, at], named)
+        named = jnp.where((row == 1 - rep) & (lane == slot), other_ref[:, at], named)
+    named = named.astype(jnp.float32).astype(jnp.bfloat16)
     outs = []
     for kind in range(kinds):
         copies[kind].wait()
@@ -63,7 +78,7 @@
                 rows_ref[kind * blocks + block, passage * BLK : (passage + 1) * BLK] = held_ref[
                     kind, passage, block * BLK : (block + 1) * BLK
                 ]
-            rows_ref[kind * blocks + block, passages * BLK :] = jnp.zeros((IDS, HD), jnp.bfloat16)
+            rows_ref[kind * blocks + block, passages * BLK :] = named
         part = pl.ds(kind * blocks, blocks)
         outs.append(
             pltpu.make_async_copy(rows_ref.at[part], out_ref.at[part], out_sems.at[kind])
@@ -73,24 +88,26 @@
         copy.wait()
 
 
-def pack(page_cache, early):
+def pack(page_cache, own_ids, other_ids, early):
     passages, kinds, page_len, _ = page_cache.shape
     shape = (kinds * page_len // BLK, passages * BLK + IDS, HD)
     return pl.pallas_call(
         pack_kernel,
         out_shape=pltpu.HBM(shape, jnp.bfloat16),
-        in_specs=[HBM, HBM],
+        in_specs=[HBM, HBM, VMEM, HBM],
         out_specs=HBM,
         scratch_shapes=[
             pltpu.VMEM((kinds, passages, page_len, HD), jnp.bfloat16),
+            pltpu.VMEM(own_ids.shape, own_ids.dtype),
             pltpu.VMEM(shape, jnp.bfloat16),
             pltpu.SemaphoreType.DMA((kinds,)),
             pltpu.SemaphoreType.DMA((kinds,)),
+            pltpu.SemaphoreType.DMA((1,)),
         ],
         compiler_params=pltpu.CompilerParams(vmem_limit_bytes=FULL),
         cost_estimate=cost(0, 2 << 20),
         name="pack",
-    )(in_hbm(page_cache), in_hbm(early))
+    )(in_hbm(page_cache), in_hbm(own_ids), other_ids, in_hbm(early))
 
 
 def select_kernel(first_ref, held_ref, out_ref, chosen_ref, sems):
@@ -428,14 +445,7 @@
     raw = out_weight[:, :, 0, :]
     other_raw = lax.ppermute(raw, "rep", SWAP)
     early = regroup_early(raw, other_ids)
-    row = jnp.arange(IDS, dtype=jnp.int32)[:, None]
-    named = jnp.where(row == rep, passage_ids, jnp.where(row == 1 - rep, other_ids, 0))
-    named = jnp.pad(named.astype(jnp.bfloat16), ((0, 0), (0, HD - pass_count)))
-    packed = lax.dynamic_update_slice(
-        pack(page_cache, early),
-        jnp.broadcast_to(named, (stores, IDS, HD)),
-        (0, per_store * BLK, 0),
-    )
+    packed = pack(page_cache, passage_ids, other_ids, early)
     held = lax.all_to_all(packed, "store", 0, 0, tiled=True)
     ids = held[:, per_store * BLK : per_store * BLK + 2, :pass_count].astype(jnp.int32)
     ids = jnp.where(rep == 0, ids, ids[:, ::-1]).reshape(2 * stores, pass_count)

time: 127 us -> 125 us (0.984)
  transfers between devices with their start and end apart: 10 -> 10, of which waited for: 5 -> 5; matrix products, arithmetic and copies ran while one was open for 3% -> 1% of each run, Pallas kernels for 23% -> 24%
where the time goes in v6:
time: 125 us; the launch traced here: 124 us
  waiting for transfers between devices  59.7 us (48%)
  Pallas kernels  33.5 us (27%)
  starting transfers between devices  25.7 us (21%)
  other arithmetic  2.31 us (2%)
  local copies, waits for them, and re-layouts  2.05 us (2%)
    all_to_all x1, waiting for transfers between devices, on_device(): far = lax.all_to_all(chosen, 'store', 0, 0, tiled=True)  31.4 us
    all_to_all x1, waiting for transfers between devices, on_device(): held = lax.all_to_all(packed, 'store', 0, 0, tiled=True)  21.5 us
    all_to_all x1, starting transfers between devices, on_device(): held = lax.all_to_all(packed, 'store', 0, 0, tiled=True)  9.48 us
    pallas_call x1, Pallas kernels, regroup_early(): pl.pallas_call(regroup_early_kernel, out_shape=pltpu.HBM((2, blocks, rows...  8.6 us
    pallas_call x1, Pallas kernels, regroup_late(): pl.pallas_call(regroup_late_kernel, out_shape=pltpu.HBM(early.shape, earl...  8.59 us
    pallas_call x2, Pallas kernels, attend(): pl.pallas_call(functools.partial(attention_kernel, request=request, shift...  7.53 us
    all_to_all x1, starting transfers between devices, on_device(): far = lax.all_to_all(chosen, 'store', 0, 0, tiled=True)  5.92 us
    ppermute x1, starting transfers between devices, on_device(): relayed = lax.ppermute(relayed, axes, ahead)  3.49 us
  transfers between devices with their start and end apart: 10, of which 5 were waited for; matrix products, arithmetic and copies ran while one was open for 1% of the time, Pallas kernels for 24%

profile of v6, /device:TPU:1, one launch (start us, length us, event | category | flops | bytes accessed | tf_op | source)
XLA Modules:
  0.0 123.6 jit_solution(16388371487661288111)
XLA Ops:
  0.0 3.2 %collective-permute-start.2 = (s32[1,8]{1,0:T(1,128)}, s32[1,8]{1,0:T(1,128)S(1)}, u32[]{:S(2)}, u32[]{:S(2)}) collective-permute-start(s32[1,8]{1,0:T(1,128)} %own_ref.1), channel_id=1, source_target_pairs={{0,1},{1,0},{2,3},{3,2},{4,5},{5,4},{6,7},{7,6},{8,9},{9,8},{10,11... | collective-permute-start | bytes 104 | tf_op jit(solution)/shard_map/ppermute | solution.py:443
  3.2 1.0 collective-permute-done.2.ids_ref.other_ref
  4.2 0.3 collective-permute-start.3
  4.5 8.6 %regroup_early.1.early_ref = bf16[2,4,2048,512]{3,2,1,0:T(8,128)(2,1)} custom-call(bf16[2048,4,512]{2,1,0:T(4,128)(2,1)} %bitcast.12, s32[1,8]{1,0:T(1,128)S(1)} %collective-permute-done.2.ids_ref.other_ref), custom_call_target="tpu_custom_call" | custom-call | bytes 16777216 | tf_op jit(solution)/shard_map/regroup_early/pallas_call | solution.py:372
  13.1 2.2 %pack.1 = bf16[32,136,128]{2,1,0:T(8,128)(2,1)} custom-call(bf16[8,2,256,256]{3,2,1,0:T(8,128)(2,1)} %cache_ref.1, s32[1,8]{1,0:T(1,128)} %own_ref.1, s32[1,8]{1,0:T(1,128)S(1)} %collective-permute-done.2.ids_ref.other_ref, bf16[2,4,2048,512]{3,2,1,0:T(8,128)(2,1)} %regroup_early.1.early_ref), custom_call_target="tpu_custom_call" | custom-call | bytes 2097152 | tf_op jit(solution)/shard_map/pack/pallas_call | solution.py:94
  15.3 9.5 %all-to-all-start = ((bf16[32,136,128]{2,1,0:T(8,128)(2,1)}), bf16[32,136,128]{2,1,0:T(8,128)(2,1)S(1)}, u32[]{:S(2)}, u32[]{:S(2)}) async-start(bf16[32,136,128]{2,1,0:T(8,128)(2,1)} %pack.1), calls=%async_computation | async-start | bytes 2228224 | tf_op jit(solution)/shard_map/all_to_all | solution.py:449
  24.9 21.5 %all-to-all-done = bf16[32,136,128]{2,1,0:T(8,128)(2,1)S(1)} async-done(((bf16[32,136,128]{2,1,0:T(8,128)(2,1)}), bf16[32,136,128]{2,1,0:T(8,128)(2,1)S(1)}, u32[]{:S(2)}, u32[]{:S(2)}) %all-to-all-start) | async-done | bytes 1114144 | tf_op jit(solution)/shard_map/all_to_all | solution.py:449
  46.6 2.6 %select.11 = bf16[64,8,2,8,128]{4,3,2,1,0:T(8,128)(2,1)} custom-call(s32[64,8]{1,0:T(8,128)S(1)} %fusion.7.first_ref, bf16[544,8,128]{2,1,0:T(8,128)(2,1)S(1)} %bitcast.10), custom_call_target="tpu_custom_call" | custom-call | bytes 2097152 | tf_op jit(solution)/shard_map/select/pallas_call | solution.py:137
  49.2 5.9 %all-to-all-start.1 = ((bf16[32,2,8,16,128]{4,3,2,1,0:T(8,128)(2,1)}), bf16[32,2,8,16,128]{4,3,2,1,0:T(8,128)(2,1)S(1)}, u32[]{:S(2)}, u32[]{:S(2)}) async-start(bf16[32,2,8,16,128]{4,3,2,1,0:T(8,128)(2,1)} %bitcast.14), calls=%async_computation.1 | async-start | bytes 4194304 | tf_op jit(solution)/shard_map/all_to_all | solution.py:471
  55.1 0.1 collective-permute-start.1
  55.3 0.8 split_heads.1
  56.1 0.5 collective-permute-start
  56.7 0.1 multiply_cosine_fusion.2
  56.9 0.1 pad_add_fusion
  57.2 0.5 fusion.2
  57.8 0.5 fusion.1
  58.3 0.7 copy-done.1
  59.0 1.0 copy-done.2
  60.0 0.3 rope_heads.1.span_ref
  60.3 8.6 %regroup_late.1.w_ref = bf16[2,4,2048,512]{3,2,1,0:T(8,128)(2,1)} custom-call(bf16[2048,4,512]{2,1,0:T(4,128)(2,1)} %bitcast.13, bf16[2048,4,512]{2,1,0:T(4,128)(2,1)} %collective-permute-done.3.other_ref, bf16[2,4,2048,512]{3,2,1,0:T(8,128)(2,1)} %regroup_early.1.early_ref), custom_call_target="tpu_custom_call", output_to_operand_aliasing={{}: (2, {})} | custom-call | bytes 33554432 | tf_op jit(solution)/shard_map/regroup_late/pallas_call | solution.py:393
  68.9 31.4 %all-to-all-done.1.far_ref = bf16[32,2,8,16,128]{4,3,2,1,0:T(8,128)(2,1)S(1)} async-done(((bf16[32,2,8,16,128]{4,3,2,1,0:T(8,128)(2,1)}), bf16[32,2,8,16,128]{4,3,2,1,0:T(8,128)(2,1)S(1)}, u32[]{:S(2)}, u32[]{:S(2)}) %all-to-all-start.1) | async-done | bytes 2097184 | tf_op jit(solution)/shard_map/all_to_all | solution.py:471
  100.4 3.7 %attend1.1 = (bf16[128,1024]{1,0:T(8,128)(2,1)S(1)}, bf16[2,2,1024,512]{3,2,1,0:T(8,128)(2,1)S(1)}, bf16[2,2,1024,512]{3,2,1,0:T(8,128)(2,1)S(1)}) custom-call(bf16[2,10,128,128]{3,2,1,0:T(8,128)(2,1)S(1)} %rope_heads.1.span_ref, bf16[32,2,8,16,128]{4,3,2,1,0:T(8,128)(2,1)S(1)} %all-to-all-done.1.far_ref, f32[2,128,128]{2,1,0:T(8,128)S(1)} %get-tuple-element.23.block_ref, ...), custom_call_target="tpu_custom_call" | custom-call | flops 1140850688 | bytes 12582912 | tf_op jit(solution)/shard_map/attend1/pallas_call | solution.py:295
  104.1 3.9 %attend0.1 = (bf16[128,1024]{1,0:T(8,128)(2,1)S(1)}, bf16[2,2,1024,512]{3,2,1,0:T(8,128)(2,1)S(1)}, bf16[2,2,1024,512]{3,2,1,0:T(8,128)(2,1)S(1)}) custom-call(bf16[2,10,128,128]{3,2,1,0:T(8,128)(2,1)S(1)} %rope_heads.1.span_ref, bf16[32,2,8,16,128]{4,3,2,1,0:T(8,128)(2,1)S(1)} %all-to-all-done.1.far_ref, f32[2,128,128]{2,1,0:T(8,128)S(1)} %get-tuple-element.24.block_ref, ...), custom_call_target="tpu_custom_call" | custom-call | flops 1140850688 | bytes 12582912 | tf_op jit(solution)/shard_map/attend0/pallas_call | solution.py:295
  108.0 0.7 opposite.1
  108.7 2.6 %collective-permute-start.6 = (bf16[128,1024]{1,0:T(8,128)(2,1)S(1)}, bf16[128,1024]{1,0:T(8,128)(2,1)S(1)}, u32[]{:S(2)}, u32[]{:S(2)}) collective-permute-start(bf16[128,1024]{1,0:T(8,128)(2,1)S(1)} %opposite.1), channel_id=1, source_target_pairs={{0,2},{1,7},{2,4},{3,1},{4,6},{5,3},{6,0},{7,5},{8,10},{9,15},{10,... | collective-permute-start | bytes 786440 | tf_op jit(solution)/shard_map/ppermute | solution.py:488
  111.3 0.7 plain.1
  112.1 3.2 %collective-permute-done.6.refs_0_ = bf16[128,1024]{1,0:T(8,128)(2,1)S(1)} collective-permute-done((bf16[128,1024]{1,0:T(8,128)(2,1)S(1)}, bf16[128,1024]{1,0:T(8,128)(2,1)S(1)}, u32[]{:S(2)}, u32[]{:S(2)}) %collective-permute-start.6) | collective-permute-done | bytes 262176 | tf_op jit(solution)/shard_map/ppermute | solution.py:488
  115.3 0.7 relayed.1
  116.0 3.5 %collective-permute-start.7 = (bf16[128,1024]{1,0:T(8,128)(2,1)S(1)}, bf16[128,1024]{1,0:T(8,128)(2,1)S(1)}, u32[]{:S(2)}, u32[]{:S(2)}) collective-permute-start(bf16[128,1024]{1,0:T(8,128)(2,1)S(1)} %relayed.1), channel_id=1, source_target_pairs={{0,2},{1,7},{2,4},{3,1},{4,6},{5,3},{6,0},{7,5},{8,10},{9,15},{10,... | collective-permute-start | bytes 786440 | tf_op jit(solution)/shard_map/ppermute | solution.py:492
  119.5 0.7 kept.1
  120.3 2.6 %collective-permute-done.7 = bf16[128,1024]{1,0:T(8,128)(2,1)S(1)} collective-permute-done((bf16[128,1024]{1,0:T(8,128)(2,1)S(1)}, bf16[128,1024]{1,0:T(8,128)(2,1)S(1)}, u32[]{:S(2)}, u32[]{:S(2)}) %collective-permute-start.7) | collective-permute-done | bytes 262176 | tf_op jit(solution)/shard_map/ppermute | solution.py:492
  122.8 0.8 fusion
  (33 shorter events, 0.7 us)
Async XLA Ops:
  0.0 4.2 %collective-permute-start.2 = (s32[1,8]{1,0:T(1,128)}, s32[1,8]{1,0:T(1,128)S(1)}, u32[]{:S(2)}, u32[]{:S(2)}) collective-permute-start(s32[1,8]{1,0:T(1,128)} %own_ref.1), channel_id=1, source_target_pairs={{0,1},{1,0},{2,3},{3,2},{4,5},{5,4},{6,7},{7,6},{8,9},{9,8},{10,11... | collective-permute-start | bytes 104 | tf_op jit(solution)/shard_map/ppermute | solution.py:443
  4.2 56.1 %collective-permute-start.3 = (bf16[2048,4,512]{2,1,0:T(4,128)(2,1)}, bf16[2048,4,512]{2,1,0:T(4,128)(2,1)}, u32[]{:S(2)}, u32[]{:S(2)}) collective-permute-start(bf16[2048,4,512]{2,1,0:T(4,128)(2,1)} %bitcast.11), channel_id=1, source_target_pairs={{0,1},{1,0},{2,3},{3,2},{4,5},{5,4},{6,7},{7,6},{8,9},{9,8},{10,11... | collective-permute-start | bytes 25165832 | tf_op jit(solution)/shard_map/ppermute | solution.py:446
  15.3 31.1 %all-to-all-start = ((bf16[32,136,128]{2,1,0:T(8,128)(2,1)}), bf16[32,136,128]{2,1,0:T(8,128)(2,1)S(1)}, u32[]{:S(2)}, u32[]{:S(2)}) async-start(bf16[32,136,128]{2,1,0:T(8,128)(2,1)} %pack.1), calls=%async_computation | async-start | bytes 2228224 | tf_op jit(solution)/shard_map/all_to_all | solution.py:449
  24.8 30.3 %copy-start.5 = (s32[1,8]{1,0:T(1,128)S(1)}, s32[1,8]{1,0:T(1,128)}, u32[]{:S(2)}) copy-start(s32[1,8]{1,0:T(1,128)} %param.12) | copy-start | bytes 100
  24.8 30.4 %copy-start = (bf16[1,128,2048]{2,1,0:T(8,128)(2,1)S(1)}, bf16[1,128,2048]{2,1,0:T(8,128)(2,1)}, u32[]{:S(2)}) copy-start(bf16[1,128,2048]{2,1,0:T(8,128)(2,1)} %q_ref.1) | copy-start | bytes 1572868
  24.9 30.4 %copy-start.3 = (bf16[1,128,256]{2,1,0:T(8,128)(2,1)S(1)}, bf16[1,128,256]{2,1,0:T(8,128)(2,1)}, u32[]{:S(2)}) copy-start(bf16[1,128,256]{2,1,0:T(8,128)(2,1)} %k_ref.1) | copy-start | bytes 196612
  24.9 30.4 %copy-start.4 = (bf16[1,128,256]{2,1,0:T(8,128)(2,1)S(1)}, bf16[1,128,256]{2,1,0:T(8,128)(2,1)}, u32[]{:S(2)}) copy-start(bf16[1,128,256]{2,1,0:T(8,128)(2,1)} %v_ref.1) | copy-start | bytes 196612
  49.2 51.2 %all-to-all-start.1 = ((bf16[32,2,8,16,128]{4,3,2,1,0:T(8,128)(2,1)}), bf16[32,2,8,16,128]{4,3,2,1,0:T(8,128)(2,1)S(1)}, u32[]{:S(2)}, u32[]{:S(2)}) async-start(bf16[32,2,8,16,128]{4,3,2,1,0:T(8,128)(2,1)} %bitcast.14), calls=%async_computation.1 | async-start | bytes 4194304 | tf_op jit(solution)/shard_map/all_to_all | solution.py:471
  55.1 1.7 %collective-permute-start.1 = (s32[1,8]{1,0:T(1,128)S(1)}, s32[1,8]{1,0:T(1,128)S(1)}, u32[]{:S(2)}, u32[]{:S(2)}) collective-permute-start(s32[1,8]{1,0:T(1,128)S(1)} %copy-done.5), channel_id=1, source_target_pairs={{0,1},{1,0},{2,3},{3,2},{4,5},{5,4},{6,7},{7,6},{8,9},{9,8},{10,11... | collective-permute-start | bytes 104 | tf_op jit(solution)/shard_map/ppermute | solution.py:460
  56.1 2.2 %collective-permute-start = (bf16[128,1280]{1,0:T(8,128)(2,1)}, bf16[128,1280]{1,0:T(8,128)(2,1)S(1)}, u32[]{:S(2)}, u32[]{:S(2)}) collective-permute-start(bf16[128,1280]{1,0:T(8,128)(2,1)} %get-tuple-element.15), channel_id=1, source_target_pairs={{0,1},{1,0},{2,3},{3,2},{4,5},{5,4},{6,7},{7,6},{8,9},{9,8},{10,11... | collective-permute-start | bytes 983048 | tf_op jit(solution)/shard_map/ppermute | solution.py:459
  58.3 0.7 copy-start.1
  59.0 1.0 copy-start.2
  104.0 4.0 %collective-permute-start.4 = (bf16[128,1024]{1,0:T(8,128)(2,1)S(1)}, bf16[128,1024]{1,0:T(8,128)(2,1)S(1)}, u32[]{:S(2)}, u32[]{:S(2)}) collective-permute-start(bf16[128,1024]{1,0:T(8,128)(2,1)S(1)} %get-tuple-element.18), channel_id=1, source_target_pairs={{0,1},{1,0},{2,3},{3,2},{4,5},{5,4},{6,7},{7,6},{8,9},{9,8},{10,11... | collective-permute-start | bytes 786440 | tf_op jit(solution)/shard_map/ppermute | solution.py:476
  108.7 6.6 %collective-permute-start.6 = (bf16[128,1024]{1,0:T(8,128)(2,1)S(1)}, bf16[128,1024]{1,0:T(8,128)(2,1)S(1)}, u32[]{:S(2)}, u32[]{:S(2)}) collective-permute-start(bf16[128,1024]{1,0:T(8,128)(2,1)S(1)} %opposite.1), channel_id=1, source_target_pairs={{0,2},{1,7},{2,4},{3,1},{4,6},{5,3},{6,0},{7,5},{8,10},{9,15},{10,... | collective-permute-start | bytes 786440 | tf_op jit(solution)/shard_map/ppermute | solution.py:488
  112.0 8.2 %collective-permute-start.5 = (bf16[128,1024]{1,0:T(8,128)(2,1)S(1)}, bf16[128,1024]{1,0:T(8,128)(2,1)S(1)}, u32[]{:S(2)}, u32[]{:S(2)}) collective-permute-start(bf16[128,1024]{1,0:T(8,128)(2,1)S(1)} %plain.1), channel_id=1, source_target_pairs={{0,6},{1,3},{2,0},{3,5},{4,2},{5,7},{6,4},{7,1},{8,14},{9,11},{10,... | collective-permute-start | bytes 786440 | tf_op jit(solution)/shard_map/ppermute | solution.py:490
  116.0 6.8 %collective-permute-start.7 = (bf16[128,1024]{1,0:T(8,128)(2,1)S(1)}, bf16[128,1024]{1,0:T(8,128)(2,1)S(1)}, u32[]{:S(2)}, u32[]{:S(2)}) collective-permute-start(bf16[128,1024]{1,0:T(8,128)(2,1)S(1)} %relayed.1), channel_id=1, source_target_pairs={{0,2},{1,7},{2,4},{3,1},{4,6},{5,3},{6,0},{7,5},{8,10},{9,15},{10,... | collective-permute-start | bytes 786440 | tf_op jit(solution)/shard_map/ppermute | solution.py:492

commit v7 on v6

--- a/solution.py
+++ b/solution.py
@@ -352,7 +352,7 @@
 
 def regroup_scratch(raw):
     rows, blocks, cols = raw.shape
-    step, slots = rows // 8, 2
+    step, slots = rows // 16, 2
     return [
         pltpu.VMEM((slots, step, blocks, cols), raw.dtype),
         pltpu.VMEM((slots, blocks, step, cols), raw.dtype),

time: 125 us -> 123 us (0.984)
  waiting for transfers between devices: 59.7 us -> 53.5 us
  Pallas kernels: 33.5 us -> 39.5 us
  starting transfers between devices: 25.7 us -> 23.9 us
    all_to_all x1, waiting for transfers between devices: 31.4 us -> 26.4 us  [on_device(): far = lax.all_to_all(chosen, 'store', 0, 0, tiled=True)]
    pallas_call x1, Pallas kernels: 8.59 us -> 11.6 us  [regroup_late(): pl.pallas_call(regroup_late_kernel, out_shape=pltpu.HBM(early.shape, earl...]
    pallas_call x1, Pallas kernels: 8.6 us -> 11.6 us  [regroup_early(): pl.pallas_call(regroup_early_kernel, out_shape=pltpu.HBM((2, blocks, rows...]
    all_to_all x1, starting transfers between devices: 5.92 us -> 4.09 us  [on_device(): far = lax.all_to_all(chosen, 'store', 0, 0, tiled=True)]
  transfers between devices with their start and end apart: 10 -> 10, of which waited for: 5 -> 5; matrix products, arithmetic and copies ran while one was open for 1% -> 2% of each run, Pallas kernels for 24% -> 29%
where the time goes in v7:
time: 123 us; the launch traced here: 122 us
  waiting for transfers between devices  53.5 us (43%)
  Pallas kernels  39.5 us (32%)
  starting transfers between devices  23.9 us (19%)
  other arithmetic  2.31 us (2%)
  local copies, waits for them, and re-layouts  2.05 us (2%)
    all_to_all x1, waiting for transfers between devices, on_device(): far = lax.all_to_all(chosen, 'store', 0, 0, tiled=True)  26.4 us
    all_to_all x1, waiting for transfers between devices, on_device(): held = lax.all_to_all(packed, 'store', 0, 0, tiled=True)  20.4 us
    pallas_call x1, Pallas kernels, regroup_late(): pl.pallas_call(regroup_late_kernel, out_shape=pltpu.HBM(early.shape, earl...  11.6 us
    pallas_call x1, Pallas kernels, regroup_early(): pl.pallas_call(regroup_early_kernel, out_shape=pltpu.HBM((2, blocks, rows...  11.6 us
    all_to_all x1, starting transfers between devices, on_device(): held = lax.all_to_all(packed, 'store', 0, 0, tiled=True)  9.48 us
    pallas_call x2, Pallas kernels, attend(): pl.pallas_call(functools.partial(attention_kernel, request=request, shift...  7.53 us
    all_to_all x1, starting transfers between devices, on_device(): far = lax.all_to_all(chosen, 'store', 0, 0, tiled=True)  4.09 us
    ppermute x1, starting transfers between devices, on_device(): relayed = lax.ppermute(relayed, axes, ahead)  3.49 us
  transfers between devices with their start and end apart: 10, of which 5 were waited for; matrix products, arithmetic and copies ran while one was open for 2% of the time, Pallas kernels for 29%

profile of v7, /device:TPU:1, one launch (start us, length us, event | category | flops | bytes accessed | tf_op | source)
XLA Modules:
  0.0 121.6 jit_solution(11086825587313954153)
XLA Ops:
  0.0 3.2 %collective-permute-start.2 = (s32[1,8]{1,0:T(1,128)}, s32[1,8]{1,0:T(1,128)S(1)}, u32[]{:S(2)}, u32[]{:S(2)}) collective-permute-start(s32[1,8]{1,0:T(1,128)} %own_ref.1), channel_id=1, source_target_pairs={{0,1},{1,0},{2,3},{3,2},{4,5},{5,4},{6,7},{7,6},{8,9},{9,8},{10,11... | collective-permute-start | bytes 104 | tf_op jit(solution)/shard_map/ppermute | solution.py:443
  3.2 1.0 collective-permute-done.2.ids_ref.other_ref
  4.2 0.3 collective-permute-start.3
  4.5 11.6 %regroup_early.1.early_ref = bf16[2,4,2048,512]{3,2,1,0:T(8,128)(2,1)} custom-call(bf16[2048,4,512]{2,1,0:T(4,128)(2,1)} %bitcast.12, s32[1,8]{1,0:T(1,128)S(1)} %collective-permute-done.2.ids_ref.other_ref), custom_call_target="tpu_custom_call" | custom-call | bytes 16777216 | tf_op jit(solution)/shard_map/regroup_early/pallas_call | solution.py:372
  16.1 2.2 %pack.1 = bf16[32,136,128]{2,1,0:T(8,128)(2,1)} custom-call(bf16[8,2,256,256]{3,2,1,0:T(8,128)(2,1)} %cache_ref.1, s32[1,8]{1,0:T(1,128)} %own_ref.1, s32[1,8]{1,0:T(1,128)S(1)} %collective-permute-done.2.ids_ref.other_ref, bf16[2,4,2048,512]{3,2,1,0:T(8,128)(2,1)} %regroup_early.1.early_ref), custom_call_target="tpu_custom_call" | custom-call | bytes 2097152 | tf_op jit(solution)/shard_map/pack/pallas_call | solution.py:94
  18.3 9.5 %all-to-all-start = ((bf16[32,136,128]{2,1,0:T(8,128)(2,1)}), bf16[32,136,128]{2,1,0:T(8,128)(2,1)S(1)}, u32[]{:S(2)}, u32[]{:S(2)}) async-start(bf16[32,136,128]{2,1,0:T(8,128)(2,1)} %pack.1), calls=%async_computation | async-start | bytes 2228224 | tf_op jit(solution)/shard_map/all_to_all | solution.py:449
  27.9 20.4 %all-to-all-done = bf16[32,136,128]{2,1,0:T(8,128)(2,1)S(1)} async-done(((bf16[32,136,128]{2,1,0:T(8,128)(2,1)}), bf16[32,136,128]{2,1,0:T(8,128)(2,1)S(1)}, u32[]{:S(2)}, u32[]{:S(2)}) %all-to-all-start) | async-done | bytes 1114144 | tf_op jit(solution)/shard_map/all_to_all | solution.py:449
  48.4 2.6 %select.11 = bf16[64,8,2,8,128]{4,3,2,1,0:T(8,128)(2,1)} custom-call(s32[64,8]{1,0:T(8,128)S(1)} %fusion.7.first_ref, bf16[544,8,128]{2,1,0:T(8,128)(2,1)S(1)} %bitcast.10), custom_call_target="tpu_custom_call" | custom-call | bytes 2097152 | tf_op jit(solution)/shard_map/select/pallas_call | solution.py:137
  51.0 4.1 %all-to-all-start.1 = ((bf16[32,2,8,16,128]{4,3,2,1,0:T(8,128)(2,1)}), bf16[32,2,8,16,128]{4,3,2,1,0:T(8,128)(2,1)S(1)}, u32[]{:S(2)}, u32[]{:S(2)}) async-start(bf16[32,2,8,16,128]{4,3,2,1,0:T(8,128)(2,1)} %bitcast.14), calls=%async_computation.1 | async-start | bytes 4194304 | tf_op jit(solution)/shard_map/all_to_all | solution.py:471
  55.1 0.1 collective-permute-start.1
  55.3 0.8 split_heads.1
  56.1 0.5 collective-permute-start
  56.7 0.1 multiply_cosine_fusion.2
  56.9 0.1 pad_add_fusion
  57.2 0.5 fusion.2
  57.8 0.5 fusion.1
  58.3 0.7 copy-done.1
  59.0 1.0 copy-done.2
  60.0 0.3 rope_heads.1.span_ref
  60.3 11.6 %regroup_late.1.w_ref = bf16[2,4,2048,512]{3,2,1,0:T(8,128)(2,1)} custom-call(bf16[2048,4,512]{2,1,0:T(4,128)(2,1)} %bitcast.13, bf16[2048,4,512]{2,1,0:T(4,128)(2,1)} %collective-permute-done.3.other_ref, bf16[2,4,2048,512]{3,2,1,0:T(8,128)(2,1)} %regroup_early.1.early_ref), custom_call_target="tpu_custom_call", output_to_operand_aliasing={{}: (2, {})} | custom-call | bytes 33554432 | tf_op jit(solution)/shard_map/regroup_late/pallas_call | solution.py:393
  71.9 26.4 %all-to-all-done.1.far_ref = bf16[32,2,8,16,128]{4,3,2,1,0:T(8,128)(2,1)S(1)} async-done(((bf16[32,2,8,16,128]{4,3,2,1,0:T(8,128)(2,1)}), bf16[32,2,8,16,128]{4,3,2,1,0:T(8,128)(2,1)S(1)}, u32[]{:S(2)}, u32[]{:S(2)}) %all-to-all-start.1) | async-done | bytes 2097184 | tf_op jit(solution)/shard_map/all_to_all | solution.py:471
  98.3 3.7 %attend1.1 = (bf16[128,1024]{1,0:T(8,128)(2,1)S(1)}, bf16[2,2,1024,512]{3,2,1,0:T(8,128)(2,1)S(1)}, bf16[2,2,1024,512]{3,2,1,0:T(8,128)(2,1)S(1)}) custom-call(bf16[2,10,128,128]{3,2,1,0:T(8,128)(2,1)S(1)} %rope_heads.1.span_ref, bf16[32,2,8,16,128]{4,3,2,1,0:T(8,128)(2,1)S(1)} %all-to-all-done.1.far_ref, f32[2,128,128]{2,1,0:T(8,128)S(1)} %get-tuple-element.23.block_ref, ...), custom_call_target="tpu_custom_call" | custom-call | flops 1140850688 | bytes 12582912 | tf_op jit(solution)/shard_map/attend1/pallas_call | solution.py:295
  102.1 3.9 %attend0.1 = (bf16[128,1024]{1,0:T(8,128)(2,1)S(1)}, bf16[2,2,1024,512]{3,2,1,0:T(8,128)(2,1)S(1)}, bf16[2,2,1024,512]{3,2,1,0:T(8,128)(2,1)S(1)}) custom-call(bf16[2,10,128,128]{3,2,1,0:T(8,128)(2,1)S(1)} %rope_heads.1.span_ref, bf16[32,2,8,16,128]{4,3,2,1,0:T(8,128)(2,1)S(1)} %all-to-all-done.1.far_ref, f32[2,128,128]{2,1,0:T(8,128)S(1)} %get-tuple-element.24.block_ref, ...), custom_call_target="tpu_custom_call" | custom-call | flops 1140850688 | bytes 12582912 | tf_op jit(solution)/shard_map/attend0/pallas_call | solution.py:295
  106.0 0.7 opposite.1
  106.7 2.6 %collective-permute-start.6 = (bf16[128,1024]{1,0:T(8,128)(2,1)S(1)}, bf16[128,1024]{1,0:T(8,128)(2,1)S(1)}, u32[]{:S(2)}, u32[]{:S(2)}) collective-permute-start(bf16[128,1024]{1,0:T(8,128)(2,1)S(1)} %opposite.1), channel_id=1, source_target_pairs={{0,2},{1,7},{2,4},{3,1},{4,6},{5,3},{6,0},{7,5},{8,10},{9,15},{10,... | collective-permute-start | bytes 786440 | tf_op jit(solution)/shard_map/ppermute | solution.py:488
  109.3 0.7 plain.1
  110.1 3.2 %collective-permute-done.6.refs_0_ = bf16[128,1024]{1,0:T(8,128)(2,1)S(1)} collective-permute-done((bf16[128,1024]{1,0:T(8,128)(2,1)S(1)}, bf16[128,1024]{1,0:T(8,128)(2,1)S(1)}, u32[]{:S(2)}, u32[]{:S(2)}) %collective-permute-start.6) | collective-permute-done | bytes 262176 | tf_op jit(solution)/shard_map/ppermute | solution.py:488
  113.3 0.7 relayed.1
  114.0 3.5 %collective-permute-start.7 = (bf16[128,1024]{1,0:T(8,128)(2,1)S(1)}, bf16[128,1024]{1,0:T(8,128)(2,1)S(1)}, u32[]{:S(2)}, u32[]{:S(2)}) collective-permute-start(bf16[128,1024]{1,0:T(8,128)(2,1)S(1)} %relayed.1), channel_id=1, source_target_pairs={{0,2},{1,7},{2,4},{3,1},{4,6},{5,3},{6,0},{7,5},{8,10},{9,15},{10,... | collective-permute-start | bytes 786440 | tf_op jit(solution)/shard_map/ppermute | solution.py:492
  117.5 0.7 kept.1
  118.3 2.6 %collective-permute-done.7 = bf16[128,1024]{1,0:T(8,128)(2,1)S(1)} collective-permute-done((bf16[128,1024]{1,0:T(8,128)(2,1)S(1)}, bf16[128,1024]{1,0:T(8,128)(2,1)S(1)}, u32[]{:S(2)}, u32[]{:S(2)}) %collective-permute-start.7) | collective-permute-done | bytes 262176 | tf_op jit(solution)/shard_map/ppermute | solution.py:492
  120.8 0.8 fusion
  (33 shorter events, 0.7 us)
Async XLA Ops:
  0.0 4.2 %collective-permute-start.2 = (s32[1,8]{1,0:T(1,128)}, s32[1,8]{1,0:T(1,128)S(1)}, u32[]{:S(2)}, u32[]{:S(2)}) collective-permute-start(s32[1,8]{1,0:T(1,128)} %own_ref.1), channel_id=1, source_target_pairs={{0,1},{1,0},{2,3},{3,2},{4,5},{5,4},{6,7},{7,6},{8,9},{9,8},{10,11... | collective-permute-start | bytes 104 | tf_op jit(solution)/shard_map/ppermute | solution.py:443
  4.2 56.1 %collective-permute-start.3 = (bf16[2048,4,512]{2,1,0:T(4,128)(2,1)}, bf16[2048,4,512]{2,1,0:T(4,128)(2,1)}, u32[]{:S(2)}, u32[]{:S(2)}) collective-permute-start(bf16[2048,4,512]{2,1,0:T(4,128)(2,1)} %bitcast.11), channel_id=1, source_target_pairs={{0,1},{1,0},{2,3},{3,2},{4,5},{5,4},{6,7},{7,6},{8,9},{9,8},{10,11... | collective-permute-start | bytes 25165832 | tf_op jit(solution)/shard_map/ppermute | solution.py:446
  18.3 29.9 %all-to-all-start = ((bf16[32,136,128]{2,1,0:T(8,128)(2,1)}), bf16[32,136,128]{2,1,0:T(8,128)(2,1)S(1)}, u32[]{:S(2)}, u32[]{:S(2)}) async-start(bf16[32,136,128]{2,1,0:T(8,128)(2,1)} %pack.1), calls=%async_computation | async-start | bytes 2228224 | tf_op jit(solution)/shard_map/all_to_all | solution.py:449
  27.8 27.3 %copy-start.5 = (s32[1,8]{1,0:T(1,128)S(1)}, s32[1,8]{1,0:T(1,128)}, u32[]{:S(2)}) copy-start(s32[1,8]{1,0:T(1,128)} %param.12) | copy-start | bytes 100
  27.8 27.4 %copy-start = (bf16[1,128,2048]{2,1,0:T(8,128)(2,1)S(1)}, bf16[1,128,2048]{2,1,0:T(8,128)(2,1)}, u32[]{:S(2)}) copy-start(bf16[1,128,2048]{2,1,0:T(8,128)(2,1)} %q_ref.1) | copy-start | bytes 1572868
  27.8 27.4 %copy-start.3 = (bf16[1,128,256]{2,1,0:T(8,128)(2,1)S(1)}, bf16[1,128,256]{2,1,0:T(8,128)(2,1)}, u32[]{:S(2)}) copy-start(bf16[1,128,256]{2,1,0:T(8,128)(2,1)} %k_ref.1) | copy-start | bytes 196612
  27.9 27.4 %copy-start.4 = (bf16[1,128,256]{2,1,0:T(8,128)(2,1)S(1)}, bf16[1,128,256]{2,1,0:T(8,128)(2,1)}, u32[]{:S(2)}) copy-start(bf16[1,128,256]{2,1,0:T(8,128)(2,1)} %v_ref.1) | copy-start | bytes 196612
  51.0 47.3 %all-to-all-start.1 = ((bf16[32,2,8,16,128]{4,3,2,1,0:T(8,128)(2,1)}), bf16[32,2,8,16,128]{4,3,2,1,0:T(8,128)(2,1)S(1)}, u32[]{:S(2)}, u32[]{:S(2)}) async-start(bf16[32,2,8,16,128]{4,3,2,1,0:T(8,128)(2,1)} %bitcast.14), calls=%async_computation.1 | async-start | bytes 4194304 | tf_op jit(solution)/shard_map/all_to_all | solution.py:471
  55.1 1.7 %collective-permute-start.1 = (s32[1,8]{1,0:T(1,128)S(1)}, s32[1,8]{1,0:T(1,128)S(1)}, u32[]{:S(2)}, u32[]{:S(2)}) collective-permute-start(s32[1,8]{1,0:T(1,128)S(1)} %copy-done.5), channel_id=1, source_target_pairs={{0,1},{1,0},{2,3},{3,2},{4,5},{5,4},{6,7},{7,6},{8,9},{9,8},{10,11... | collective-permute-start | bytes 104 | tf_op jit(solution)/shard_map/ppermute | solution.py:460
  56.1 2.2 %collective-permute-start = (bf16[128,1280]{1,0:T(8,128)(2,1)}, bf16[128,1280]{1,0:T(8,128)(2,1)S(1)}, u32[]{:S(2)}, u32[]{:S(2)}) collective-permute-start(bf16[128,1280]{1,0:T(8,128)(2,1)} %get-tuple-element.15), channel_id=1, source_target_pairs={{0,1},{1,0},{2,3},{3,2},{4,5},{5,4},{6,7},{7,6},{8,9},{9,8},{10,11... | collective-permute-start | bytes 983048 | tf_op jit(solution)/shard_map/ppermute | solution.py:459
  58.3 0.7 copy-start.1
  59.0 1.0 copy-start.2
  102.0 4.0 %collective-permute-start.4 = (bf16[128,1024]{1,0:T(8,128)(2,1)S(1)}, bf16[128,1024]{1,0:T(8,128)(2,1)S(1)}, u32[]{:S(2)}, u32[]{:S(2)}) collective-permute-start(bf16[128,1024]{1,0:T(8,128)(2,1)S(1)} %get-tuple-element.18), channel_id=1, source_target_pairs={{0,1},{1,0},{2,3},{3,2},{4,5},{5,4},{6,7},{7,6},{8,9},{9,8},{10,11... | collective-permute-start | bytes 786440 | tf_op jit(solution)/shard_map/ppermute | solution.py:476
  106.7 6.6 %collective-permute-start.6 = (bf16[128,1024]{1,0:T(8,128)(2,1)S(1)}, bf16[128,1024]{1,0:T(8,128)(2,1)S(1)}, u32[]{:S(2)}, u32[]{:S(2)}) collective-permute-start(bf16[128,1024]{1,0:T(8,128)(2,1)S(1)} %opposite.1), channel_id=1, source_target_pairs={{0,2},{1,7},{2,4},{3,1},{4,6},{5,3},{6,0},{7,5},{8,10},{9,15},{10,... | collective-permute-start | bytes 786440 | tf_op jit(solution)/shard_map/ppermute | solution.py:488
  110.0 8.2 %collective-permute-start.5 = (bf16[128,1024]{1,0:T(8,128)(2,1)S(1)}, bf16[128,1024]{1,0:T(8,128)(2,1)S(1)}, u32[]{:S(2)}, u32[]{:S(2)}) collective-permute-start(bf16[128,1024]{1,0:T(8,128)(2,1)S(1)} %plain.1), channel_id=1, source_target_pairs={{0,6},{1,3},{2,0},{3,5},{4,2},{5,7},{6,4},{7,1},{8,14},{9,11},{10,... | collective-permute-start | bytes 786440 | tf_op jit(solution)/shard_map/ppermute | solution.py:490
  114.0 6.8 %collective-permute-start.7 = (bf16[128,1024]{1,0:T(8,128)(2,1)S(1)}, bf16[128,1024]{1,0:T(8,128)(2,1)S(1)}, u32[]{:S(2)}, u32[]{:S(2)}) collective-permute-start(bf16[128,1024]{1,0:T(8,128)(2,1)S(1)} %relayed.1), channel_id=1, source_target_pairs={{0,2},{1,7},{2,4},{3,1},{4,6},{5,3},{6,0},{7,5},{8,10},{9,15},{10,... | collective-permute-start | bytes 786440 | tf_op jit(solution)/shard_map/ppermute | solution.py:492
